TPU v7x, 32 devices: a whole 2x2x4 slice. The times are simulated.
32 devices in a mesh: space: 8 (over z, x), chan: 4 (over y, core).
Axes of the slice: x: 2, y: 2, z: 4, core: 2. Of those that a mesh axis runs over, the one named last changes fastest.
Arguments:
- features: bfloat16 [128, 2048], P('chan', 'space'), may hold values from -6 to 6
- positions: float32 [3, 2048], P(None, 'space'), may hold values from 0 to 16, as said below
- species: int32 [2048], P('space'), may hold values from 0 to 5
- block_count: int32 [32], P('space'), may hold values from 48 to 64, as said below
- pair_home: int32 [128], P('space'), may hold values from 0 to 3, as said below
- pair_reach: int32 [128], P('space'), may hold values from 1 to 4, as said below
- pair_count: int32 [8], P('space'), may hold values from 4 to 16, as said below
- wave_ints: int32 [3, 1024], replicated, may hold values from -8 to 8, as said below
- species_gain: float32 [6, 128], P(None, 'chan'), may hold values from 0.5 to 2
- w_in: bfloat16 [128, 128], replicated, may hold values from -0.5 to 0.5
- w_rad: float32 [16, 128], P(None, 'chan'), may hold values from -1.5 to 1.5
- cotangent: bfloat16 [9, 128, 2048], P(None, 'chan', 'space'), may hold values from -6 to 6
Outputs:
- messages: bfloat16 [9, 128, 2048], P(None, 'chan', 'space')
- grad_features: float32 [128, 2048], P('chan', 'space')
Inputs may be any that keep to these rules, and one draw needn't show every extreme that they name: `positions`: atom a lies in block a // 64: its first coordinate lies in [0.5 (a // 64), 0.5 (a // 64 + 1)); the other two lie in [0, 1.5). `block_count`: some block is full. `pair_home`: the 16 slots of one index of space hold every pair (home, reach) with home in 0..3 and reach in 1..4 exactly once, in an order drawn from the seed. `pair_reach`: as for pair_home, the same slots. `pair_count`: live slots come first; some index of space has all 16 live. `wave_ints`: no wavevector is all zeros; the first component lies in -8..8, the others in -4..4.
All inputs are finite; a program needn't handle non-finite values.
Results may differ from a plain program's by a relative error of at most 0.0051.
Values may be sent and summed in bfloat16 or wider, within the bound.
No kernel may reach another device: no remote copies, remote signals or barrier semaphores. Data moves between devices by JAX's collectives and lax.ppermute only.
A program may use at most 64 MiB of HBM per device.

v0:
```python
import math

import jax
import jax.numpy as jnp
from jax import lax
from jax.sharding import PartitionSpec as P

NSPEC = 6
BLOCK = 64
REACH = 4


SLICE_WIDTH = 0.5
SIDE_WIDTH = 12.0
GAP_HEIGHT = 24.0
SCREEN = 0.5
HARM_SIGNS = (1.0, -1.0, -1.0, -1.0, 1.0, 1.0, 1.0, 1.0, 1.0)
HIGH = lax.Precision.HIGHEST


def passed_along(block, axis, distance):
    devices = range(lax.axis_size(axis))
    route = [((i - distance) % len(devices), i) for i in devices]
    return lax.ppermute(block, axis, route)


def harmonics(unit):
    ux, uy, uz = (unit[0], unit[1], unit[2])
    squared = ux * ux + uy * uy + uz * uz
    root_three = math.sqrt(3.0)
    root_fifteen = math.sqrt(15.0)
    root_five = math.sqrt(5.0)
    return jnp.stack(
        [
            jnp.ones_like(ux),
            root_three * ux,
            root_three * uy,
            root_three * uz,
            root_fifteen * ux * uy,
            root_fifteen * uy * uz,
            0.5 * root_five * (3.0 * uz * uz - squared),
            root_fifteen * ux * uz,
            0.5 * root_fifteen * (ux * ux - uy * uy),
        ]
    )


def pair_filter(pos_home, pos_far, w_rad, cutoff, self_pair):
    disp = pos_far[:, None, :] - pos_home[:, :, None]
    unit = disp / cutoff
    squared = unit[0] * unit[0] + unit[1] * unit[1] + unit[2] * unit[2]
    envelope = jnp.square(jnp.maximum(1.0 - squared, 0.0))
    count = w_rad.shape[0]
    centres = jnp.arange(count).astype(jnp.float32) / (count - 1)
    gamma = 0.5 * (count - 1) ** 2
    radial = envelope[None] * jnp.exp(-gamma * jnp.square(squared[None] - centres[:, None, None]))
    if self_pair:
        radial = radial * (1.0 - jnp.eye(pos_home.shape[1], dtype=jnp.float32))[None]
    filt = jnp.einsum("rc,rij->cij", w_rad, radial, precision=HIGH)
    harm = harmonics(unit)
    signed = harm * jnp.array(HARM_SIGNS, jnp.float32)[:, None, None]
    return (filt, harm, signed)


def pair_terms(pos_home, pos_far, data_home, data_far, w_rad, cutoff, self_pair):
    filt, harm, signed = pair_filter(pos_home, pos_far, w_rad, cutoff, self_pair)
    source_home = data_home[0].astype(jnp.float32)
    source_far = data_far[0].astype(jnp.float32)
    grad_home = data_home[1:].astype(jnp.float32)
    grad_far = data_far[1:].astype(jnp.float32)
    home_msg = jnp.einsum("lij,cij->lci", harm, filt * source_far[:, None, :], precision=HIGH)
    far_dx = jnp.sum(filt * jnp.einsum("lij,lci->cij", harm, grad_home, precision=HIGH), axis=1)
    far_msg = jnp.einsum("lij,cij->lcj", signed, filt * source_home[:, :, None], precision=HIGH)
    home_dx = jnp.sum(filt * jnp.einsum("lij,lcj->cij", signed, grad_far, precision=HIGH), axis=2)
    return (home_msg, far_dx, far_msg, home_dx)


def add_block(total, update, start):
    current = lax.dynamic_slice_in_dim(total, start, update.shape[2], 2)
    return lax.dynamic_update_slice_in_dim(total, current + update, start, 2)


def wave_table(positions, wave_ints, length):
    box = jnp.array([length, SIDE_WIDTH, GAP_HEIGHT], jnp.float32)
    freq = 2.0 * math.pi * wave_ints.astype(jnp.float32) / box[:, None]
    angle = freq[0][:, None] * positions[0][None, :] + freq[1][:, None] * positions[1][None, :]
    angle = angle + freq[2][:, None] * positions[2][None, :]
    return jnp.concatenate([jnp.cos(angle), jnp.sin(angle)], 0).astype(jnp.bfloat16)


def wave_weight(wave_ints, length):
    box = jnp.array([length, SIDE_WIDTH, GAP_HEIGHT], jnp.float32)
    freq = 2.0 * math.pi * wave_ints.astype(jnp.float32) / box[:, None]
    ksq = freq[0] * freq[0] + freq[1] * freq[1] + freq[2] * freq[2]
    value = jnp.exp(-0.5 * ksq) / (ksq + SCREEN * SCREEN)
    return jnp.concatenate([value, value], 0)


def on_device(
    features,
    positions,
    species,
    block_count,
    pair_home,
    pair_reach,
    pair_count,
    wave_ints,
    species_gain,
    w_in,
    w_rad,
    cotangent,
):
    local_channels = features.shape[0]
    atoms = features.shape[1]
    spaces = lax.axis_size("space")
    place = lax.axis_index("space")
    lane = lax.axis_index("chan")
    blocks = atoms // BLOCK
    length = SLICE_WIDTH * blocks * spaces
    cutoff = SLICE_WIDTH * REACH
    rim = REACH * BLOCK
    x_unit = jnp.array([1.0, 0.0, 0.0], jnp.float32)[:, None]
    valid = (jnp.arange(atoms) % BLOCK < jnp.repeat(block_count, BLOCK)).astype(jnp.float32)
    onehot = (species[None, :] == jnp.arange(NSPEC)[:, None]).astype(jnp.float32)
    gain = jnp.dot(species_gain.T, onehot, precision=HIGH)
    w_cols = lax.dynamic_slice_in_dim(w_in, lane * local_channels, local_channels, 1)
    mixed = jnp.einsum(
        "kc,ka->ca",
        w_cols,
        lax.all_gather(features, "chan", axis=0, tiled=True),
        preferred_element_type=jnp.float32,
    )
    source = (mixed * gain * valid).astype(jnp.bfloat16)
    grad_in = cotangent * valid.astype(jnp.bfloat16)[None, None, :]
    table = wave_table(positions, wave_ints, length)
    weight = wave_weight(wave_ints, length) * (1.0 / math.sqrt(wave_ints.shape[1] * atoms * spaces))
    local_sums = jnp.einsum("ka,ca->kc", table, source, preferred_element_type=jnp.float32)
    local_grads = jnp.einsum("ka,ca->kc", table, grad_in[0], preferred_element_type=jnp.float32)
    sums = lax.psum(local_sums, "space")
    far_field = jnp.einsum(
        "kc,ka->ca",
        (sums * weight[:, None]).astype(jnp.bfloat16),
        table,
        preferred_element_type=jnp.float32,
    )
    stacked = jnp.concatenate([source[None], grad_in], 0)
    ahead = passed_along(stacked, "space", -1)
    ahead_pos = passed_along(positions, "space", -1)
    ahead_pos = ahead_pos + jnp.where(place == spaces - 1, length, 0.0) * x_unit
    extended = jnp.concatenate([stacked, ahead], 2)
    extended_pos = jnp.concatenate([positions, ahead_pos], 1)

    def self_step(block, total):
        start = block * BLOCK
        pos = lax.dynamic_slice_in_dim(extended_pos, start, BLOCK, 1)
        data = lax.dynamic_slice_in_dim(extended, start, BLOCK, 2)
        home_msg, far_dx, far_msg, home_dx = pair_terms(pos, pos, data, data, w_rad, cutoff, True)
        return add_block(total, jnp.concatenate([home_msg, far_dx[None]], 0), start)

    total = jnp.zeros((stacked.shape[0], local_channels, atoms + rim), jnp.float32)
    total = lax.fori_loop(0, blocks, self_step, total)

    def cross_step(slot, total):
        home_start = pair_home[slot] * BLOCK
        far_start = (pair_home[slot] + pair_reach[slot]) * BLOCK
        pos_home = lax.dynamic_slice_in_dim(extended_pos, home_start, BLOCK, 1)
        pos_far = lax.dynamic_slice_in_dim(extended_pos, far_start, BLOCK, 1)
        data_home = lax.dynamic_slice_in_dim(extended, home_start, BLOCK, 2)
        data_far = lax.dynamic_slice_in_dim(extended, far_start, BLOCK, 2)
        home_msg, far_dx, far_msg, home_dx = pair_terms(
            pos_home, pos_far, data_home, data_far, w_rad, cutoff, False
        )
        total = add_block(total, jnp.concatenate([home_msg, home_dx[None]], 0), home_start)
        return add_block(total, jnp.concatenate([far_msg, far_dx[None]], 0), far_start)

    total = lax.fori_loop(0, pair_count[0], cross_step, total)
    returned = passed_along(total[:, :, atoms:].astype(jnp.bfloat16), "space", 1).astype(
        jnp.float32
    )
    near = total[:, :, :atoms].at[:, :, :rim].add(returned)
    first = near[0] + far_field
    messages = (jnp.concatenate([first[None], near[1:9]], 0) * valid).astype(jnp.bfloat16)
    grads = lax.psum(local_grads, "space")
    far_grad = jnp.einsum(
        "kc,ka->ca",
        (grads * weight[:, None]).astype(jnp.bfloat16),
        table,
        preferred_element_type=jnp.float32,
    )
    scaled = ((near[9] + far_grad) * gain * valid).astype(jnp.bfloat16)
    w_rows = lax.dynamic_slice_in_dim(w_in, lane * local_channels, local_channels, 0)
    grad_features = jnp.dot(
        w_rows,
        lax.all_gather(scaled, "chan", axis=0, tiled=True),
        preferred_element_type=jnp.float32,
    )
    return (messages, grad_features)


def solution(mesh):
    return jax.shard_map(
        on_device,
        mesh=mesh,
        in_specs=(
            P("chan", "space"),
            P(None, "space"),
            P("space"),
            P("space"),
            P("space"),
            P("space"),
            P("space"),
            P(),
            P(None, "chan"),
            P(),
            P(None, "chan"),
            P(None, "chan", "space"),
        ),
        out_specs=(P(None, "chan", "space"), P("chan", "space")),
        check_vma=False,
    )
```

profile of v0, /device:TPU:17, one launch (start us, length us, event | category | flops | bytes accessed | tf_op | source)
XLA Modules:
  0.0 519.9 jit_solution(13406611545747681216)
XLA Ops:
  9.2 6.2 %all_gather.6 = bf16[128,256]{1,0:T(8,128)(2,1)S(1)} all-gather(bf16[32,256]{1,0:T(8,128)(2,1)} %param.24), channel_id=1, replica_groups=mesh['space'=8,'chan'=4] {'chan'}, dimensions={0}, use_global_device_ids=true | all-gather | bytes 81920 | tf_op jit(solution)/shard_map/all_gather | solution.py:130
  20.1 4.3 cosine_convert_fusion
  26.9 2.8 copy.91
  30.6 39.3 %while.26 = (s32[]{:T(128)}, f32[10,32,512]{2,1,0:T(8,128)}, f32[3,512]{1,0:T(4,128)S(1)}, f32[16,32]{1,0:T(8,128)S(1)}, bf16[10,32,512]{1,0,2:T(8,128)(2,1)}, /...) while((s32[]{:T(128)}, f32[10,32,512]{2,1,0:T(8,128)}, f32[3,512]{1,0:T(4,128)S(1)}, ...), condition=%wide.region_2.3_spmd, body=%wide.region_0.2_spmd.sunk | while | flops 54378532 | bytes 3744319 | solution.py:161
  32.1 1.8 fusion.106
  34.9 1.9 convolution_bitcast_fusion.13
  37.9 1.7 dynamic_update_slice.20
  41.2 1.8 fusion.106
  44.0 1.9 convolution_bitcast_fusion.13
  47.1 3.2 dynamic_update_slice.20
  51.7 1.8 fusion.106
  54.5 1.9 convolution_bitcast_fusion.13
  60.8 1.8 fusion.106
  63.6 1.9 convolution_bitcast_fusion.13
  66.7 3.2 dynamic_update_slice.20
  69.9 130.8 %while.27 = (s32[]{:T(128)}, f32[10,32,512]{2,1,0:T(8,128)}, s32[]{:T(128)}, s32[16]{0:T(128)S(1)}, s32[16]{0:T(128)S(1)}, /*index=5*/f32[3,512]{1,0:T(4,128)S(1...) while((s32[]{:T(128)}, f32[10,32,512]{2,1,0:T(8,128)}, ...), condition=%wide.region_6.7_spmd.clone, body=%wide.region_3.6_spmd.sunk.clone.sunk | while | flops 83083312 | bytes 9731859 | solution.py:176
  77.3 2.0 copy.121
  79.3 2.6 broadcast_multiply_fusion.7
  82.0 1.9 convolution_bitcast_fusion.14
  85.9 1.8 dynamic_update_slice.21
  87.6 1.8 fusion.117
  90.5 1.7 convolution_bitcast_fusion.15
  102.4 2.0 copy.121
  104.4 2.6 broadcast_multiply_fusion.7
  107.2 1.9 convolution_bitcast_fusion.14
  111.0 3.2 dynamic_update_slice.21
  114.2 1.8 fusion.117
  117.1 1.7 convolution_bitcast_fusion.15
  129.0 2.0 copy.121
  131.0 2.6 broadcast_multiply_fusion.7
  133.8 1.9 convolution_bitcast_fusion.14
  139.3 1.8 fusion.117
  142.2 1.7 convolution_bitcast_fusion.15
  145.2 3.2 dynamic_update_slice.22
  155.6 2.0 copy.121
  157.6 2.6 broadcast_multiply_fusion.7
  160.3 1.9 convolution_bitcast_fusion.14
  164.2 1.7 dynamic_update_slice.21
  165.9 1.8 fusion.117
  168.8 1.7 convolution_bitcast_fusion.15
  171.8 3.2 dynamic_update_slice.22
  182.2 2.0 copy.121
  184.2 2.6 broadcast_multiply_fusion.7
  186.9 1.9 convolution_bitcast_fusion.14
  192.5 1.8 fusion.117
  201.8 295.8 %collective-permute-start.2 = (bf16[10,32,256]{2,1,0:T(8,128)(2,1)S(1)}, bf16[10,32,256]{2,1,0:T(8,128)(2,1)S(1)}, u32[]{:S(2)}, u32[]{:S(2)}) collective-permute-start(bf16[10,32,256]{2,1,0:T(8,128)(2,1)S(1)} %slice.230), channel_id=1, source_target_pairs={{28,0},{0,4},{4,8},{8,12},{12,16},{16,20},{20,24},{24,28},{29,1},{... | collective-permute-start | bytes 491528 | tf_op jit(solution)/shard_map/ppermute | solution.py:24
  498.4 3.3 collective-permute-done.2
  505.5 6.1 %all_gather.7 = bf16[128,256]{1,0:T(8,128)(2,1)S(1)} all-gather(bf16[32,256]{1,0:T(8,128)(2,1)S(1)} %fusion.60), channel_id=1, replica_groups=mesh['space'=8,'chan'=4] {'chan'}, dimensions={0}, use_global_device_ids=true | all-gather | bytes 81920 | tf_op jit(solution)/shard_map/all_gather | solution.py:194
  (301 shorter events, 87.9 us)
Async XLA Ops:
  7.2 10.1 %copy-start = (bf16[128,128]{1,0:T(8,128)(2,1)S(1)}, bf16[128,128]{1,0:T(8,128)(2,1)}, u32[]{:S(2)}) copy-start(bf16[128,128]{1,0:T(8,128)(2,1)} %param.33) | copy-start | bytes 98308
  7.2 495.5 %all-reduce.3.cloned.1.call-start = ((), (), s32[]{:S(2)}) async-start(), calls=%async_computation | async-start | bytes 1048576 | tf_op jit(solution)/shard_map/psum | solution.py:139
  7.2 19.5 %collective-permute-start = (f32[3,256]{1,0:T(4,128)}, f32[3,256]{1,0:T(4,128)S(1)}, u32[]{:S(2)}, u32[]{:S(2)}) collective-permute-start(f32[3,256]{1,0:T(4,128)} %param.25), channel_id=1, source_target_pairs={{4,0},{8,4},{12,8},{16,12},{20,16},{24,20},{28,24},{0,28},{5,1},{9... | collective-permute-start | bytes 9224 | tf_op jit(solution)/shard_map/ppermute | solution.py:24
  9.2 8.3 %copy-start.9 = (f32[256]{0:T(256)}, f32[256]{0:T(256)S(1)}, u32[]{:S(2)}) copy-start(f32[256]{0:T(256)S(1)} %get-tuple-element.279) | copy-start | bytes 3076
  17.5 9.3 %collective-permute-start.1 = (bf16[10,32,256]{2,1,0:T(8,128)(2,1)S(1)}, bf16[10,32,256]{2,1,0:T(8,128)(2,1)S(1)}, u32[]{:S(2)}, u32[]{:S(2)}) collective-permute-start(bf16[10,32,256]{2,1,0:T(8,128)(2,1)S(1)} %pad_maximum_fusion.2), channel_id=1, source_target_pairs={{4,0},{8,4},{12,8},{16,12},{20,16},{24,20},{28,24},{0,28},{5,1},{9... | collective-permute-start | bytes 491528 | tf_op jit(solution)/shard_map/ppermute | solution.py:24
  24.4 1.2 copy-start.2
  24.4 1.2 copy-start.4
  24.4 2.3 copy-start.15
  24.4 2.4 copy-start.8
  26.7 3.9 copy-start.1
  30.6 39.3 %copy-start.6 = (f32[9]{0:T(128)S(1)}, f32[9]{0:T(128)}, u32[]{:S(2)}) copy-start(f32[9]{0:T(128)} %constant.219.clone..sunk.2) | copy-start | bytes 112
  30.6 39.3 %copy-start.11 = (s32[16]{0:T(128)S(1)}, s32[16]{0:T(128)}, u32[]{:S(2)}) copy-start(s32[16]{0:T(128)} %param.28) | copy-start | bytes 196
  30.6 39.3 %copy-start.13 = (s32[16]{0:T(128)S(1)}, s32[16]{0:T(128)}, u32[]{:S(2)}) copy-start(s32[16]{0:T(128)} %param.29) | copy-start | bytes 196
  90.5 4.7 copy-start.7
  90.5 4.7 copy-start.12
  90.5 4.7 copy-start.14
  117.1 4.7 copy-start.7
  117.1 4.7 copy-start.12
  117.1 4.7 copy-start.14
  142.2 6.2 %copy-start.7 = (f32[9]{0:T(128)S(1)}, f32[9]{0:T(128)}, u32[]{:S(2)}) copy-start(f32[9]{0:T(128)} %get-tuple-element.502) | copy-start | bytes 112 | tf_op jit(solution)/shard_map/while
  142.2 6.2 %copy-start.12 = (s32[16]{0:T(128)S(1)}, s32[16]{0:T(128)}, u32[]{:S(2)}) copy-start(s32[16]{0:T(128)} %get-tuple-element.524) | copy-start | bytes 196 | tf_op jit(solution)/shard_map/while
  142.2 6.2 %copy-start.14 = (s32[16]{0:T(128)S(1)}, s32[16]{0:T(128)}, u32[]{:S(2)}) copy-start(s32[16]{0:T(128)} %get-tuple-element.542) | copy-start | bytes 196 | tf_op jit(solution)/shard_map/while
  168.8 6.2 %copy-start.7 = (f32[9]{0:T(128)S(1)}, f32[9]{0:T(128)}, u32[]{:S(2)}) copy-start(f32[9]{0:T(128)} %get-tuple-element.502) | copy-start | bytes 112 | tf_op jit(solution)/shard_map/while
  168.8 6.2 %copy-start.12 = (s32[16]{0:T(128)S(1)}, s32[16]{0:T(128)}, u32[]{:S(2)}) copy-start(s32[16]{0:T(128)} %get-tuple-element.524) | copy-start | bytes 196 | tf_op jit(solution)/shard_map/while
  168.8 6.2 %copy-start.14 = (s32[16]{0:T(128)S(1)}, s32[16]{0:T(128)}, u32[]{:S(2)}) copy-start(s32[16]{0:T(128)} %get-tuple-element.542) | copy-start | bytes 196 | tf_op jit(solution)/shard_map/while
  195.4 4.6 copy-start.7
  195.4 4.6 copy-start.12
  195.4 4.6 copy-start.14
  200.6 303.6 %copy-start.3 = (bf16[1024,256]{1,0:T(8,128)(2,1)S(1)}, bf16[1024,256]{1,0:T(8,128)(2,1)}, u32[]{:S(2)}) copy-start(bf16[1024,256]{1,0:T(8,128)(2,1)} %copy-done.2) | copy-start | bytes 1572868
  200.7 303.6 %copy-start.5 = (bf16[1024,256]{1,0:T(8,128)(2,1)S(1)}, bf16[1024,256]{1,0:T(8,128)(2,1)}, u32[]{:S(2)}) copy-start(bf16[1024,256]{1,0:T(8,128)(2,1)} %copy-done.4) | copy-start | bytes 1572868
  200.7 303.6 %copy-start.10 = (f32[256]{0:T(256)S(1)}, f32[256]{0:T(256)}, u32[]{:S(2)}) copy-start(f32[256]{0:T(256)} %copy-done.9) | copy-start | bytes 3076
  201.8 299.9 %collective-permute-start.2 = (bf16[10,32,256]{2,1,0:T(8,128)(2,1)S(1)}, bf16[10,32,256]{2,1,0:T(8,128)(2,1)S(1)}, u32[]{:S(2)}, u32[]{:S(2)}) collective-permute-start(bf16[10,32,256]{2,1,0:T(8,128)(2,1)S(1)} %slice.230), channel_id=1, source_target_pairs={{28,0},{0,4},{4,8},{8,12},{12,16},{16,20},{20,24},{24,28},{29,1},{... | collective-permute-start | bytes 491528 | tf_op jit(solution)/shard_map/ppermute | solution.py:24
Sparse Core Ops, SparseCore 0:
  26.8 70.8 all-reduce.2
where the time goes:
time: 526 us; the launch traced here: 520 us
  starting transfers between devices  297 us (56%)
  matrix products  74.4 us (14%)
  local copies, waits for them, and re-layouts  68.3 us (13%)
  other arithmetic  34.7 us (7%)
  loops' own time  15.2 us (3%)
  between operations  14.3 us (3%)
  blocking collectives  12.3 us (2%)
    ppermute x3, starting transfers between devices, passed_along(): return lax.ppermute(block, axis, route)  297 us
    dynamic_update_slice x14, local copies, waits for them, and re-layouts, add_block(): return lax.dynamic_update_slice_in_dim(total, current + update, start, 2)  31.5 us
    dot_general x9, matrix products, pair_filter(): filt = jnp.einsum('rc,rij->cij', w_rad, radial, precision=HIGH)  17.5 us
    dot_general x9, matrix products, pair_terms(): jnp.einsum('lij,cij->lci', harm, filt * source_far[:, None, :], precision...  16.9 us
    dot_general x9, matrix products, pair_terms(): jnp.einsum('lij,lci->cij', harm, grad_home, precision=HIGH)  16 us
    add x14, other arithmetic, add_block(): return lax.dynamic_update_slice_in_dim(total, current + update, start, 2)  14.7 us
    another operation x1, loops' own time, on_device(): total = lax.fori_loop(0, pair_count[0], cross_step, total)  14.7 us
  transfers between devices with their start and end apart: 4, of which 1 were waited for; matrix products, arithmetic and copies ran while one was open for 33% of the time, Pallas kernels for 0%

commit v1 on v0

v1 whole, which is shorter than its diff:
```python
import functools
import math

import jax
import jax.numpy as jnp
from jax import lax
from jax.experimental import pallas as pl
from jax.experimental.pallas import tpu as pltpu
from jax.sharding import PartitionSpec as P

NSPEC = 6
BLOCK = 64
REACH = 4
NRAD = 16
NHARM = 9
KLONG = 8
KMODE = 128
MID = NRAD // 2

SLICE_WIDTH = 0.5
CUTOFF = SLICE_WIDTH * REACH
SIDE_WIDTH = 12.0
GAP_HEIGHT = 24.0
SIDE_CENTRE = 0.75
SCREEN = 0.5
HIGH = lax.Precision.HIGHEST
BF = jnp.bfloat16
F32 = jnp.float32
R3 = math.sqrt(3.0)
R5 = math.sqrt(5.0)
R15 = math.sqrt(15.0)

VMEM = pl.BlockSpec(memory_space=pltpu.VMEM)
SMEM = pl.BlockSpec(memory_space=pltpu.SMEM)


def dot_nt(a, b):
    return lax.dot_general(a, b, (((1,), (1,)), ((), ())), preferred_element_type=F32)


def dot_nn(a, b):
    return lax.dot_general(a, b, (((1,), (0,)), ((), ())), preferred_element_type=F32)


def harmonic_rows(x, y, z):
    s = x * x + y * y + z * z
    return [
        None,
        R3 * x,
        R3 * y,
        R3 * z,
        R15 * x * y,
        R15 * y * z,
        0.5 * R5 * (3.0 * z * z - s),
        R15 * x * z,
        0.5 * R15 * (x * x - y * y),
    ]


def shift_terms(x, y, z):
    q = R15 / R3
    return {
        (1, 0): -R3 * x,
        (2, 0): -R3 * y,
        (3, 0): -R3 * z,
        (4, 1): -q * y,
        (4, 2): -q * x,
        (4, 0): R15 * x * y,
        (5, 3): -q * y,
        (5, 2): -q * z,
        (5, 0): R15 * y * z,
        (6, 3): (-2.0 * R5 / R3) * z,
        (6, 1): (R5 / R3) * x,
        (6, 2): (R5 / R3) * y,
        (6, 0): 0.5 * R5 * (2.0 * z * z - x * x - y * y),
        (7, 3): -q * x,
        (7, 1): -q * z,
        (7, 0): R15 * x * z,
        (8, 1): -q * x,
        (8, 2): q * y,
        (8, 0): 0.5 * R15 * (x * x - y * y),
    }


def sincos_turns(turns):
    r = turns - jnp.floor(turns + 0.5)
    x = r * math.pi
    x2 = x * x
    s = jnp.full_like(x, -1.0 / math.factorial(11))
    for k, sign in ((9, 1.0), (7, -1.0), (5, 1.0), (3, -1.0), (1, 1.0)):
        s = s * x2 + sign / math.factorial(k)
    s = s * x
    c = jnp.full_like(x, 1.0 / math.factorial(12))
    for k, sign in ((10, -1.0), (8, 1.0), (6, -1.0), (4, 1.0), (2, -1.0), (0, 1.0)):
        c = c * x2 + sign / math.factorial(k)
    return 1.0 - 2.0 * s * s, 2.0 * s * c


def valid_row(count_ref, atoms):
    lane = lax.broadcasted_iota(jnp.int32, (1, atoms), 1)
    limit = jnp.zeros((1, atoms), jnp.int32)
    for b in range(atoms // BLOCK):
        limit = jnp.where(lane // BLOCK == b, count_ref[b] + b * BLOCK, limit)
    return (lane < limit).astype(F32)


def gain_rows(species_ref, species_gain_ref):
    ids = species_ref[...]
    rows = lax.broadcasted_iota(jnp.int32, (8, ids.shape[1]), 0)
    onehot = (rows == ids).astype(F32)[:NSPEC]
    return lax.dot_general(
        species_gain_ref[...],
        onehot,
        (((0,), (0,)), ((), ())),
        precision=HIGH,
        preferred_element_type=F32,
    )


def source_kernel(
    count_ref,
    home_ref,
    reach_ref,
    live_ref,
    lane_ref,
    features_ref,
    w_ref,
    species_ref,
    gain_ref,
    pos_ref,
    cot_ref,
    pack_ref,
    mix_ref,
):
    channels, atoms = cot_ref.shape[1], cot_ref.shape[2]
    valid = valid_row(count_ref, atoms)
    gain = gain_rows(species_ref, gain_ref)
    mix_ref[...] = lax.dot_general(
        w_ref[...], features_ref[...], (((0,), (0,)), ((), ())), preferred_element_type=F32
    )
    first = pl.multiple_of(lane_ref[0] * channels, channels)
    mixed = mix_ref[pl.ds(first, channels), :]
    pack_ref[0:channels, :] = (mixed * gain * valid).astype(BF)
    pack_ref[channels : 2 * channels, :] = (cot_ref[0].astype(F32) * valid).astype(BF)
    pos = pos_ref[...]
    top = pos.astype(BF).astype(F32)
    rest = pos - top
    mid = rest.astype(BF).astype(F32)
    low = rest - mid
    lane = lax.broadcasted_iota(jnp.int32, (1, atoms), 1)
    flags = jnp.zeros((1, atoms), F32)
    for p in range(home_ref.shape[0]):
        slot = home_ref[p] * REACH + reach_ref[p] - 1
        flags = jnp.where(jnp.logical_and(lane == slot, p < live_ref[0]), 1.0, flags)
    tail = jnp.concatenate([top, mid, low, flags, valid, jnp.zeros((5, atoms), F32)], 0)
    pack_ref[2 * channels :, :] = tail.astype(BF)


def mode_weights(wave_ref, length, total):
    k = wave_ref[...]
    count = k.shape[1]
    k = jnp.where(k[0:1] < 0, -k, k)
    k1, k2, k3 = k[0:1], k[1:2], k[2:3]
    code = jnp.where(k3 == 4, 76 + k2, (k2 + 4) * 8 + k3 + 4)
    rows = lax.broadcasted_iota(jnp.int32, (KMODE, count), 0)
    hot = (rows == code).astype(F32).astype(BF)
    longs = lax.broadcasted_iota(jnp.int32, (16, count), 0)
    hot1 = (longs == k1).astype(F32).astype(BF)
    mult = dot_nt(hot1, hot)
    lane = lax.broadcasted_iota(jnp.int32, (16, KMODE), 1)
    row = lax.broadcasted_iota(jnp.int32, (16, KMODE), 0)
    g2 = jnp.where(lane < 72, lane // 8 - 4, lane - 76).astype(F32)
    g3 = jnp.where(lane < 72, lane % 8 - 4, 4).astype(F32)
    f1 = row.astype(F32) * (2.0 * math.pi / length)
    f2 = g2 * (2.0 * math.pi / SIDE_WIDTH)
    f3 = g3 * (2.0 * math.pi / GAP_HEIGHT)
    ksq = f1 * f1 + f2 * f2 + f3 * f3
    value = jnp.exp(-0.5 * ksq) / (ksq + SCREEN * SCREEN) * (1.0 / math.sqrt(count * total))
    return jnp.where(mult > 0.0, mult * value, 0.0)


def phase_rows(x, y, z, length):
    atoms = x.shape[1]
    step = lax.broadcasted_iota(jnp.int32, (8, atoms), 0).astype(F32)
    first = sincos_turns((step + 1.0) * (x * (1.0 / length)))
    second = sincos_turns((step - 4.0) * (y * (1.0 / SIDE_WIDTH)))
    third = sincos_turns((step - 4.0) * (z * (1.0 / GAP_HEIGHT)))
    return first, second, third


def mode_table(second, third):
    c2, s2 = second
    c3, s3 = third
    atoms = c2.shape[1]
    cos, sin = [], []
    for k2 in range(9):
        a = c2[k2 : k2 + 1] if k2 < 8 else c2[0:1]
        b = s2[k2 : k2 + 1] if k2 < 8 else -s2[0:1]
        cos.append(a * c3 - b * s3)
        sin.append(a * s3 + b * c3)
    a, b = c3[0:1], -s3[0:1]
    cos.append(c2 * a - s2 * b)
    sin.append(c2 * b + s2 * a)
    one = lax.broadcasted_iota(jnp.int32, (8, atoms), 0) == 0
    cos.append(jnp.where(one, c2[0:1] * a + s2[0:1] * b, 0.0))
    sin.append(jnp.where(one, c2[0:1] * b - s2[0:1] * a, 0.0))
    pad = jnp.zeros((KMODE - 88, atoms), F32)
    return jnp.concatenate(cos + [pad] + sin + [pad], 0).astype(BF)


def unpack_pos(tail):
    t = tail.astype(F32)
    pos = (t[0:3] + t[3:6]) + t[6:9]
    return pos[0:1], pos[1:2], pos[2:3]


def far_part(spaces, length, wave_ref, gath_ref, terms_ref, modes_ref, rows_per):
    atoms = gath_ref.shape[2]
    group = min(spaces, modes_ref.shape[1] // atoms)
    weights = mode_weights(wave_ref, length, atoms * spaces)

    def fill(s, base):
        tile = gath_ref[base + s]
        x, y, z = unpack_pos(tile[rows_per : rows_per + 16])
        first, second, third = phase_rows(x, y, z, length)
        at = pl.ds(pl.multiple_of(s * atoms, atoms), atoms)
        modes_ref[:, at] = mode_table(second, third)
        data = tile[0:rows_per].astype(F32)
        terms_ref[0:rows_per, at] = tile[0:rows_per]
        for k in range(KLONG):
            lo = (1 + 2 * k) * rows_per
            terms_ref[lo : lo + rows_per, at] = (data * first[0][k : k + 1]).astype(BF)
            terms_ref[lo + rows_per : lo + 2 * rows_per, at] = (
                data * first[1][k : k + 1]
            ).astype(BF)
        return base

    sums = None
    for base in range(0, spaces, group):
        lax.fori_loop(0, group, fill, base)
        part = dot_nt(terms_ref[...], modes_ref[...])
        sums = part if sums is None else sums + part
    tile = gath_ref[0]
    x, y, z = unpack_pos(tile[rows_per : rows_per + 16])
    first, second, third = phase_rows(x, y, z, length)
    own = mode_table(second, third)
    rows_re, rows_im = [], []
    for k in range(KLONG + 1):
        w = weights[k : k + 1]
        if k == 0:
            real = sums[0:rows_per]
            cos, sin = real[:, :KMODE], real[:, KMODE:]
        else:
            lo = (2 * k - 1) * rows_per
            real, imag = sums[lo : lo + rows_per], sums[lo + rows_per : lo + 2 * rows_per]
            cos = real[:, :KMODE] - imag[:, KMODE:]
            sin = real[:, KMODE:] + imag[:, :KMODE]
        cos, sin = cos * w, sin * w
        rows_re.append(jnp.concatenate([cos, sin], 1))
        if k > 0:
            rows_im.append(jnp.concatenate([sin, -cos], 1))
    waves = jnp.concatenate(rows_re + rows_im, 0).astype(BF)
    back = dot_nn(waves, own)
    far = back[0:rows_per]
    for k in range(KLONG):
        lo = (1 + k) * rows_per
        far = far + back[lo : lo + rows_per] * first[0][k : k + 1]
        lo = (1 + KLONG + k) * rows_per
        far = far + back[lo : lo + rows_per] * first[1][k : k + 1]
    return far


def main_kernel(
    spaces,
    place_ref,
    gath_ref,
    cot_prev_ref,
    cot_ref,
    cot_next_ref,
    wave_ref,
    w_rad_ref,
    species_ref,
    gain_ref,
    messages_ref,
    scaled_ref,
    radial_ref,
    left_ref,
    cols_ref,
    live_ref,
    filt_ref,
    total_ref,
    terms_ref,
    modes_ref,
):
    channels, atoms = cot_ref.shape[1], cot_ref.shape[2]
    blocks = atoms // BLOCK
    rows = 2 * channels
    length = SLICE_WIDTH * blocks * spaces
    place = place_ref[0]
    before = lax.rem(place + spaces - 1, spaces)
    after = lax.rem(place + 1, spaces)
    tiles = [gath_ref[before ^ place], gath_ref[0], gath_ref[after ^ place]]
    shifts = [
        jnp.where(place == 0, -length, 0.0),
        0.0,
        jnp.where(place == spaces - 1, length, 0.0),
    ]
    centre = (place.astype(F32) + 0.5) * (SLICE_WIDTH * blocks)
    lane = lax.broadcasted_iota(jnp.int32, (1, atoms), 1)
    home = lane // BLOCK

    def flag_row(tail, h, r):
        index = h * REACH + r - 1
        return jnp.broadcast_to(tail[9:10, index : index + 1].astype(F32), (1, atoms))

    coords, valids = [], []
    for t in range(3):
        tail = tiles[t][rows : rows + 16]
        x, y, z = unpack_pos(tail)
        x = (x - (centre - shifts[t])) * (1.0 / CUTOFF)
        y = (y - SIDE_CENTRE) * (1.0 / CUTOFF)
        z = (z - SIDE_CENTRE) * (1.0 / CUTOFF)
        coords.append((x, y, z))
        valids.append(tail[10:11].astype(F32))
        padded = jnp.concatenate([x, y, z, jnp.zeros((5, atoms), F32)], 0)
        cols_ref[t * atoms : (t + 1) * atoms, :] = padded.T
    for e in range(3 * blocks):
        row = jnp.zeros((1, atoms), F32)
        for h in range(blocks):
            d = e - blocks - h
            if abs(d) > REACH:
                continue
            if d == 0:
                value = jnp.ones((1, atoms), F32)
            elif d > 0:
                value = flag_row(tiles[1][rows : rows + 16], h, d)
            elif h + d >= 0:
                value = flag_row(tiles[1][rows : rows + 16], h + d, -d)
            else:
                value = flag_row(tiles[0][rows : rows + 16], h + d + blocks, -d)
            row = jnp.where(home == h, value, row)
        live_ref[e : e + 1, :] = row

    w_cols = w_rad_ref[...].T
    for n in range(NRAD):
        filt_ref[n] = jnp.broadcast_to(w_cols[:, n : n + 1], (channels, atoms))

    for t, cot in enumerate((cot_prev_ref, cot_ref, cot_next_ref)):
        x, y, z = coords[t]
        at = slice(t * atoms, (t + 1) * atoms)
        left_ref[0:channels, at] = tiles[t][0:channels]
        source = tiles[t][0:channels].astype(F32)
        harm = harmonic_rows(x, y, z)
        for m in range(1, NHARM):
            left_ref[m * channels : (m + 1) * channels, at] = (source * harm[m]).astype(BF)
        grads = [cot[l].astype(F32) * valids[t] for l in range(NHARM)]
        moved = list(grads)
        for (l, m), term in shift_terms(x, y, z).items():
            moved[m] = moved[m] + grads[l] * term
        for m in range(NHARM):
            lo = (NHARM + m) * channels
            left_ref[lo : lo + channels, at] = moved[m].astype(BF)

    xa, ya, za = coords[1]
    chunk = 16

    def radial_step(step, carry):
        lo = pl.multiple_of(step * chunk, chunk)
        at = pl.ds(lo, chunk)
        col = cols_ref[at, :]
        dx = col[:, 0:1] - xa
        dy = col[:, 1:2] - ya
        dz = col[:, 2:3] - za
        s = jnp.minimum(dx * dx + dy * dy + dz * dz, 1.0)
        live = live_ref[pl.ds(lo // BLOCK, 1), :]
        other = lax.broadcasted_iota(jnp.int32, (chunk, atoms), 0) + (lo - atoms)
        me = lax.broadcasted_iota(jnp.int32, (chunk, atoms), 1)
        gap = 1.0 - s
        envelope = jnp.where(other == me, 0.0, gap * gap * live)
        off = s - MID / (NRAD - 1)
        middle = envelope * jnp.exp(-0.5 * (NRAD - 1) ** 2 * (off * off))
        radial_ref[MID, at, :] = middle.astype(BF)
        grow = jnp.exp((NRAD - 1.0) * s)
        value = middle
        for n in range(MID, NRAD - 1):
            value = value * (grow * math.exp(-(2 * n + 1) / 2))
            radial_ref[n + 1, at, :] = value.astype(BF)
        shrink = jnp.exp((1.0 - NRAD) * s)
        value = middle
        for n in range(MID, 0, -1):
            value = value * (shrink * math.exp((2 * n - 1) / 2))
            radial_ref[n - 1, at, :] = value.astype(BF)
        return carry

    lax.fori_loop(0, 3 * atoms // chunk, radial_step, 0)

    total_ref[...] = jnp.zeros_like(total_ref)

    def mix_step(n, carry):
        part = dot_nn(left_ref[...], radial_ref[n])
        total_ref[...] += part.reshape(2 * NHARM, channels, atoms) * filt_ref[n][None]
        return carry

    lax.fori_loop(0, NRAD, mix_step, 0)

    far = far_part(spaces, length, wave_ref, gath_ref, terms_ref, modes_ref, rows)
    valid = valids[1]
    sums = [total_ref[m] for m in range(NHARM)]
    near = list(sums)
    for (l, m), term in shift_terms(xa, ya, za).items():
        near[l] = near[l] + sums[m] * term
    near[0] = near[0] + far[0:channels]
    for l in range(NHARM):
        messages_ref[l] = (near[l] * valid).astype(BF)
    harm = harmonic_rows(xa, ya, za)
    grad = total_ref[NHARM] + far[channels:rows]
    for m in range(1, NHARM):
        grad = grad + total_ref[NHARM + m] * harm[m]
    gain = gain_rows(species_ref, gain_ref)
    scaled_ref[...] = (grad * gain * valid).astype(BF)


def final_kernel(lane_ref, w_ref, scaled_ref, out_ref):
    channels = out_ref.shape[0]
    first = pl.multiple_of(lane_ref[0] * channels, channels)
    out_ref[...] = dot_nn(w_ref[pl.ds(first, channels), :], scaled_ref[...])


def gathered(pack, axis):
    count = lax.axis_size(axis)
    held = pack[None]
    bit = 1
    while bit < count:
        other = lax.ppermute(held, axis, [(i, i ^ bit) for i in range(count)])
        held = jnp.concatenate([held, other], 0)
        bit *= 2
    return held


def passed_along(block, axis, distance):
    count = lax.axis_size(axis)
    return lax.ppermute(block, axis, [((i - distance) % count, i) for i in range(count)])


def on_device(
    features,
    positions,
    species,
    block_count,
    pair_home,
    pair_reach,
    pair_count,
    wave_ints,
    species_gain,
    w_in,
    w_rad,
    cotangent,
):
    channels, atoms = features.shape
    spaces = lax.axis_size("space")
    place = lax.axis_index("space").astype(jnp.int32).reshape(1)
    lane = lax.axis_index("chan").astype(jnp.int32).reshape(1)
    params = pltpu.CompilerParams(vmem_limit_bytes=48 * 1024 * 1024)
    rows = 2 * channels
    species = species.reshape(1, atoms)

    cot_prev = passed_along(cotangent, "space", 1)
    cot_next = passed_along(cotangent, "space", -1)
    mixed_from = lax.all_gather(features, "chan", axis=0, tiled=True)
    pack = pl.pallas_call(
        source_kernel,
        out_shape=jax.ShapeDtypeStruct((rows + 16, atoms), BF),
        in_specs=[SMEM] * 5 + [VMEM] * 6,
        out_specs=VMEM,
        scratch_shapes=[pltpu.VMEM((w_in.shape[1], atoms), F32)],
        compiler_params=params,
        name="source",
    )(
        block_count,
        pair_home,
        pair_reach,
        pair_count,
        lane,
        mixed_from,
        w_in,
        species,
        species_gain,
        positions,
        cotangent,
    )
    gath = gathered(pack, "space")
    group = min(spaces, 8) * atoms
    messages, scaled = pl.pallas_call(
        functools.partial(main_kernel, spaces),
        out_shape=(
            jax.ShapeDtypeStruct((NHARM, channels, atoms), BF),
            jax.ShapeDtypeStruct((channels, atoms), BF),
        ),
        in_specs=[SMEM] + [VMEM] * 8,
        out_specs=(VMEM, VMEM),
        scratch_shapes=[
            pltpu.VMEM((NRAD, 3 * atoms, atoms), BF),
            pltpu.VMEM((2 * NHARM * channels, 3 * atoms), BF),
            pltpu.VMEM((3 * atoms, 8), F32),
            pltpu.VMEM((16, atoms), F32),
            pltpu.VMEM((NRAD, channels, atoms), F32),
            pltpu.VMEM((2 * NHARM, channels, atoms), F32),
            pltpu.VMEM(((2 * KLONG + 1) * rows, group), BF),
            pltpu.VMEM((2 * KMODE, group), BF),
        ],
        compiler_params=params,
        name="main",
    )(
        place,
        gath,
        cot_prev,
        cotangent,
        cot_next,
        wave_ints,
        w_rad,
        species,
        species_gain,
    )
    all_scaled = lax.all_gather(scaled, "chan", axis=0, tiled=True)
    grad_features = pl.pallas_call(
        final_kernel,
        out_shape=jax.ShapeDtypeStruct((channels, atoms), F32),
        in_specs=[SMEM, VMEM, VMEM],
        out_specs=VMEM,
        compiler_params=params,
        name="final",
    )(lane, w_in, all_scaled)
    return (messages, grad_features)


def solution(mesh):
    return jax.shard_map(
        on_device,
        mesh=mesh,
        in_specs=(
            P("chan", "space"),
            P(None, "space"),
            P("space"),
            P("space"),
            P("space"),
            P("space"),
            P("space"),
            P(),
            P(None, "chan"),
            P(),
            P(None, "chan"),
            P(None, "chan", "space"),
        ),
        out_specs=(P(None, "chan", "space"), P("chan", "space")),
        check_vma=False,
    )
```

time: 526 us -> 54.1 us (0.10)
  the two profiles are of different devices: /device:TPU:17 before, /device:TPU:0 now
where the time goes in v1:
time: 54.1 us; the launch traced here: 53.5 us
  Pallas kernels  19.2 us (35%)
  starting transfers between devices  11.9 us (22%)
  blocking collectives  11.8 us (22%)
  waiting for transfers between devices  8.53 us (16%)
  between operations  1.42 us (3%)
  local copies, waits for them, and re-layouts  0.65 us (1%)
    pallas_call x1, Pallas kernels, on_device(): pl.pallas_call(functools.partial(main_kernel, spaces), out_shape=(jax.Sha...  17.2 us
    ppermute x3, starting transfers between devices, gathered(): other = lax.ppermute(held, axis, [(i, i ^ bit) for i in range(count)])  7.19 us
    ppermute x3, waiting for transfers between devices, gathered(): other = lax.ppermute(held, axis, [(i, i ^ bit) for i in range(count)])  6.9 us
    all_gather x1, blocking collectives, on_device(): mixed_from = lax.all_gather(features, 'chan', axis=0, tiled=True)  6.59 us
    all_gather x1, blocking collectives, on_device(): all_scaled = lax.all_gather(scaled, 'chan', axis=0, tiled=True)  5.23 us
    ppermute x2, starting transfers between devices, passed_along(): lax.ppermute(block, axis, [((i - distance) % count, i) for i in range(cou...  4.72 us
    ppermute x2, waiting for transfers between devices, passed_along(): lax.ppermute(block, axis, [((i - distance) % count, i) for i in range(cou...  1.63 us
    pallas_call x1, Pallas kernels, on_device(): pl.pallas_call(source_kernel, out_shape=jax.ShapeDtypeStruct((rows + 16,...  1.17 us
  transfers between devices with their start and end apart: 5, of which 5 were waited for; matrix products, arithmetic and copies ran while one was open for 0% of the time, Pallas kernels for 0%

profile of v1, /device:TPU:0, one launch (start us, length us, event | category | flops | bytes accessed | tf_op | source)
XLA Modules:
  0.0 53.5 jit_solution(4341497315894322322)
XLA Ops:
  0.6 0.0 copy-start
  0.6 0.0 copy-start.4
  0.7 0.0 copy-start.7
  0.7 0.0 copy-start.8
  0.7 6.6 %all_gather.6.features_ref = bf16[128,256]{1,0:T(8,128)(2,1)S(1)} all-gather(bf16[32,256]{1,0:T(8,128)(2,1)} %param.12), channel_id=1, replica_groups=mesh['space'=8,'chan'=4] {'chan'}, dimensions={0}, use_global_device_ids=true | all-gather | bytes 81920 | tf_op jit(solution)/shard_map/all_gather | solution.py:469
  7.3 0.0 copy-start.1
  7.9 0.0 copy-start.5
  7.9 0.0 copy-start.6
  8.0 0.0 copy-done
  8.0 0.0 copy-done.4
  8.0 0.0 copy-done.7
  8.0 0.0 copy-done.8
  8.0 0.0 copy-done.1
  8.0 0.6 %copy-done.5 = s32[256]{0:T(256)S(1)} copy-done((s32[256]{0:T(256)S(1)}, s32[256]{0:T(256)}, u32[]{:S(2)}) %copy-start.5) | copy-done | bytes 1048
  8.6 0.0 copy-done.6
  8.6 1.2 %source.1 = bf16[80,256]{1,0:T(8,128)(2,1)S(1)} custom-call(s32[4]{0:T(128)S(1)} %copy-done.6, s32[16]{0:T(128)S(1)} %copy-done.7, s32[16]{0:T(128)S(1)} %copy-done.8, s32[1]{0:T(128)S(6)} %copy.14.live_ref, s32[1]{0:T(128)} %bitcast.1.lane_ref, bf16[128,256]{1,0:T(8,128)(2,1)S(1)} %all_gather.6.features_ref, bf16[128,128]{1,0:T(8,128)(2,1)S(1)} %copy-done, ...), custom_call_target="tpu_custom_call" | custom-call | tf_op jit(solution)/shard_map/source/pallas_call | solution.py:470
  9.8 2.0 %collective-permute-start = (bf16[1,80,256]{2,1,0:T(8,128)(2,1)S(1)}, bf16[1,80,256]{2,1,0:T(8,128)(2,1)S(1)}, u32[]{:S(2)}, u32[]{:S(2)}) collective-permute-start(bf16[1,80,256]{2,1,0:T(8,128)(2,1)S(1)} %bitcast.4), channel_id=1, source_target_pairs={{0,4},{4,0},{8,12},{12,8},{16,20},{20,16},{24,28},{28,24},{1,5},{5... | collective-permute-start | bytes 122888 | tf_op jit(solution)/shard_map/ppermute | solution.py:434
  11.8 2.1 %collective-permute-done = bf16[1,80,256]{2,1,0:T(8,128)(2,1)S(1)} collective-permute-done((bf16[1,80,256]{2,1,0:T(8,128)(2,1)S(1)}, bf16[1,80,256]{2,1,0:T(8,128)(2,1)S(1)}, u32[]{:S(2)}, u32[]{:S(2)}) %collective-permute-start) | collective-permute-done | bytes 40992 | tf_op jit(solution)/shard_map/ppermute | solution.py:434
  13.9 2.1 %collective-permute-start.1 = (bf16[2,80,256]{2,1,0:T(8,128)(2,1)S(1)}, bf16[2,80,256]{2,1,0:T(8,128)(2,1)S(1)}, u32[]{:S(2)}, u32[]{:S(2)}) collective-permute-start(bf16[2,80,256]{2,1,0:T(8,128)(2,1)S(1)} %pad_maximum_fusion.2), channel_id=1, source_target_pairs={{0,8},{4,12},{8,0},{12,4},{16,24},{20,28},{24,16},{28,20},{1,9},{5... | collective-permute-start | bytes 245768 | tf_op jit(solution)/shard_map/ppermute | solution.py:434
  16.0 2.4 %collective-permute-done.1 = bf16[2,80,256]{2,1,0:T(8,128)(2,1)S(1)} collective-permute-done((bf16[2,80,256]{2,1,0:T(8,128)(2,1)S(1)}, bf16[2,80,256]{2,1,0:T(8,128)(2,1)S(1)}, u32[]{:S(2)}, u32[]{:S(2)}) %collective-permute-start.1) | collective-permute-done | bytes 81952 | tf_op jit(solution)/shard_map/ppermute | solution.py:434
  18.4 3.1 %collective-permute-start.2 = (bf16[4,80,256]{2,1,0:T(8,128)(2,1)S(1)}, bf16[4,80,256]{2,1,0:T(8,128)(2,1)S(1)}, u32[]{:S(2)}, u32[]{:S(2)}) collective-permute-start(bf16[4,80,256]{2,1,0:T(8,128)(2,1)S(1)} %pad_maximum_fusion.1), channel_id=1, source_target_pairs={{0,16},{4,20},{8,24},{12,28},{16,0},{20,4},{24,8},{28,12},{1,17},{... | collective-permute-start | bytes 491528 | tf_op jit(solution)/shard_map/ppermute | solution.py:434
  21.5 1.5 %collective-permute-start.3 = (bf16[9,32,256]{2,1,0:T(8,128)(2,1)}, bf16[9,32,256]{2,1,0:T(8,128)(2,1)S(1)}, u32[]{:S(2)}, u32[]{:S(2)}) collective-permute-start(bf16[9,32,256]{2,1,0:T(8,128)(2,1)} %cot_ref.3), channel_id=1, source_target_pairs={{28,0},{0,4},{4,8},{8,12},{12,16},{16,20},{20,24},{24,28},{29,1},{... | collective-permute-start | bytes 442376 | tf_op jit(solution)/shard_map/ppermute | solution.py:442
  23.0 3.2 %collective-permute-start.4 = (bf16[9,32,256]{2,1,0:T(8,128)(2,1)}, bf16[9,32,256]{2,1,0:T(8,128)(2,1)S(1)}, u32[]{:S(2)}, u32[]{:S(2)}) collective-permute-start(bf16[9,32,256]{2,1,0:T(8,128)(2,1)} %cot_ref.3), channel_id=1, source_target_pairs={{4,0},{8,4},{12,8},{16,12},{20,16},{24,20},{28,24},{0,28},{5,1},{9... | collective-permute-start | bytes 442376 | tf_op jit(solution)/shard_map/ppermute | solution.py:442
  26.2 0.0 copy-start.2
  26.2 0.0 copy-start.3
  26.2 2.4 %collective-permute-done.2 = bf16[4,80,256]{2,1,0:T(8,128)(2,1)S(1)} collective-permute-done((bf16[4,80,256]{2,1,0:T(8,128)(2,1)S(1)}, bf16[4,80,256]{2,1,0:T(8,128)(2,1)S(1)}, u32[]{:S(2)}, u32[]{:S(2)}) %collective-permute-start.2) | collective-permute-done | bytes 163872 | tf_op jit(solution)/shard_map/ppermute | solution.py:434
  28.7 1.2 %collective-permute-done.3.cot_prev_ref = bf16[9,32,256]{2,1,0:T(8,128)(2,1)S(1)} collective-permute-done((bf16[9,32,256]{2,1,0:T(8,128)(2,1)}, bf16[9,32,256]{2,1,0:T(8,128)(2,1)S(1)}, u32[]{:S(2)}, u32[]{:S(2)}) %collective-permute-start.3) | collective-permute-done | bytes 147488 | tf_op jit(solution)/shard_map/ppermute | solution.py:442
  29.9 0.4 collective-permute-done.4.cot_next_ref
  30.3 0.0 copy-done.2
  30.3 0.0 copy-done.3
  30.3 17.2 %main.1 = (bf16[9,32,256]{2,1,0:T(8,128)(2,1)}, bf16[32,256]{1,0:T(8,128)(2,1)S(1)}) custom-call(s32[1]{0:T(128)} %bitcast.place_ref, bf16[8,80,256]{2,1,0:T(8,128)(2,1)S(1)} %pad_maximum_fusion.gath_ref, bf16[9,32,256]{2,1,0:T(8,128)(2,1)S(1)} %collective-permute-done.3.cot_prev_ref, bf16[9,32,256]{2,1,0:T(8,128)(2,1)} %cot_ref.3, ...), custom_call_target="tpu_custom_call" | custom-call | tf_op jit(solution)/shard_map/main/pallas_call | solution.py:493
  47.6 5.2 %all_gather.7.scaled_ref = bf16[128,256]{1,0:T(8,128)(2,1)S(1)} all-gather(bf16[32,256]{1,0:T(8,128)(2,1)S(1)} %get-tuple-element.5), channel_id=1, replica_groups=mesh['space'=8,'chan'=4] {'chan'}, dimensions={0}, use_global_device_ids=true | all-gather | bytes 81920 | tf_op jit(solution)/shard_map/all_gather | solution.py:524
  52.8 0.7 %final.1 = f32[32,256]{1,0:T(8,128)} custom-call(s32[1]{0:T(128)} %bitcast.1.lane_ref, bf16[128,128]{1,0:T(8,128)(2,1)S(1)} %copy-done, bf16[128,256]{1,0:T(8,128)(2,1)S(1)} %all_gather.7.scaled_ref), custom_call_target="tpu_custom_call" | custom-call | tf_op jit(solution)/shard_map/final/pallas_call | solution.py:525
  (3 shorter events, 0.1 us)
Async XLA Ops:
  0.6 7.3 %copy-start = (bf16[128,128]{1,0:T(8,128)(2,1)S(1)}, bf16[128,128]{1,0:T(8,128)(2,1)}, u32[]{:S(2)}) copy-start(bf16[128,128]{1,0:T(8,128)(2,1)} %w_ref.3) | copy-start | bytes 98308
  0.6 7.3 %copy-start.4 = (f32[3,256]{1,0:T(4,128)S(1)}, f32[3,256]{1,0:T(4,128)}, u32[]{:S(2)}) copy-start(f32[3,256]{1,0:T(4,128)} %pos_ref.1) | copy-start | bytes 9220
  0.7 7.3 %copy-start.7 = (s32[16]{0:T(128)S(1)}, s32[16]{0:T(128)}, u32[]{:S(2)}) copy-start(s32[16]{0:T(128)} %home_ref.1) | copy-start | bytes 196
  0.7 7.3 %copy-start.8 = (s32[16]{0:T(128)S(1)}, s32[16]{0:T(128)}, u32[]{:S(2)}) copy-start(s32[16]{0:T(128)} %reach_ref.1) | copy-start | bytes 196
  7.3 0.7 %copy-start.1 = (f32[6,32]{1,0:T(8,128)S(1)}, f32[6,32]{1,0:T(8,128)}, u32[]{:S(2)}) copy-start(f32[6,32]{1,0:T(8,128)} %gain_ref.3) | copy-start | bytes 2308
  7.9 0.7 %copy-start.5 = (s32[256]{0:T(256)S(1)}, s32[256]{0:T(256)}, u32[]{:S(2)}) copy-start(s32[256]{0:T(256)} %param.14) | copy-start | bytes 3076
  7.9 0.7 %copy-start.6 = (s32[4]{0:T(128)S(1)}, s32[4]{0:T(128)}, u32[]{:S(2)}) copy-start(s32[4]{0:T(128)} %count_ref.1) | copy-start | bytes 52
  9.8 4.1 %collective-permute-start = (bf16[1,80,256]{2,1,0:T(8,128)(2,1)S(1)}, bf16[1,80,256]{2,1,0:T(8,128)(2,1)S(1)}, u32[]{:S(2)}, u32[]{:S(2)}) collective-permute-start(bf16[1,80,256]{2,1,0:T(8,128)(2,1)S(1)} %bitcast.4), channel_id=1, source_target_pairs={{0,4},{4,0},{8,12},{12,8},{16,20},{20,16},{24,28},{28,24},{1,5},{5... | collective-permute-start | bytes 122888 | tf_op jit(solution)/shard_map/ppermute | solution.py:434
  13.9 4.5 %collective-permute-start.1 = (bf16[2,80,256]{2,1,0:T(8,128)(2,1)S(1)}, bf16[2,80,256]{2,1,0:T(8,128)(2,1)S(1)}, u32[]{:S(2)}, u32[]{:S(2)}) collective-permute-start(bf16[2,80,256]{2,1,0:T(8,128)(2,1)S(1)} %pad_maximum_fusion.2), channel_id=1, source_target_pairs={{0,8},{4,12},{8,0},{12,4},{16,24},{20,28},{24,16},{28,20},{1,9},{5... | collective-permute-start | bytes 245768 | tf_op jit(solution)/shard_map/ppermute | solution.py:434
  18.4 10.2 %collective-permute-start.2 = (bf16[4,80,256]{2,1,0:T(8,128)(2,1)S(1)}, bf16[4,80,256]{2,1,0:T(8,128)(2,1)S(1)}, u32[]{:S(2)}, u32[]{:S(2)}) collective-permute-start(bf16[4,80,256]{2,1,0:T(8,128)(2,1)S(1)} %pad_maximum_fusion.1), channel_id=1, source_target_pairs={{0,16},{4,20},{8,24},{12,28},{16,0},{20,4},{24,8},{28,12},{1,17},{... | collective-permute-start | bytes 491528 | tf_op jit(solution)/shard_map/ppermute | solution.py:434
  21.5 8.4 %collective-permute-start.3 = (bf16[9,32,256]{2,1,0:T(8,128)(2,1)}, bf16[9,32,256]{2,1,0:T(8,128)(2,1)S(1)}, u32[]{:S(2)}, u32[]{:S(2)}) collective-permute-start(bf16[9,32,256]{2,1,0:T(8,128)(2,1)} %cot_ref.3), channel_id=1, source_target_pairs={{28,0},{0,4},{4,8},{8,12},{12,16},{16,20},{20,24},{24,28},{29,1},{... | collective-permute-start | bytes 442376 | tf_op jit(solution)/shard_map/ppermute | solution.py:442
  23.0 7.3 %collective-permute-start.4 = (bf16[9,32,256]{2,1,0:T(8,128)(2,1)}, bf16[9,32,256]{2,1,0:T(8,128)(2,1)S(1)}, u32[]{:S(2)}, u32[]{:S(2)}) collective-permute-start(bf16[9,32,256]{2,1,0:T(8,128)(2,1)} %cot_ref.3), channel_id=1, source_target_pairs={{4,0},{8,4},{12,8},{16,12},{20,16},{24,20},{28,24},{0,28},{5,1},{9... | collective-permute-start | bytes 442376 | tf_op jit(solution)/shard_map/ppermute | solution.py:442
  26.2 4.1 %copy-start.2 = (s32[3,1024]{1,0:T(4,128)S(1)}, s32[3,1024]{1,0:T(4,128)}, u32[]{:S(2)}) copy-start(s32[3,1024]{1,0:T(4,128)} %wave_ref.1) | copy-start | bytes 36868
  26.2 4.1 %copy-start.3 = (f32[16,32]{1,0:T(8,128)S(1)}, f32[16,32]{1,0:T(8,128)}, u32[]{:S(2)}) copy-start(f32[16,32]{1,0:T(8,128)} %w_rad_ref.1) | copy-start | bytes 6148

commit v2 on v0

v2 whole, which is shorter than its diff:
```python
import functools
import math

import jax
import jax.numpy as jnp
from jax import lax
from jax.experimental import pallas as pl
from jax.experimental.pallas import tpu as pltpu
from jax.sharding import PartitionSpec as P

NSPEC = 6
BLOCK = 64
REACH = 4
NRAD = 16
NHARM = 9
KLONG = 8
KMODE = 128
MID = NRAD // 2

SLICE_WIDTH = 0.5
CUTOFF = SLICE_WIDTH * REACH
SIDE_WIDTH = 12.0
GAP_HEIGHT = 24.0
SIDE_CENTRE = 0.75
SCREEN = 0.5
HIGH = lax.Precision.HIGHEST
BF = jnp.bfloat16
F32 = jnp.float32
R3 = math.sqrt(3.0)
R5 = math.sqrt(5.0)
R15 = math.sqrt(15.0)

VMEM = pl.BlockSpec(memory_space=pltpu.VMEM)
SMEM = pl.BlockSpec(memory_space=pltpu.SMEM)


def dot_nt(a, b):
    return lax.dot_general(a, b, (((1,), (1,)), ((), ())), preferred_element_type=F32)


def dot_nn(a, b):
    return lax.dot_general(a, b, (((1,), (0,)), ((), ())), preferred_element_type=F32)


def harmonic_rows(x, y, z):
    s = x * x + y * y + z * z
    return [
        None,
        R3 * x,
        R3 * y,
        R3 * z,
        R15 * x * y,
        R15 * y * z,
        0.5 * R5 * (3.0 * z * z - s),
        R15 * x * z,
        0.5 * R15 * (x * x - y * y),
    ]


def shift_terms(x, y, z):
    q = R15 / R3
    return {
        (1, 0): -R3 * x,
        (2, 0): -R3 * y,
        (3, 0): -R3 * z,
        (4, 1): -q * y,
        (4, 2): -q * x,
        (4, 0): R15 * x * y,
        (5, 3): -q * y,
        (5, 2): -q * z,
        (5, 0): R15 * y * z,
        (6, 3): (-2.0 * R5 / R3) * z,
        (6, 1): (R5 / R3) * x,
        (6, 2): (R5 / R3) * y,
        (6, 0): 0.5 * R5 * (2.0 * z * z - x * x - y * y),
        (7, 3): -q * x,
        (7, 1): -q * z,
        (7, 0): R15 * x * z,
        (8, 1): -q * x,
        (8, 2): q * y,
        (8, 0): 0.5 * R15 * (x * x - y * y),
    }


def sincos_turns(turns):
    r = turns - jnp.floor(turns + 0.5)
    x = r * math.pi
    x2 = x * x
    s = jnp.full_like(x, -1.0 / math.factorial(11))
    for k, sign in ((9, 1.0), (7, -1.0), (5, 1.0), (3, -1.0), (1, 1.0)):
        s = s * x2 + sign / math.factorial(k)
    s = s * x
    c = jnp.full_like(x, 1.0 / math.factorial(12))
    for k, sign in ((10, -1.0), (8, 1.0), (6, -1.0), (4, 1.0), (2, -1.0), (0, 1.0)):
        c = c * x2 + sign / math.factorial(k)
    return 1.0 - 2.0 * s * s, 2.0 * s * c


def valid_row(count_ref, atoms):
    lane = lax.broadcasted_iota(jnp.int32, (1, atoms), 1)
    limit = jnp.zeros((1, atoms), jnp.int32)
    for b in range(atoms // BLOCK):
        limit = jnp.where(lane // BLOCK == b, count_ref[b] + b * BLOCK, limit)
    return (lane < limit).astype(F32)


def gain_rows(species_ref, species_gain_ref):
    ids = species_ref[...]
    rows = lax.broadcasted_iota(jnp.int32, (8, ids.shape[1]), 0)
    onehot = (rows == ids).astype(F32)[:NSPEC]
    return lax.dot_general(
        species_gain_ref[...],
        onehot,
        (((0,), (0,)), ((), ())),
        precision=HIGH,
        preferred_element_type=F32,
    )


def tail_rows(pos, flags, valid):
    atoms = pos.shape[1]
    top = pos.astype(BF).astype(F32)
    rest = pos - top
    mid = rest.astype(BF).astype(F32)
    low = rest - mid
    return jnp.concatenate([top, mid, low, flags, valid, jnp.zeros((5, atoms), F32)], 0).astype(BF)


def prep_kernel(
    live_ref,
    count_hbm,
    home_hbm,
    reach_hbm,
    pos_hbm,
    cot_hbm,
    species_hbm,
    gain_hbm,
    feats_hbm,
    w_hbm,
    halo_ref,
    gain_ref,
    feats_ref,
    w_ref,
    count_ref,
    home_ref,
    reach_ref,
    pos_ref,
    species_ref,
    species_gain_ref,
    sems,
):
    rows, atoms = cot_hbm.shape
    pairs = (
        (count_hbm, count_ref),
        (home_hbm, home_ref),
        (reach_hbm, reach_ref),
        (pos_hbm, pos_ref),
        (species_hbm, species_ref),
        (gain_hbm, species_gain_ref),
        (cot_hbm, halo_ref.at[0:rows, :]),
        (feats_hbm, feats_ref),
        (w_hbm, w_ref),
    )
    copies = [pltpu.make_async_copy(a, b, sems.at[i]) for i, (a, b) in enumerate(pairs)]
    for copy in copies:
        copy.start()
    for copy in copies[:6]:
        copy.wait()
    lane = lax.broadcasted_iota(jnp.int32, (1, atoms), 1)
    flags = jnp.zeros((1, atoms), F32)
    for p in range(home_ref.shape[0]):
        slot = home_ref[p] * REACH + reach_ref[p] - 1
        flags = jnp.where(jnp.logical_and(lane == slot, p < live_ref[0]), 1.0, flags)
    valid = valid_row(count_ref, atoms)
    halo_ref[rows:, :] = tail_rows(pos_ref[...], flags, valid)
    gain_ref[...] = gain_rows(species_ref, species_gain_ref) * valid
    for copy in copies[6:]:
        copy.wait()


def source_kernel(
    lane_ref, own_ref, first_ref, other_ref, w_ref, gain_ref, source_ref, all_ref, mix_ref
):
    channels, atoms = source_ref.shape
    lane = lane_ref[0]
    pieces = [own_ref[...], first_ref[...]]
    if other_ref is not None:
        pieces += [other_ref[m * channels : (m + 1) * channels, :] for m in range(2)]
    for m, piece in enumerate(pieces):
        at = pl.multiple_of((lane ^ m) * channels, channels)
        all_ref[pl.ds(at, channels), :] = piece
    mix_ref[...] = lax.dot_general(
        w_ref[...], all_ref[...], (((0,), (0,)), ((), ())), preferred_element_type=F32
    )
    mixed = mix_ref[pl.ds(pl.multiple_of(lane * channels, channels), channels), :]
    source_ref[...] = (mixed * gain_ref[...]).astype(BF)


def geometry(place, spaces, halos, cols_ref, live_ref, coord_ref):
    atoms = halos[0].shape[1]
    blocks = atoms // BLOCK
    length = SLICE_WIDTH * blocks * spaces
    even = lax.rem(place, 2) == 0
    wrap = jnp.where(place == 0, -length, jnp.where(place == spaces - 1, length, 0.0))
    centre = (place.astype(F32) + 0.5) * (SLICE_WIDTH * blocks)
    lane = lax.broadcasted_iota(jnp.int32, (1, atoms), 1)
    home = lane // BLOCK
    tails = [h[h.shape[0] - 16 :, :] for h in halos]

    def flag_row(tail, h, r):
        index = h * REACH + r - 1
        return jnp.broadcast_to(tail[9:10, index : index + 1].astype(F32), (1, atoms))

    coords, valids = [], []
    for t in range(3):
        x, y, z = unpack_pos(tails[t])
        x = x - (centre - wrap) if t == 2 else x - centre
        x = x * (1.0 / CUTOFF)
        y = (y - SIDE_CENTRE) * (1.0 / CUTOFF)
        z = (z - SIDE_CENTRE) * (1.0 / CUTOFF)
        coords.append((x, y, z))
        valids.append(tails[t][10:11].astype(F32))
        padded = jnp.concatenate([x, y, z, valids[t], jnp.zeros((4, atoms), F32)], 0)
        coord_ref[t] = padded
        cols_ref[t * atoms : (t + 1) * atoms, :] = padded.T
    none = jnp.zeros((1, atoms), F32)
    for e in range(blocks):
        row = none
        for h in range(blocks):
            d = abs(e - h)
            value = none + 1.0 if d == 0 else flag_row(tails[0], min(e, h), d)
            row = jnp.where(home == h, value, row)
        live_ref[e : e + 1, :] = row
        ahead = none
        for h in range(blocks):
            d = e + blocks - h
            if d <= REACH:
                ahead = jnp.where(home == h, flag_row(tails[0], h, d), ahead)
        for t in (1, 2):
            behind = none
            for h in range(blocks):
                d = h + blocks - e
                if d <= REACH:
                    behind = jnp.where(home == h, flag_row(tails[t], e, d), behind)
            is_ahead = even if t == 1 else jnp.logical_not(even)
            live_ref[t * blocks + e : t * blocks + e + 1, :] = jnp.where(is_ahead, ahead, behind)
    return coords[0]


def radial_kernel(
    spaces,
    place_ref,
    own_ref,
    first_ref,
    second_ref,
    wave_ref,
    w_rad_ref,
    radial_ref,
    coord_ref,
    filt_ref,
    weight_ref,
    cols_ref,
    live_ref,
):
    atoms = own_ref.shape[1]
    length = SLICE_WIDTH * (atoms // BLOCK) * spaces
    halos = (own_ref, first_ref, second_ref)
    xa, ya, za = geometry(place_ref[0], spaces, halos, cols_ref, live_ref, coord_ref)
    w_cols = w_rad_ref[...].T
    for n in range(NRAD):
        filt_ref[n] = jnp.broadcast_to(w_cols[:, n : n + 1], filt_ref.shape[1:])
    chunk = BLOCK
    for index in range(3 * atoms // chunk):
        lo = index * chunk
        at = slice(lo, lo + chunk)
        col = cols_ref[at, :]
        dx = col[:, 0:1] - xa
        dy = col[:, 1:2] - ya
        dz = col[:, 2:3] - za
        s = jnp.minimum(dx * dx + dy * dy + dz * dz, 1.0)
        gap = 1.0 - s
        envelope = gap * gap * live_ref[index : index + 1, :]
        if lo < atoms:
            other = lax.broadcasted_iota(jnp.int32, (chunk, atoms), 0) + lo
            me = lax.broadcasted_iota(jnp.int32, (chunk, atoms), 1)
            envelope = jnp.where(other == me, 0.0, envelope)
        off = s - MID / (NRAD - 1)
        middle = envelope * jnp.exp(-0.5 * (NRAD - 1) ** 2 * (off * off))
        radial_ref[MID, at, :] = middle.astype(BF)
        grow = jnp.exp((NRAD - 1.0) * s)
        value = middle
        for n in range(MID, NRAD - 1):
            value = value * (grow * math.exp(-(2 * n + 1) / 2))
            radial_ref[n + 1, at, :] = value.astype(BF)
        shrink = jnp.exp((1.0 - NRAD) * s)
        value = middle
        for n in range(MID, 0, -1):
            value = value * (shrink * math.exp((2 * n - 1) / 2))
            radial_ref[n - 1, at, :] = value.astype(BF)
    weight_ref[...] = mode_weights(wave_ref, length, atoms * spaces)


def near_mix(left_ref, radial_ref, filt_ref, total_ref):
    for n in range(NRAD):
        part = dot_nn(left_ref[...], radial_ref[n]).reshape(total_ref.shape) * filt_ref[n][None]
        if n == 0:
            total_ref[...] = part
        else:
            total_ref[...] += part


def near_scratch(channels, atoms):
    return [
        pltpu.VMEM((NHARM * channels, 3 * atoms), BF),
        pltpu.VMEM((NHARM, channels, atoms), F32),
    ]


def coord_rows(coord_ref, t):
    tile = coord_ref[t]
    return (tile[0:1], tile[1:2], tile[2:3])


def near_grad_kernel(
    own_ref, first_ref, second_ref, radial_ref, coord_ref, filt_ref, grad_ref, left_ref, total_ref
):
    channels, atoms = grad_ref.shape
    for t, halo in enumerate((own_ref, first_ref, second_ref)):
        at = slice(t * atoms, (t + 1) * atoms)
        valid = coord_ref[t][3:4]
        grads = [
            halo[l * channels : (l + 1) * channels, :].astype(F32) * valid for l in range(NHARM)
        ]
        moved = list(grads)
        for (l, m), term in shift_terms(*coord_rows(coord_ref, t)).items():
            moved[m] = moved[m] + grads[l] * term
        for m in range(NHARM):
            left_ref[m * channels : (m + 1) * channels, at] = moved[m].astype(BF)
    near_mix(left_ref, radial_ref, filt_ref, total_ref)
    harm = harmonic_rows(*coord_rows(coord_ref, 0))
    grad = total_ref[0]
    for m in range(1, NHARM):
        grad = grad + total_ref[m] * harm[m]
    grad_ref[...] = grad


def fill_terms(data, cos, sin, terms_ref, at):
    channels = data.shape[0]
    terms_ref[0:channels, at] = data.astype(BF)
    for k in range(KLONG):
        lo = (1 + 2 * k) * channels
        terms_ref[lo : lo + channels, at] = (data * cos[k : k + 1]).astype(BF)
        terms_ref[lo + channels : lo + 2 * channels, at] = (data * sin[k : k + 1]).astype(BF)


def far_part(weight_ref, fill, step, pairs, channels, terms_ref, modes_ref, longs_ref):
    group_atoms = terms_ref.shape[1]
    group = min(pairs, pairs * group_atoms // modes_ref.shape[1])
    atoms = modes_ref.shape[1] // (2 * pairs)
    sums = None
    for base in range(0, pairs, group):
        lax.fori_loop(0, group // step, fill, base)
        at = slice(base * 2 * atoms, base * 2 * atoms + group_atoms)
        part = dot_nt(terms_ref[...], modes_ref[:, at])
        sums = part if sums is None else sums + part
    rows_re, rows_im = [], []
    for k in range(KLONG + 1):
        w = weight_ref[k : k + 1, :]
        if k == 0:
            real = sums[0:channels]
            cos, sin = real[:, :KMODE], real[:, KMODE:]
        else:
            lo = (2 * k - 1) * channels
            real, imag = sums[lo : lo + channels], sums[lo + channels : lo + 2 * channels]
            cos = real[:, :KMODE] - imag[:, KMODE:]
            sin = real[:, KMODE:] + imag[:, :KMODE]
        cos, sin = cos * w, sin * w
        rows_re.append(jnp.concatenate([cos, sin], 1))
        if k > 0:
            rows_im.append(jnp.concatenate([sin, -cos], 1))
    waves = jnp.concatenate(rows_re + rows_im, 0).astype(BF)
    back = dot_nn(waves, modes_ref[:, 0:atoms])
    cos, sin = longs_ref[0:8, 0:atoms], longs_ref[8:16, 0:atoms]
    far = back[0:channels]
    for k in range(KLONG):
        lo = (1 + k) * channels
        far = far + back[lo : lo + channels] * cos[k : k + 1]
        lo = (1 + KLONG + k) * channels
        far = far + back[lo : lo + channels] * sin[k : k + 1]
    return far


def far_scratch(channels, atoms, spaces):
    return [pltpu.VMEM(((2 * KLONG + 1) * channels, min(spaces, 8) * atoms), BF)]


def scaled_kernel(
    length,
    held_ref,
    near_ref,
    weight_ref,
    gain_ref,
    order_ref,
    scaled_ref,
    modes_ref,
    longs_ref,
    terms_ref,
):
    channels, atoms = near_ref.shape
    unit = channels + 16

    def fill(p, base):
        for q in range(2):
            tail = held_ref[base + p, q * unit + channels : (q + 1) * unit, :]
            first, second, third = phase_rows(*unpack_pos(tail), length)
            at = pl.ds(pl.multiple_of((2 * (base + p) + q) * atoms, atoms), atoms)
            modes_ref[:, at] = mode_table(second, third)
            longs_ref[0:8, at] = first[0]
            longs_ref[8:16, at] = first[1]
            cot = held_ref[base + p, q * unit : q * unit + channels, :].astype(F32)
            at = pl.ds(pl.multiple_of((2 * p + q) * atoms, atoms), atoms)
            fill_terms(cot * tail[10:11].astype(F32), *first, terms_ref, at)
        return base

    far = far_part(
        weight_ref, fill, 1, held_ref.shape[0], channels, terms_ref, modes_ref, longs_ref
    )
    scaled_ref[...] = ((near_ref[...] + far) * gain_ref[...]).astype(BF)


def near_messages_kernel(
    source_ref,
    first_ref,
    second_ref,
    radial_ref,
    coord_ref,
    filt_ref,
    scalar_ref,
    rest_ref,
    left_ref,
    total_ref,
):
    channels, atoms = source_ref.shape
    for t, ref in enumerate((source_ref, first_ref, second_ref)):
        at = slice(t * atoms, (t + 1) * atoms)
        left_ref[0:channels, at] = ref[...]
        source = ref[...].astype(F32)
        harm = harmonic_rows(*coord_rows(coord_ref, t))
        for m in range(1, NHARM):
            left_ref[m * channels : (m + 1) * channels, at] = (source * harm[m]).astype(BF)
    near_mix(left_ref, radial_ref, filt_ref, total_ref)
    valid = coord_ref[0][3:4]
    sums = [total_ref[m] for m in range(NHARM)]
    near = list(sums)
    for (l, m), term in shift_terms(*coord_rows(coord_ref, 0)).items():
        near[l] = near[l] + sums[m] * term
    scalar_ref[...] = near[0] * valid
    for l in range(1, NHARM):
        rest_ref[l - 1] = (near[l] * valid).astype(BF)


def messages_kernel(
    held_ref,
    held_two_ref,
    scalar_ref,
    rest_ref,
    coord_ref,
    weight_ref,
    modes_ref,
    longs_ref,
    messages_ref,
    token_ref,
    terms_ref,
):
    channels, atoms = scalar_ref.shape
    pairs = 2 * held_ref.shape[0]

    def fill(index, base):
        for r, ref in enumerate((held_ref, held_two_ref)):
            for q in range(2):
                data = ref[base // 2 + index, q * channels : (q + 1) * channels, :]
                m = 4 * index + 2 * r + q
                at = pl.ds(pl.multiple_of((2 * base + m) * atoms, atoms), atoms)
                cos, sin = longs_ref[0:8, at], longs_ref[8:16, at]
                at = pl.ds(pl.multiple_of(m * atoms, atoms), atoms)
                fill_terms(data.astype(F32), cos, sin, terms_ref, at)
        return base

    far = far_part(weight_ref, fill, 2, pairs, channels, terms_ref, modes_ref, longs_ref)
    valid = coord_ref[0][3:4]
    messages_ref[0] = (scalar_ref[...] + far * valid).astype(BF)
    messages_ref[1:NHARM] = rest_ref[...]
    token_ref[...] = jnp.zeros_like(token_ref)


def final_kernel(
    lane_ref, w_ref, own_ref, first_ref, other_ref, token_ref, out_ref, all_ref
):
    channels = out_ref.shape[0]
    lane = lane_ref[0]
    pieces = [own_ref[...], first_ref[...]]
    if other_ref is not None:
        pieces += [other_ref[m * channels : (m + 1) * channels, :] for m in range(2)]
    for m, piece in enumerate(pieces):
        at = pl.multiple_of((lane ^ m) * channels, channels)
        all_ref[pl.ds(at, channels), :] = piece
    first = pl.multiple_of(lane * channels, channels)
    out_ref[...] = dot_nn(w_ref[pl.ds(first, channels), :], all_ref[...])


def two_chan(kernel, place):
    def without(*refs):
        kernel(*refs[:place], None, *refs[place:])

    return without


def cost(micros):
    return pl.CostEstimate(
        flops=int(micros * 1e9), bytes_accessed=int(micros * 3e6), transcendentals=0
    )


def swapped(block, axis, bit):
    return lax.ppermute(block, axis, [(i, i ^ bit) for i in range(lax.axis_size(axis))])


def chan_pieces(raw, kept):
    first = swapped(raw, "chan", 1)
    if lax.axis_size("chan") == 2:
        return [kept, first]
    return [kept, first, swapped(jnp.concatenate([kept, first], 0), "chan", 2)]


def on_device(
    features,
    positions,
    species,
    block_count,
    pair_home,
    pair_reach,
    pair_count,
    wave_ints,
    species_gain,
    w_in,
    w_rad,
    cotangent,
):
    channels, atoms = features.shape
    spaces = lax.axis_size("space")
    chans = lax.axis_size("chan")
    length = SLICE_WIDTH * (atoms // BLOCK) * spaces
    place = lax.axis_index("space").astype(jnp.int32).reshape(1)
    lane = lax.axis_index("chan").astype(jnp.int32).reshape(1)
    rows = NHARM * channels + 16
    species = species.reshape(1, atoms)
    shape = jax.ShapeDtypeStruct

    def call(kernel, out_shape, smem, vmem, scratch, name, micros):
        return pl.pallas_call(
            kernel,
            out_shape=out_shape,
            in_specs=[SMEM] * len(smem) + [VMEM] * len(vmem),
            out_specs=jax.tree.map(lambda _: VMEM, out_shape),
            scratch_shapes=scratch,
            compiler_params=pltpu.CompilerParams(vmem_limit_bytes=32 * 1024 * 1024),
            cost_estimate=cost(micros),
            name=name,
        )(*smem, *vmem)

    def in_hbm(x):
        return pltpu.with_memory_space_constraint(x, pltpu.HBM)

    own, gain, feats_copy, w_copy = pl.pallas_call(
        prep_kernel,
        out_shape=(
            shape((rows, atoms), BF),
            shape((channels, atoms), F32),
            shape(features.shape, BF),
            shape(w_in.shape, BF),
        ),
        in_specs=[SMEM] + [pl.BlockSpec(memory_space=pltpu.HBM)] * 9,
        out_specs=(VMEM,) * 4,
        scratch_shapes=[
            pltpu.SMEM(block_count.shape, jnp.int32),
            pltpu.SMEM(pair_home.shape, jnp.int32),
            pltpu.SMEM(pair_reach.shape, jnp.int32),
            pltpu.VMEM(positions.shape, F32),
            pltpu.VMEM(species.shape, jnp.int32),
            pltpu.VMEM(species_gain.shape, F32),
            pltpu.SemaphoreType.DMA((9,)),
        ],
        compiler_params=pltpu.CompilerParams(vmem_limit_bytes=8 * 1024 * 1024),
        cost_estimate=cost(1),
        name="prep",
    )(
        pair_count,
        *[
            in_hbm(x)
            for x in (
                block_count,
                pair_home,
                pair_reach,
                positions,
                cotangent.reshape(NHARM * channels, atoms),
                species,
                species_gain,
                features,
                w_in,
            )
        ]
    )
    pieces = chan_pieces(features, feats_copy)
    first = swapped(own, "space", 1)
    other = [i - 1 if i % 2 == 0 else i + 1 for i in range(spaces)]
    second = lax.ppermute(own, "space", [(i, other[i] % spaces) for i in range(spaces)])
    source = call(
        source_kernel if chans > 2 else two_chan(source_kernel, 3),
        shape((channels, atoms), BF),
        (lane,),
        (*pieces, w_copy, gain),
        [pltpu.VMEM((w_in.shape[0], atoms), BF), pltpu.VMEM((w_in.shape[1], atoms), F32)],
        "source",
        1,
    )
    source_first = swapped(source, "space", 1)
    source_second = lax.ppermute(source, "space", [(i, other[i] % spaces) for i in range(spaces)])
    cut = NHARM * channels
    unit = 2 * (channels + 16)
    block = jnp.concatenate([own[:channels], own[cut:], first[:channels], first[cut:]], 0)
    held = jnp.concatenate([block[None], swapped(block, "space", 2)[None]], 0)
    sources = jnp.concatenate([source, source_first], 0)[None]
    bit = 4
    while bit < spaces:
        flat = jnp.concatenate(
            [held.reshape(-1, atoms), sources.reshape(-1, atoms)], 0
        )
        other_flat = swapped(flat, "space", bit)
        split = held.shape[0] * unit
        held = jnp.concatenate([held, other_flat[:split].reshape(held.shape)], 0)
        sources = jnp.concatenate([sources, other_flat[split:].reshape(sources.shape)], 0)
        bit *= 2
    sources_two = swapped(sources, "space", 2)
    radial, coord, filt, weight = call(
        functools.partial(radial_kernel, spaces),
        (
            shape((NRAD, 3 * atoms, atoms), BF),
            shape((3, 8, atoms), F32),
            shape((NRAD, channels, atoms), F32),
            shape((16, KMODE), F32),
        ),
        (place,),
        (own, first, second, wave_ints, w_rad),
        [pltpu.VMEM((3 * atoms, 8), F32), pltpu.VMEM((16, atoms), F32)],
        "radial",
        3,
    )
    near_grad = call(
        near_grad_kernel,
        shape((channels, atoms), F32),
        (),
        (own, first, second, radial, coord, filt),
        near_scratch(channels, atoms),
        "near_grad",
        3,
    )
    scalar, rest = call(
        near_messages_kernel,
        (shape((channels, atoms), F32), shape((NHARM - 1, channels, atoms), BF)),
        (),
        (source, source_first, source_second, radial, coord, filt),
        near_scratch(channels, atoms),
        "near_messages",
        3,
    )
    scaled, modes, longs = call(
        functools.partial(scaled_kernel, length),
        (
            shape((channels, atoms), BF),
            shape((2 * KMODE, spaces * atoms), BF),
            shape((16, spaces * atoms), F32),
        ),
        (),
        (held, near_grad, weight, gain, scalar),
        far_scratch(channels, atoms, spaces),
        "scaled",
        2,
    )
    scaled_pieces = chan_pieces(scaled, scaled)
    messages, token = call(
        messages_kernel,
        (shape((NHARM, channels, atoms), BF), shape((8, 128), F32)),
        (),
        (sources, sources_two, scalar, rest, coord, weight, modes, longs),
        far_scratch(channels, atoms, spaces),
        "messages",
        2,
    )
    grad_features = call(
        final_kernel if chans > 2 else two_chan(final_kernel, 4),
        shape((channels, atoms), F32),
        (lane,),
        (w_copy, *scaled_pieces, token),
        [pltpu.VMEM((chans * channels, atoms), BF)],
        "final",
        1,
    )
    return (messages, grad_features)


def mode_weights(wave_ref, length, total):
    k = wave_ref[...]
    count = k.shape[1]
    k = jnp.where(k[0:1] < 0, -k, k)
    k1, k2, k3 = k[0:1], k[1:2], k[2:3]
    code = jnp.where(k3 == 4, 76 + k2, (k2 + 4) * 8 + k3 + 4)
    rows = lax.broadcasted_iota(jnp.int32, (KMODE, count), 0)
    hot = (rows == code).astype(F32).astype(BF)
    longs = lax.broadcasted_iota(jnp.int32, (16, count), 0)
    hot1 = (longs == k1).astype(F32).astype(BF)
    mult = dot_nt(hot1, hot)
    lane = lax.broadcasted_iota(jnp.int32, (16, KMODE), 1)
    row = lax.broadcasted_iota(jnp.int32, (16, KMODE), 0)
    g2 = jnp.where(lane < 72, lane // 8 - 4, lane - 76).astype(F32)
    g3 = jnp.where(lane < 72, lane % 8 - 4, 4).astype(F32)
    f1 = row.astype(F32) * (2.0 * math.pi / length)
    f2 = g2 * (2.0 * math.pi / SIDE_WIDTH)
    f3 = g3 * (2.0 * math.pi / GAP_HEIGHT)
    ksq = f1 * f1 + f2 * f2 + f3 * f3
    value = jnp.exp(-0.5 * ksq) / (ksq + SCREEN * SCREEN) * (1.0 / math.sqrt(count * total))
    return jnp.where(mult > 0.0, mult * value, 0.0)


def phase_rows(x, y, z, length):
    atoms = x.shape[1]
    step = lax.broadcasted_iota(jnp.int32, (8, atoms), 0).astype(F32)
    first = sincos_turns((step + 1.0) * (x * (1.0 / length)))
    second = sincos_turns((step - 4.0) * (y * (1.0 / SIDE_WIDTH)))
    third = sincos_turns((step - 4.0) * (z * (1.0 / GAP_HEIGHT)))
    return first, second, third


def mode_table(second, third):
    c2, s2 = second
    c3, s3 = third
    atoms = c2.shape[1]
    cos, sin = [], []
    for k2 in range(9):
        a = c2[k2 : k2 + 1] if k2 < 8 else c2[0:1]
        b = s2[k2 : k2 + 1] if k2 < 8 else -s2[0:1]
        cos.append(a * c3 - b * s3)
        sin.append(a * s3 + b * c3)
    a, b = c3[0:1], -s3[0:1]
    cos.append(c2 * a - s2 * b)
    sin.append(c2 * b + s2 * a)
    one = lax.broadcasted_iota(jnp.int32, (8, atoms), 0) == 0
    cos.append(jnp.where(one, c2[0:1] * a + s2[0:1] * b, 0.0))
    sin.append(jnp.where(one, c2[0:1] * b - s2[0:1] * a, 0.0))
    pad = jnp.zeros((KMODE - 88, atoms), F32)
    return jnp.concatenate(cos + [pad] + sin + [pad], 0).astype(BF)


def unpack_pos(tail):
    t = tail.astype(F32)
    pos = (t[0:3] + t[3:6]) + t[6:9]
    return pos[0:1], pos[1:2], pos[2:3]


def solution(mesh):
    return jax.shard_map(
        on_device,
        mesh=mesh,
        in_specs=(
            P("chan", "space"),
            P(None, "space"),
            P("space"),
            P("space"),
            P("space"),
            P("space"),
            P("space"),
            P(),
            P(None, "chan"),
            P(),
            P(None, "chan"),
            P(None, "chan", "space"),
        ),
        out_specs=(P(None, "chan", "space"), P("chan", "space")),
        check_vma=False,
    )
```

time: 526 us -> 38.7 us (0.07)
  the two profiles are of different devices: /device:TPU:17 before, /device:TPU:0 now
where the time goes in v2:
time: 38.7 us; the launch traced here: 38.5 us
  starting transfers between devices  15.1 us (39%)
  Pallas kernels  12.5 us (32%)
  waiting for transfers between devices  9.39 us (24%)
  between operations  1.45 us (4%)
    pallas_call x7, Pallas kernels, call(): pl.pallas_call(kernel, out_shape=out_shape, in_specs=[SMEM] * len(smem) +...  11.4 us
    ppermute x9, starting transfers between devices, swapped(): lax.ppermute(block, axis, [(i, i ^ bit) for i in range(lax.axis_size(axis...  10.4 us
    ppermute x9, waiting for transfers between devices, swapped(): lax.ppermute(block, axis, [(i, i ^ bit) for i in range(lax.axis_size(axis...  7.81 us
    ppermute x1, starting transfers between devices, on_device(): lax.ppermute(own, 'space', [(i, other[i] % spaces) for i in range(spaces)])  3.57 us
    ppermute x1, waiting for transfers between devices, on_device(): lax.ppermute(own, 'space', [(i, other[i] % spaces) for i in range(spaces)])  1.57 us
    ppermute x1, starting transfers between devices, on_device(): lax.ppermute(source, 'space', [(i, other[i] % spaces) for i in range(spac...  1.15 us
    pallas_call x1, Pallas kernels, on_device(): pl.pallas_call(prep_kernel, out_shape=(shape((rows, atoms), BF), shape((c...  1.04 us
  transfers between devices with their start and end apart: 11, of which 6 were waited for; matrix products, arithmetic and copies ran while one was open for 0% of the time, Pallas kernels for 25%

profile of v2, /device:TPU:0, one launch (start us, length us, event | category | flops | bytes accessed | tf_op | source)
XLA Modules:
  0.0 38.5 jit_solution(9213666499378621475)
XLA Ops:
  0.6 0.0 copy-start
  0.6 0.0 copy-start.1
  0.7 0.5 %collective-permute-start = (bf16[32,256]{1,0:T(8,128)(2,1)}, bf16[32,256]{1,0:T(8,128)(2,1)S(1)}, u32[]{:S(2)}, u32[]{:S(2)}) collective-permute-start(bf16[32,256]{1,0:T(8,128)(2,1)} %feats_hbm.1), channel_id=1, source_target_pairs={{0,1},{1,0},{2,3},{3,2},{4,5},{5,4},{6,7},{7,6},{8,9},{9,8},{10,11... | collective-permute-start | bytes 49160 | tf_op jit(solution)/shard_map/ppermute | solution.py:525
  1.8 1.0 %prep.1 = (bf16[304,256]{1,0:T(8,128)(2,1)S(1)}, f32[32,256]{1,0:T(8,128)S(1)}, bf16[32,256]{1,0:T(8,128)(2,1)S(1)}, bf16[128,128]{1,0:T(8,128)(2,1)S(1)}) custom-call(s32[1]{0:T(128)S(6)} %copy.14.live_ref, s32[4]{0:T(128)} %count_hbm.1, s32[16]{0:T(128)} %home_hbm.1, s32[16]{0:T(128)} %reach_hbm.1, f32[3,256]{1,0:T(4,128)} %pos_hbm.1, ...), custom_call_target="tpu_custom_call" | custom-call | flops 1000000000 | bytes 3000000 | tf_op jit(solution)/shard_map/prep/pallas_call | solution.py:574
  2.9 0.0 collective-permute-done.first_ref
  2.9 2.6 %collective-permute-start.1 = (bf16[64,256]{1,0:T(8,128)(2,1)S(1)}, bf16[64,256]{1,0:T(8,128)(2,1)S(1)}, u32[]{:S(2)}, u32[]{:S(2)}) collective-permute-start(bf16[64,256]{1,0:T(8,128)(2,1)S(1)} %pad_maximum_fusion.5), channel_id=1, source_target_pairs={{0,2},{1,3},{2,0},{3,1},{4,6},{5,7},{6,4},{7,5},{8,10},{9,11},{10,... | collective-permute-start | bytes 98312 | tf_op jit(solution)/shard_map/ppermute | solution.py:525
  5.5 1.5 %collective-permute-start.3 = (bf16[304,256]{1,0:T(8,128)(2,1)S(1)}, bf16[304,256]{1,0:T(8,128)(2,1)S(1)}, u32[]{:S(2)}, u32[]{:S(2)}) collective-permute-start(bf16[304,256]{1,0:T(8,128)(2,1)S(1)} %get-tuple-element.20.own_ref), channel_id=1, source_target_pairs={{0,4},{4,0},{8,12},{12,8},{16,20},{20,16},{24,28},{28,24},{1,5},{5... | collective-permute-start | bytes 466952 | tf_op jit(solution)/shard_map/ppermute | solution.py:525
  7.0 0.6 %collective-permute-done.1.other_ref = bf16[64,256]{1,0:T(8,128)(2,1)S(1)} collective-permute-done((bf16[64,256]{1,0:T(8,128)(2,1)S(1)}, bf16[64,256]{1,0:T(8,128)(2,1)S(1)}, u32[]{:S(2)}, u32[]{:S(2)}) %collective-permute-start.1) | collective-permute-done | bytes 32800 | tf_op jit(solution)/shard_map/ppermute | solution.py:525
  7.5 0.2 source.1.source_ref
  7.7 1.9 %collective-permute-start.2 = (bf16[32,256]{1,0:T(8,128)(2,1)S(1)}, bf16[32,256]{1,0:T(8,128)(2,1)S(1)}, u32[]{:S(2)}, u32[]{:S(2)}) collective-permute-start(bf16[32,256]{1,0:T(8,128)(2,1)S(1)} %source.1.source_ref), channel_id=1, source_target_pairs={{0,4},{4,0},{8,12},{12,8},{16,20},{20,16},{24,28},{28,24},{1,5},{5... | collective-permute-start | bytes 49160 | tf_op jit(solution)/shard_map/ppermute | solution.py:525
  9.6 3.6 %collective-permute-start.8 = (bf16[304,256]{1,0:T(8,128)(2,1)S(1)}, bf16[304,256]{1,0:T(8,128)(2,1)S(1)}, u32[]{:S(2)}, u32[]{:S(2)}) collective-permute-start(bf16[304,256]{1,0:T(8,128)(2,1)S(1)} %get-tuple-element.20.own_ref), channel_id=1, source_target_pairs={{0,28},{4,8},{8,4},{12,16},{16,12},{20,24},{24,20},{28,0},{1,29},{... | collective-permute-start | bytes 466952 | tf_op jit(solution)/shard_map/ppermute | solution.py:616
  13.2 1.1 %collective-permute-start.7 = (bf16[32,256]{1,0:T(8,128)(2,1)S(1)}, bf16[32,256]{1,0:T(8,128)(2,1)S(1)}, u32[]{:S(2)}, u32[]{:S(2)}) collective-permute-start(bf16[32,256]{1,0:T(8,128)(2,1)S(1)} %source.1.source_ref), channel_id=1, source_target_pairs={{0,28},{4,8},{8,4},{12,16},{16,12},{20,24},{24,20},{28,0},{1,29},{... | collective-permute-start | bytes 49160 | tf_op jit(solution)/shard_map/ppermute | solution.py:627
  14.4 0.2 collective-permute-done.2.first_ref
  14.5 0.0 collective-permute-done.3.first_ref
  14.6 1.6 %collective-permute-start.4 = (bf16[96,256]{1,0:T(8,128)(2,1)S(1)}, bf16[96,256]{1,0:T(8,128)(2,1)S(1)}, u32[]{:S(2)}, u32[]{:S(2)}) collective-permute-start(bf16[96,256]{1,0:T(8,128)(2,1)S(1)} %get-tuple-element.33), channel_id=1, source_target_pairs={{0,8},{4,12},{8,0},{12,4},{16,24},{20,28},{24,16},{28,20},{1,9},{5... | collective-permute-start | bytes 147464 | tf_op jit(solution)/shard_map/ppermute | solution.py:525
  16.2 1.6 %collective-permute-done.8.second_ref = bf16[304,256]{1,0:T(8,128)(2,1)S(1)} collective-permute-done((bf16[304,256]{1,0:T(8,128)(2,1)S(1)}, bf16[304,256]{1,0:T(8,128)(2,1)S(1)}, u32[]{:S(2)}, u32[]{:S(2)}) %collective-permute-start.8) | collective-permute-done | bytes 155680 | tf_op jit(solution)/shard_map/ppermute | solution.py:616
  17.8 0.0 copy-done
  17.8 0.0 copy-done.1
  17.8 2.1 %radial.1 = (bf16[16,768,256]{2,1,0:T(8,128)(2,1)S(1)}, f32[3,8,256]{2,1,0:T(8,128)S(1)}, f32[16,32,256]{2,1,0:T(8,128)S(1)}, f32[16,128]{1,0:T(8,128)S(1)}) custom-call(s32[1]{0:T(128)} %bitcast.8.place_ref, bf16[304,256]{1,0:T(8,128)(2,1)S(1)} %get-tuple-element.20.own_ref, bf16[304,256]{1,0:T(8,128)(2,1)S(1)} %collective-permute-done.3.first_ref, ...), custom_call_target="tpu_custom_call" | custom-call | flops 3000000000 | bytes 9000000 | tf_op jit(solution)/shard_map/radial/pallas_call | solution.py:560
  19.9 2.1 %near_grad.1.near_ref = f32[32,256]{1,0:T(8,128)S(1)} custom-call(bf16[304,256]{1,0:T(8,128)(2,1)S(1)} %get-tuple-element.20.own_ref, bf16[304,256]{1,0:T(8,128)(2,1)S(1)} %collective-permute-done.3.first_ref, bf16[304,256]{1,0:T(8,128)(2,1)S(1)} %collective-permute-done.8.second_ref, bf16[16,768,256]{2,1,0:T(8,128)(2,1)S(1)} %get-tuple-element.21.radial_ref, ...), custom_call_target="tpu_custom_call" | custom-call | flops 3000000000 | bytes 9000000 | tf_op jit(solution)/shard_map/near_grad/pallas_call | solution.py:560
  22.0 0.0 collective-permute-done.4
  22.1 0.6 %collective-permute-start.5 = (bf16[256,256]{1,0:T(8,128)(2,1)S(1)}, bf16[256,256]{1,0:T(8,128)(2,1)S(1)}, u32[]{:S(2)}, u32[]{:S(2)}) collective-permute-start(bf16[256,256]{1,0:T(8,128)(2,1)S(1)} %pad_maximum_fusion.1), channel_id=1, source_target_pairs={{0,16},{4,20},{8,24},{12,28},{16,0},{20,4},{24,8},{28,12},{1,17},{... | collective-permute-start | bytes 393224 | tf_op jit(solution)/shard_map/ppermute | solution.py:525
  22.7 0.0 collective-permute-done.7.second_ref
  22.7 2.1 %near_messages.1 = (f32[32,256]{1,0:T(8,128)S(1)}, bf16[8,32,256]{2,1,0:T(8,128)(2,1)S(1)}) custom-call(bf16[32,256]{1,0:T(8,128)(2,1)S(1)} %source.1.source_ref, bf16[32,256]{1,0:T(8,128)(2,1)S(1)} %collective-permute-done.2.first_ref, bf16[32,256]{1,0:T(8,128)(2,1)S(1)} %collective-permute-done.7.second_ref, ...), custom_call_target="tpu_custom_call" | custom-call | flops 3000000000 | bytes 9000000 | tf_op jit(solution)/shard_map/near_messages/pallas_call | solution.py:560
  24.8 4.1 %collective-permute-done.5 = bf16[256,256]{1,0:T(8,128)(2,1)S(1)} collective-permute-done((bf16[256,256]{1,0:T(8,128)(2,1)S(1)}, bf16[256,256]{1,0:T(8,128)(2,1)S(1)}, u32[]{:S(2)}, u32[]{:S(2)}) %collective-permute-start.5) | collective-permute-done | bytes 131104 | tf_op jit(solution)/shard_map/ppermute | solution.py:525
  28.9 1.9 %scaled.1 = (bf16[32,256]{1,0:T(8,128)(2,1)S(1)}, bf16[256,2048]{1,0:T(8,128)(2,1)S(1)}, f32[16,2048]{1,0:T(8,128)S(1)}) custom-call(bf16[4,96,256]{2,1,0:T(8,128)(2,1)S(1)} %pad_maximum_fusion.held_ref, f32[32,256]{1,0:T(8,128)S(1)} %near_grad.1.near_ref, f32[16,128]{1,0:T(8,128)S(1)} %get-tuple-element.26.weight_ref, ...), custom_call_target="tpu_custom_call" | custom-call | flops 2000000000 | bytes 6000000 | tf_op jit(solution)/shard_map/scaled/pallas_call | solution.py:560
  30.9 0.1 collective-permute-start.9
  31.0 0.1 collective-permute-start.6
  31.1 1.1 %collective-permute-done.9.first_ref = bf16[32,256]{1,0:T(8,128)(2,1)S(1)} collective-permute-done((bf16[32,256]{1,0:T(8,128)(2,1)S(1)}, bf16[32,256]{1,0:T(8,128)(2,1)S(1)}, u32[]{:S(2)}, u32[]{:S(2)}) %collective-permute-start.9) | collective-permute-done | bytes 16416 | tf_op jit(solution)/shard_map/ppermute | solution.py:525
  32.1 1.5 %collective-permute-start.10 = (bf16[64,256]{1,0:T(8,128)(2,1)S(1)}, bf16[64,256]{1,0:T(8,128)(2,1)S(1)}, u32[]{:S(2)}, u32[]{:S(2)}) collective-permute-start(bf16[64,256]{1,0:T(8,128)(2,1)S(1)} %pad_maximum_fusion.6), channel_id=1, source_target_pairs={{0,2},{1,3},{2,0},{3,1},{4,6},{5,7},{6,4},{7,5},{8,10},{9,11},{10,... | collective-permute-start | bytes 98312 | tf_op jit(solution)/shard_map/ppermute | solution.py:525
  33.7 1.9 %collective-permute-done.6.held_two_ref = bf16[2,64,256]{2,1,0:T(8,128)(2,1)S(1)} collective-permute-done((bf16[2,64,256]{2,1,0:T(8,128)(2,1)S(1)}, bf16[2,64,256]{2,1,0:T(8,128)(2,1)S(1)}, u32[]{:S(2)}, u32[]{:S(2)}) %collective-permute-start.6) | collective-permute-done | bytes 65568 | tf_op jit(solution)/shard_map/ppermute | solution.py:525
  35.5 2.2 %messages.1 = (bf16[9,32,256]{2,1,0:T(8,128)(2,1)}, f32[8,128]{1,0:T(8,128)S(1)}) custom-call(bf16[2,64,256]{2,1,0:T(8,128)(2,1)S(1)} %pad_maximum_fusion.3.held_ref, bf16[2,64,256]{2,1,0:T(8,128)(2,1)S(1)} %collective-permute-done.6.held_two_ref, f32[32,256]{1,0:T(8,128)S(1)} %get-tuple-element.24.order_ref.scalar_ref, ...), custom_call_target="tpu_custom_call" | custom-call | flops 2000000000 | bytes 6000000 | tf_op jit(solution)/shard_map/messages/pallas_call | solution.py:560
  37.8 0.0 collective-permute-done.10.other_ref
  37.8 0.8 %final.1 = f32[32,256]{1,0:T(8,128)} custom-call(s32[1]{0:T(128)} %bitcast.lane_ref, bf16[128,128]{1,0:T(8,128)(2,1)S(1)} %get-tuple-element.18.w_ref, bf16[32,256]{1,0:T(8,128)(2,1)S(1)} %get-tuple-element.30.own_ref, bf16[32,256]{1,0:T(8,128)(2,1)S(1)} %collective-permute-done.9.first_ref, bf16[64,256]{1,0:T(8,128)(2,1)S(1)} %collective-permute-done.10.other_ref, ...), custom_call_target="tpu_custom_call" | custom-call | flops 1000000000 | bytes 3000000 | tf_op jit(solution)/shard_map/final/pallas_call | solution.py:560
  (14 shorter events, 0.1 us)
Async XLA Ops:
  0.6 17.2 %copy-start = (s32[3,1024]{1,0:T(4,128)S(1)}, s32[3,1024]{1,0:T(4,128)}, u32[]{:S(2)}) copy-start(s32[3,1024]{1,0:T(4,128)} %wave_ref.1) | copy-start | bytes 36868
  0.6 17.2 %copy-start.1 = (f32[16,32]{1,0:T(8,128)S(1)}, f32[16,32]{1,0:T(8,128)}, u32[]{:S(2)}) copy-start(f32[16,32]{1,0:T(8,128)} %w_rad_ref.1) | copy-start | bytes 6148
  0.7 2.2 %collective-permute-start = (bf16[32,256]{1,0:T(8,128)(2,1)}, bf16[32,256]{1,0:T(8,128)(2,1)S(1)}, u32[]{:S(2)}, u32[]{:S(2)}) collective-permute-start(bf16[32,256]{1,0:T(8,128)(2,1)} %feats_hbm.1), channel_id=1, source_target_pairs={{0,1},{1,0},{2,3},{3,2},{4,5},{5,4},{6,7},{7,6},{8,9},{9,8},{10,11... | collective-permute-start | bytes 49160 | tf_op jit(solution)/shard_map/ppermute | solution.py:525
  2.9 4.6 %collective-permute-start.1 = (bf16[64,256]{1,0:T(8,128)(2,1)S(1)}, bf16[64,256]{1,0:T(8,128)(2,1)S(1)}, u32[]{:S(2)}, u32[]{:S(2)}) collective-permute-start(bf16[64,256]{1,0:T(8,128)(2,1)S(1)} %pad_maximum_fusion.5), channel_id=1, source_target_pairs={{0,2},{1,3},{2,0},{3,1},{4,6},{5,7},{6,4},{7,5},{8,10},{9,11},{10,... | collective-permute-start | bytes 98312 | tf_op jit(solution)/shard_map/ppermute | solution.py:525
  5.5 9.1 %collective-permute-start.3 = (bf16[304,256]{1,0:T(8,128)(2,1)S(1)}, bf16[304,256]{1,0:T(8,128)(2,1)S(1)}, u32[]{:S(2)}, u32[]{:S(2)}) collective-permute-start(bf16[304,256]{1,0:T(8,128)(2,1)S(1)} %get-tuple-element.20.own_ref), channel_id=1, source_target_pairs={{0,4},{4,0},{8,12},{12,8},{16,20},{20,16},{24,28},{28,24},{1,5},{5... | collective-permute-start | bytes 466952 | tf_op jit(solution)/shard_map/ppermute | solution.py:525
  7.7 6.8 %collective-permute-start.2 = (bf16[32,256]{1,0:T(8,128)(2,1)S(1)}, bf16[32,256]{1,0:T(8,128)(2,1)S(1)}, u32[]{:S(2)}, u32[]{:S(2)}) collective-permute-start(bf16[32,256]{1,0:T(8,128)(2,1)S(1)} %source.1.source_ref), channel_id=1, source_target_pairs={{0,4},{4,0},{8,12},{12,8},{16,20},{20,16},{24,28},{28,24},{1,5},{5... | collective-permute-start | bytes 49160 | tf_op jit(solution)/shard_map/ppermute | solution.py:525
  9.6 8.2 %collective-permute-start.8 = (bf16[304,256]{1,0:T(8,128)(2,1)S(1)}, bf16[304,256]{1,0:T(8,128)(2,1)S(1)}, u32[]{:S(2)}, u32[]{:S(2)}) collective-permute-start(bf16[304,256]{1,0:T(8,128)(2,1)S(1)} %get-tuple-element.20.own_ref), channel_id=1, source_target_pairs={{0,28},{4,8},{8,4},{12,16},{16,12},{20,24},{24,20},{28,0},{1,29},{... | collective-permute-start | bytes 466952 | tf_op jit(solution)/shard_map/ppermute | solution.py:616
  13.2 9.5 %collective-permute-start.7 = (bf16[32,256]{1,0:T(8,128)(2,1)S(1)}, bf16[32,256]{1,0:T(8,128)(2,1)S(1)}, u32[]{:S(2)}, u32[]{:S(2)}) collective-permute-start(bf16[32,256]{1,0:T(8,128)(2,1)S(1)} %source.1.source_ref), channel_id=1, source_target_pairs={{0,28},{4,8},{8,4},{12,16},{16,12},{20,24},{24,20},{28,0},{1,29},{... | collective-permute-start | bytes 49160 | tf_op jit(solution)/shard_map/ppermute | solution.py:627
  14.6 7.4 %collective-permute-start.4 = (bf16[96,256]{1,0:T(8,128)(2,1)S(1)}, bf16[96,256]{1,0:T(8,128)(2,1)S(1)}, u32[]{:S(2)}, u32[]{:S(2)}) collective-permute-start(bf16[96,256]{1,0:T(8,128)(2,1)S(1)} %get-tuple-element.33), channel_id=1, source_target_pairs={{0,8},{4,12},{8,0},{12,4},{16,24},{20,28},{24,16},{28,20},{1,9},{5... | collective-permute-start | bytes 147464 | tf_op jit(solution)/shard_map/ppermute | solution.py:525
  22.1 6.8 %collective-permute-start.5 = (bf16[256,256]{1,0:T(8,128)(2,1)S(1)}, bf16[256,256]{1,0:T(8,128)(2,1)S(1)}, u32[]{:S(2)}, u32[]{:S(2)}) collective-permute-start(bf16[256,256]{1,0:T(8,128)(2,1)S(1)} %pad_maximum_fusion.1), channel_id=1, source_target_pairs={{0,16},{4,20},{8,24},{12,28},{16,0},{20,4},{24,8},{28,12},{1,17},{... | collective-permute-start | bytes 393224 | tf_op jit(solution)/shard_map/ppermute | solution.py:525
  30.9 1.2 %collective-permute-start.9 = (bf16[32,256]{1,0:T(8,128)(2,1)S(1)}, bf16[32,256]{1,0:T(8,128)(2,1)S(1)}, u32[]{:S(2)}, u32[]{:S(2)}) collective-permute-start(bf16[32,256]{1,0:T(8,128)(2,1)S(1)} %get-tuple-element.30.own_ref), channel_id=1, source_target_pairs={{0,1},{1,0},{2,3},{3,2},{4,5},{5,4},{6,7},{7,6},{8,9},{9,8},{10,11... | collective-permute-start | bytes 49160 | tf_op jit(solution)/shard_map/ppermute | solution.py:525
  31.0 4.5 %collective-permute-start.6 = (bf16[2,64,256]{2,1,0:T(8,128)(2,1)S(1)}, bf16[2,64,256]{2,1,0:T(8,128)(2,1)S(1)}, u32[]{:S(2)}, u32[]{:S(2)}) collective-permute-start(bf16[2,64,256]{2,1,0:T(8,128)(2,1)S(1)} %pad_maximum_fusion.3.held_ref), channel_id=1, source_target_pairs={{0,8},{4,12},{8,0},{12,4},{16,24},{20,28},{24,16},{28,20},{1,9},{5... | collective-permute-start | bytes 196616 | tf_op jit(solution)/shard_map/ppermute | solution.py:525
  32.1 5.6 %collective-permute-start.10 = (bf16[64,256]{1,0:T(8,128)(2,1)S(1)}, bf16[64,256]{1,0:T(8,128)(2,1)S(1)}, u32[]{:S(2)}, u32[]{:S(2)}) collective-permute-start(bf16[64,256]{1,0:T(8,128)(2,1)S(1)} %pad_maximum_fusion.6), channel_id=1, source_target_pairs={{0,2},{1,3},{2,0},{3,1},{4,6},{5,7},{6,4},{7,5},{8,10},{9,11},{10,... | collective-permute-start | bytes 98312 | tf_op jit(solution)/shard_map/ppermute | solution.py:525

commit v3 on v2

--- a/solution.py
+++ b/solution.py
@@ -30,6 +30,7 @@
 R5 = math.sqrt(5.0)
 R15 = math.sqrt(15.0)
 
+COST = dict(prep=1, source=1, radial=3, near_grad=3, near_messages=1.5, scaled=2, half=0.2, messages=2, final=1)
 VMEM = pl.BlockSpec(memory_space=pltpu.VMEM)
 SMEM = pl.BlockSpec(memory_space=pltpu.SMEM)
 
@@ -137,7 +138,7 @@
     gain_hbm,
     feats_hbm,
     w_hbm,
-    halo_ref,
+    head_ref,
     gain_ref,
     feats_ref,
     w_ref,
@@ -149,7 +150,7 @@
     species_gain_ref,
     sems,
 ):
-    rows, atoms = cot_hbm.shape
+    channels, atoms = feats_hbm.shape
     pairs = (
         (count_hbm, count_ref),
         (home_hbm, home_ref),
@@ -157,7 +158,7 @@
         (pos_hbm, pos_ref),
         (species_hbm, species_ref),
         (gain_hbm, species_gain_ref),
-        (cot_hbm, halo_ref.at[0:rows, :]),
+        (cot_hbm.at[0:channels, :], head_ref.at[0:channels, :]),
         (feats_hbm, feats_ref),
         (w_hbm, w_ref),
     )
@@ -172,31 +173,29 @@
         slot = home_ref[p] * REACH + reach_ref[p] - 1
         flags = jnp.where(jnp.logical_and(lane == slot, p < live_ref[0]), 1.0, flags)
     valid = valid_row(count_ref, atoms)
-    halo_ref[rows:, :] = tail_rows(pos_ref[...], flags, valid)
+    head_ref[channels:, :] = tail_rows(pos_ref[...], flags, valid)
     gain_ref[...] = gain_rows(species_ref, species_gain_ref) * valid
     for copy in copies[6:]:
         copy.wait()
 
 
-def source_kernel(
-    lane_ref, own_ref, first_ref, other_ref, w_ref, gain_ref, source_ref, all_ref, mix_ref
-):
-    channels, atoms = source_ref.shape
+def source_kernel(chans, lane_ref, *refs):
+    pieces, (w_ref, gain_ref, head_ref) = refs[:chans], refs[chans : chans + 3]
+    out_ref, all_ref, mix_ref = refs[-3:]
+    channels = gain_ref.shape[0]
     lane = lane_ref[0]
-    pieces = [own_ref[...], first_ref[...]]
-    if other_ref is not None:
-        pieces += [other_ref[m * channels : (m + 1) * channels, :] for m in range(2)]
+    out_ref[0 : channels + 16, :] = head_ref[...]
     for m, piece in enumerate(pieces):
         at = pl.multiple_of((lane ^ m) * channels, channels)
-        all_ref[pl.ds(at, channels), :] = piece
+        all_ref[pl.ds(at, channels), :] = piece[...]
     mix_ref[...] = lax.dot_general(
         w_ref[...], all_ref[...], (((0,), (0,)), ((), ())), preferred_element_type=F32
     )
     mixed = mix_ref[pl.ds(pl.multiple_of(lane * channels, channels), channels), :]
-    source_ref[...] = (mixed * gain_ref[...]).astype(BF)
-
-
-def geometry(place, spaces, halos, cols_ref, live_ref, coord_ref):
+    out_ref[channels + 16 :, :] = (mixed * gain_ref[...]).astype(BF)
+
+
+def geometry(place, spaces, halos, channels, cols_ref, live_ref, coord_ref):
     atoms = halos[0].shape[1]
     blocks = atoms // BLOCK
     length = SLICE_WIDTH * blocks * spaces
@@ -205,7 +204,10 @@
     centre = (place.astype(F32) + 0.5) * (SLICE_WIDTH * blocks)
     lane = lax.broadcasted_iota(jnp.int32, (1, atoms), 1)
     home = lane // BLOCK
-    tails = [h[h.shape[0] - 16 :, :] for h in halos]
+    tails = []
+    for h in halos:
+        cut = h.shape[0] - channels
+        tails.append(h[cut - 16 : cut, :])
 
     def flag_row(tail, h, r):
         index = h * REACH + r - 1
@@ -265,7 +267,9 @@
     atoms = own_ref.shape[1]
     length = SLICE_WIDTH * (atoms // BLOCK) * spaces
     halos = (own_ref, first_ref, second_ref)
-    xa, ya, za = geometry(place_ref[0], spaces, halos, cols_ref, live_ref, coord_ref)
+    xa, ya, za = geometry(
+        place_ref[0], spaces, halos, w_rad_ref.shape[1], cols_ref, live_ref, coord_ref
+    )
     w_cols = w_rad_ref[...].T
     for n in range(NRAD):
         filt_ref[n] = jnp.broadcast_to(w_cols[:, n : n + 1], filt_ref.shape[1:])
@@ -353,16 +357,19 @@
         terms_ref[lo + channels : lo + 2 * channels, at] = (data * sin[k : k + 1]).astype(BF)
 
 
-def far_part(weight_ref, fill, step, pairs, channels, terms_ref, modes_ref, longs_ref):
-    group_atoms = terms_ref.shape[1]
-    group = min(pairs, pairs * group_atoms // modes_ref.shape[1])
-    atoms = modes_ref.shape[1] // (2 * pairs)
+def gathered_sums(fill, pairs, terms_ref, modes_ref):
+    span = terms_ref.shape[1]
+    group = pairs * span // modes_ref.shape[1]
     sums = None
     for base in range(0, pairs, group):
-        lax.fori_loop(0, group // step, fill, base)
-        at = slice(base * 2 * atoms, base * 2 * atoms + group_atoms)
+        lax.fori_loop(0, group, fill, base)
+        at = slice(base // group * span, (base // group + 1) * span)
         part = dot_nt(terms_ref[...], modes_ref[:, at])
         sums = part if sums is None else sums + part
+    return sums
+
+
+def far_field(sums, weight_ref, own_ref, own_longs_ref, channels):
     rows_re, rows_im = [], []
     for k in range(KLONG + 1):
         w = weight_ref[k : k + 1, :]
@@ -379,8 +386,8 @@
         if k > 0:
             rows_im.append(jnp.concatenate([sin, -cos], 1))
     waves = jnp.concatenate(rows_re + rows_im, 0).astype(BF)
-    back = dot_nn(waves, modes_ref[:, 0:atoms])
-    cos, sin = longs_ref[0:8, 0:atoms], longs_ref[8:16, 0:atoms]
+    back = dot_nn(waves, own_ref[...])
+    cos, sin = own_longs_ref[0:8, :], own_longs_ref[8:16, :]
     far = back[0:channels]
     for k in range(KLONG):
         lo = (1 + k) * channels
@@ -391,45 +398,92 @@
 
 
 def far_scratch(channels, atoms, spaces):
-    return [pltpu.VMEM(((2 * KLONG + 1) * channels, min(spaces, 8) * atoms), BF)]
+    return [pltpu.VMEM(((2 * KLONG + 1) * channels, min(spaces // 2, 8) * atoms), BF)]
+
+
+def cot_filler(length, held_ref, channels, modes_ref, longs_ref, terms_ref):
+    unit = 2 * channels + 16
+    atoms = held_ref.shape[2]
+
+    def fill(p, base):
+        for q in range(2):
+            lo = q * unit
+            tail = held_ref[base + p, lo + channels : lo + channels + 16, :]
+            first, second, third = phase_rows(*unpack_pos(tail), length)
+            at = pl.ds(pl.multiple_of((2 * (base + p) + q) * atoms, atoms), atoms)
+            modes_ref[:, at] = mode_table(second, third)
+            longs_ref[0:8, at] = first[0]
+            longs_ref[8:16, at] = first[1]
+            cot = held_ref[base + p, lo : lo + channels, :].astype(F32)
+            at = pl.ds(pl.multiple_of((2 * p + q) * atoms, atoms), atoms)
+            fill_terms(cot * tail[10:11].astype(F32), *first, terms_ref, at)
+        return base
+
+    return fill
+
+
+def source_filler(held_ref, channels, longs_ref, terms_ref):
+    unit = 2 * channels + 16
+    atoms = held_ref.shape[2]
+
+    def fill(p, base):
+        for q in range(2):
+            lo = q * unit + channels + 16
+            data = held_ref[base + p, lo : lo + channels, :].astype(F32)
+            at = pl.ds(pl.multiple_of((2 * (base + p) + q) * atoms, atoms), atoms)
+            cos, sin = longs_ref[0:8, at], longs_ref[8:16, at]
+            at = pl.ds(pl.multiple_of((2 * p + q) * atoms, atoms), atoms)
+            fill_terms(data, cos, sin, terms_ref, at)
+        return base
+
+    return fill
+
+
+def half_kernel(
+    length,
+    held_ref,
+    cot_sums_ref,
+    source_sums_ref,
+    own_ref,
+    own_longs_ref,
+    terms_ref,
+    modes_ref,
+    longs_ref,
+):
+    pairs, rows, atoms = held_ref.shape
+    channels = (rows // 2 - 16) // 2
+    fill = cot_filler(length, held_ref, channels, modes_ref, longs_ref, terms_ref)
+    cot_sums_ref[...] = gathered_sums(fill, pairs, terms_ref, modes_ref)
+    fill = source_filler(held_ref, channels, longs_ref, terms_ref)
+    source_sums_ref[...] = gathered_sums(fill, pairs, terms_ref, modes_ref)
+    own_ref[...] = modes_ref[:, 0:atoms]
+    own_longs_ref[...] = longs_ref[:, 0:atoms]
 
 
 def scaled_kernel(
     length,
-    held_ref,
+    rest_ref,
     near_ref,
     weight_ref,
     gain_ref,
+    sums_ref,
+    own_ref,
+    own_longs_ref,
     order_ref,
     scaled_ref,
     modes_ref,
     longs_ref,
     terms_ref,
 ):
-    channels, atoms = near_ref.shape
-    unit = channels + 16
-
-    def fill(p, base):
-        for q in range(2):
-            tail = held_ref[base + p, q * unit + channels : (q + 1) * unit, :]
-            first, second, third = phase_rows(*unpack_pos(tail), length)
-            at = pl.ds(pl.multiple_of((2 * (base + p) + q) * atoms, atoms), atoms)
-            modes_ref[:, at] = mode_table(second, third)
-            longs_ref[0:8, at] = first[0]
-            longs_ref[8:16, at] = first[1]
-            cot = held_ref[base + p, q * unit : q * unit + channels, :].astype(F32)
-            at = pl.ds(pl.multiple_of((2 * p + q) * atoms, atoms), atoms)
-            fill_terms(cot * tail[10:11].astype(F32), *first, terms_ref, at)
-        return base
-
-    far = far_part(
-        weight_ref, fill, 1, held_ref.shape[0], channels, terms_ref, modes_ref, longs_ref
-    )
+    channels = near_ref.shape[0]
+    fill = cot_filler(length, rest_ref, channels, modes_ref, longs_ref, terms_ref)
+    sums = gathered_sums(fill, rest_ref.shape[0], terms_ref, modes_ref) + sums_ref[...]
+    far = far_field(sums, weight_ref, own_ref, own_longs_ref, channels)
     scaled_ref[...] = ((near_ref[...] + far) * gain_ref[...]).astype(BF)
 
 
 def near_messages_kernel(
-    source_ref,
+    own_ref,
     first_ref,
     second_ref,
     radial_ref,
@@ -440,11 +494,12 @@
     left_ref,
     total_ref,
 ):
-    channels, atoms = source_ref.shape
-    for t, ref in enumerate((source_ref, first_ref, second_ref)):
+    channels, atoms = scalar_ref.shape
+    for t, ref in enumerate((own_ref, first_ref, second_ref)):
+        lo = ref.shape[0] - channels
         at = slice(t * atoms, (t + 1) * atoms)
-        left_ref[0:channels, at] = ref[...]
-        source = ref[...].astype(F32)
+        left_ref[0:channels, at] = ref[lo : lo + channels, :]
+        source = ref[lo : lo + channels, :].astype(F32)
         harm = harmonic_rows(*coord_rows(coord_ref, t))
         for m in range(1, NHARM):
             left_ref[m * channels : (m + 1) * channels, at] = (source * harm[m]).astype(BF)
@@ -461,32 +516,23 @@
 
 def messages_kernel(
     held_ref,
-    held_two_ref,
     scalar_ref,
     rest_ref,
     coord_ref,
     weight_ref,
+    sums_ref,
+    own_ref,
+    own_longs_ref,
     modes_ref,
     longs_ref,
     messages_ref,
     token_ref,
     terms_ref,
 ):
-    channels, atoms = scalar_ref.shape
-    pairs = 2 * held_ref.shape[0]
-
-    def fill(index, base):
-        for r, ref in enumerate((held_ref, held_two_ref)):
-            for q in range(2):
-                data = ref[base // 2 + index, q * channels : (q + 1) * channels, :]
-                m = 4 * index + 2 * r + q
-                at = pl.ds(pl.multiple_of((2 * base + m) * atoms, atoms), atoms)
-                cos, sin = longs_ref[0:8, at], longs_ref[8:16, at]
-                at = pl.ds(pl.multiple_of(m * atoms, atoms), atoms)
-                fill_terms(data.astype(F32), cos, sin, terms_ref, at)
-        return base
-
-    far = far_part(weight_ref, fill, 2, pairs, channels, terms_ref, modes_ref, longs_ref)
+    channels = scalar_ref.shape[0]
+    fill = source_filler(held_ref, channels, longs_ref, terms_ref)
+    sums = gathered_sums(fill, held_ref.shape[0], terms_ref, modes_ref) + sums_ref[...]
+    far = far_field(sums, weight_ref, own_ref, own_longs_ref, channels)
     valid = coord_ref[0][3:4]
     messages_ref[0] = (scalar_ref[...] + far * valid).astype(BF)
     messages_ref[1:NHARM] = rest_ref[...]
@@ -552,7 +598,6 @@
     length = SLICE_WIDTH * (atoms // BLOCK) * spaces
     place = lax.axis_index("space").astype(jnp.int32).reshape(1)
     lane = lax.axis_index("chan").astype(jnp.int32).reshape(1)
-    rows = NHARM * channels + 16
     species = species.reshape(1, atoms)
     shape = jax.ShapeDtypeStruct
 
@@ -571,10 +616,11 @@
     def in_hbm(x):
         return pltpu.with_memory_space_constraint(x, pltpu.HBM)
 
-    own, gain, feats_copy, w_copy = pl.pallas_call(
+    cots = cotangent.reshape(NHARM * channels, atoms)
+    head, gain, feats_copy, w_copy = pl.pallas_call(
         prep_kernel,
         out_shape=(
-            shape((rows, atoms), BF),
+            shape((channels + 16, atoms), BF),
             shape((channels, atoms), F32),
             shape(features.shape, BF),
             shape(w_in.shape, BF),
@@ -591,7 +637,7 @@
             pltpu.SemaphoreType.DMA((9,)),
         ],
         compiler_params=pltpu.CompilerParams(vmem_limit_bytes=8 * 1024 * 1024),
-        cost_estimate=cost(1),
+        cost_estimate=cost(COST["prep"]),
         name="prep",
     )(
         pair_count,
@@ -602,7 +648,7 @@
                 pair_home,
                 pair_reach,
                 positions,
-                cotangent.reshape(NHARM * channels, atoms),
+                cots,
                 species,
                 species_gain,
                 features,
@@ -610,37 +656,29 @@
             )
         ]
     )
-    pieces = chan_pieces(features, feats_copy)
-    first = swapped(own, "space", 1)
+    pieces = [feats_copy] + [swapped(features, "chan", m) for m in range(1, chans)]
     other = [i - 1 if i % 2 == 0 else i + 1 for i in range(spaces)]
-    second = lax.ppermute(own, "space", [(i, other[i] % spaces) for i in range(spaces)])
-    source = call(
-        source_kernel if chans > 2 else two_chan(source_kernel, 3),
-        shape((channels, atoms), BF),
+    route = [(i, other[i] % spaces) for i in range(spaces)]
+    second = lax.ppermute(cots, "space", route)
+    first = swapped(cots, "space", 1)
+    unit = call(
+        functools.partial(source_kernel, chans),
+        shape((2 * channels + 16, atoms), BF),
         (lane,),
-        (*pieces, w_copy, gain),
+        (*pieces, w_copy, gain, head, first, second),
         [pltpu.VMEM((w_in.shape[0], atoms), BF), pltpu.VMEM((w_in.shape[1], atoms), F32)],
         "source",
-        1,
-    )
-    source_first = swapped(source, "space", 1)
-    source_second = lax.ppermute(source, "space", [(i, other[i] % spaces) for i in range(spaces)])
-    cut = NHARM * channels
-    unit = 2 * (channels + 16)
-    block = jnp.concatenate([own[:channels], own[cut:], first[:channels], first[cut:]], 0)
-    held = jnp.concatenate([block[None], swapped(block, "space", 2)[None]], 0)
-    sources = jnp.concatenate([source, source_first], 0)[None]
-    bit = 4
-    while bit < spaces:
-        flat = jnp.concatenate(
-            [held.reshape(-1, atoms), sources.reshape(-1, atoms)], 0
-        )
-        other_flat = swapped(flat, "space", bit)
-        split = held.shape[0] * unit
-        held = jnp.concatenate([held, other_flat[:split].reshape(held.shape)], 0)
-        sources = jnp.concatenate([sources, other_flat[split:].reshape(sources.shape)], 0)
-        bit *= 2
-    sources_two = swapped(sources, "space", 2)
+        COST["source"],
+    )
+    unit_first = swapped(unit, "space", 1)
+    unit_second = lax.ppermute(unit[channels:], "space", route)
+    block = jnp.concatenate([unit, unit_first], 0)
+    held = block[None]
+    bit = spaces // 2
+    while bit > 2:
+        held = jnp.concatenate([held, swapped(held, "space", bit)], 0)
+        bit //= 2
+    held_rest = swapped(held, "space", 2)
     radial, coord, filt, weight = call(
         functools.partial(radial_kernel, spaces),
         (
@@ -650,51 +688,79 @@
             shape((16, KMODE), F32),
         ),
         (place,),
-        (own, first, second, wave_ints, w_rad),
+        (unit, unit_first, unit_second, wave_ints, w_rad),
         [pltpu.VMEM((3 * atoms, 8), F32), pltpu.VMEM((16, atoms), F32)],
         "radial",
-        3,
+        COST["radial"],
     )
     near_grad = call(
         near_grad_kernel,
         shape((channels, atoms), F32),
         (),
-        (own, first, second, radial, coord, filt),
+        (cots, first, second, radial, coord, filt),
         near_scratch(channels, atoms),
         "near_grad",
-        3,
+        COST["near_grad"],
     )
     scalar, rest = call(
         near_messages_kernel,
         (shape((channels, atoms), F32), shape((NHARM - 1, channels, atoms), BF)),
         (),
-        (source, source_first, source_second, radial, coord, filt),
+        (unit, unit_first, unit_second, radial, coord, filt),
         near_scratch(channels, atoms),
         "near_messages",
-        3,
+        COST["near_messages"],
+    )
+    terms = ((2 * KLONG + 1) * channels, 2 * KMODE)
+    table = pltpu.VMEM((2 * KMODE, spaces // 2 * atoms), BF)
+    long_rows = pltpu.VMEM((16, spaces // 2 * atoms), F32)
+    cot_sums, source_sums, modes_own, longs_own = call(
+        functools.partial(half_kernel, length),
+        (
+            shape(terms, F32),
+            shape(terms, F32),
+            shape((2 * KMODE, atoms), BF),
+            shape((16, atoms), F32),
+        ),
+        (),
+        (held,),
+        far_scratch(channels, atoms, spaces) + [table, long_rows],
+        "half",
+        COST["half"],
     )
     scaled, modes, longs = call(
         functools.partial(scaled_kernel, length),
         (
             shape((channels, atoms), BF),
-            shape((2 * KMODE, spaces * atoms), BF),
-            shape((16, spaces * atoms), F32),
+            shape((2 * KMODE, spaces // 2 * atoms), BF),
+            shape((16, spaces // 2 * atoms), F32),
         ),
         (),
-        (held, near_grad, weight, gain, scalar),
+        (held_rest, near_grad, weight, gain, cot_sums, modes_own, longs_own, scalar),
         far_scratch(channels, atoms, spaces),
         "scaled",
-        2,
+        COST["scaled"],
     )
     scaled_pieces = chan_pieces(scaled, scaled)
     messages, token = call(
         messages_kernel,
         (shape((NHARM, channels, atoms), BF), shape((8, 128), F32)),
         (),
-        (sources, sources_two, scalar, rest, coord, weight, modes, longs),
+        (
+            held_rest,
+            scalar,
+            rest,
+            coord,
+            weight,
+            source_sums,
+            modes_own,
+            longs_own,
+            modes,
+            longs,
+        ),
         far_scratch(channels, atoms, spaces),
         "messages",
-        2,
+        COST["messages"],
     )
     grad_features = call(
         final_kernel if chans > 2 else two_chan(final_kernel, 4),
@@ -703,7 +769,7 @@
         (w_copy, *scaled_pieces, token),
         [pltpu.VMEM((chans * channels, atoms), BF)],
         "final",
-        1,
+        COST["final"],
     )
     return (messages, grad_features)
 

time: 38.7 us -> 36.5 us (0.943)
  waiting for transfers between devices: 9.39 us -> 5.66 us
  Pallas kernels: 12.5 us -> 13.3 us
  starting transfers between devices: 15.1 us -> 15.9 us
    ppermute x9, waiting for transfers between devices: 7.81 us -> 3.93 us  [swapped(): lax.ppermute(block, axis, [(i, i ^ bit) for i in range(lax.axis_size(axis...]
    ppermute x2, starting transfers between devices: 4.72 us -> 7.15 us  [the longest x1 3.57 us: on_device(): second = lax.ppermute(cots, 'space', route)]
    ppermute x9, starting transfers between devices: 10.4 us -> 8.76 us  [swapped(): lax.ppermute(block, axis, [(i, i ^ bit) for i in range(lax.axis_size(axis...]
    pallas_call x7 -> x8, Pallas kernels: 11.4 us -> 12.3 us  [call(): pl.pallas_call(kernel, out_shape=out_shape, in_specs=[SMEM] * len(smem) +...]
  transfers between devices with their start and end apart: 11 -> 11, of which waited for: 6 -> 6; matrix products, arithmetic and copies ran while one was open for 0% -> 0% of each run, Pallas kernels for 25% -> 31%
where the time goes in v3:
time: 36.5 us; the launch traced here: 36.3 us
  starting transfers between devices  15.9 us (44%)
  Pallas kernels  13.3 us (36%)
  waiting for transfers between devices  5.66 us (16%)
  between operations  1.41 us (4%)
    pallas_call x8, Pallas kernels, call(): pl.pallas_call(kernel, out_shape=out_shape, in_specs=[SMEM] * len(smem) +...  12.3 us
    ppermute x9, starting transfers between devices, swapped(): lax.ppermute(block, axis, [(i, i ^ bit) for i in range(lax.axis_size(axis...  8.76 us
    ppermute x9, waiting for transfers between devices, swapped(): lax.ppermute(block, axis, [(i, i ^ bit) for i in range(lax.axis_size(axis...  3.93 us
    ppermute x1, starting transfers between devices, on_device(): second = lax.ppermute(cots, 'space', route)  3.57 us
    ppermute x1, starting transfers between devices, on_device(): unit_second = lax.ppermute(unit[channels:], 'space', route)  3.57 us
    ppermute x1, waiting for transfers between devices, on_device(): unit_second = lax.ppermute(unit[channels:], 'space', route)  1.73 us
    pallas_call x1, Pallas kernels, on_device(): pl.pallas_call(prep_kernel, out_shape=(shape((channels + 16, atoms), BF),...  1.03 us
  transfers between devices with their start and end apart: 11, of which 6 were waited for; matrix products, arithmetic and copies ran while one was open for 0% of the time, Pallas kernels for 31%

profile of v3, /device:TPU:0, one launch (start us, length us, event | category | flops | bytes accessed | tf_op | source)
XLA Modules:
  0.0 36.3 jit_solution(16600347671971376598)
XLA Ops:
  0.6 0.0 copy-start.1
  0.6 0.0 copy-start.2
  0.7 3.0 %collective-permute-start.3 = (bf16[288,256]{1,0:T(8,128)(2,1)}, bf16[288,256]{1,0:T(8,128)(2,1)S(1)}, u32[]{:S(2)}, u32[]{:S(2)}) collective-permute-start(bf16[288,256]{1,0:T(8,128)(2,1)} %bitcast.6), channel_id=1, source_target_pairs={{0,4},{4,0},{8,12},{12,8},{16,20},{20,16},{24,28},{28,24},{1,5},{5... | collective-permute-start | bytes 442376 | tf_op jit(solution)/shard_map/ppermute | solution.py:571
  3.7 3.6 %collective-permute-start.4 = (bf16[288,256]{1,0:T(8,128)(2,1)}, bf16[288,256]{1,0:T(8,128)(2,1)S(1)}, u32[]{:S(2)}, u32[]{:S(2)}) collective-permute-start(bf16[288,256]{1,0:T(8,128)(2,1)} %bitcast.7), channel_id=1, source_target_pairs={{0,28},{4,8},{8,4},{12,16},{16,12},{20,24},{24,20},{28,0},{1,29},{... | collective-permute-start | bytes 442376 | tf_op jit(solution)/shard_map/ppermute | solution.py:662
  7.2 0.0 collective-permute-start
  7.2 1.5 %collective-permute-start.1 = (bf16[32,256]{1,0:T(8,128)(2,1)}, bf16[32,256]{1,0:T(8,128)(2,1)S(1)}, u32[]{:S(2)}, u32[]{:S(2)}) collective-permute-start(bf16[32,256]{1,0:T(8,128)(2,1)} %feats_hbm.1), channel_id=1, source_target_pairs={{0,2},{1,3},{2,0},{3,1},{4,6},{5,7},{6,4},{7,5},{8,10},{9,11},{10,... | collective-permute-start | bytes 49160 | tf_op jit(solution)/shard_map/ppermute | solution.py:571
  8.8 0.3 collective-permute-start.2
  9.7 1.0 %prep.1 = (bf16[48,256]{1,0:T(8,128)(2,1)S(1)}, f32[32,256]{1,0:T(8,128)S(1)}, bf16[32,256]{1,0:T(8,128)(2,1)S(1)}, bf16[128,128]{1,0:T(8,128)(2,1)S(1)}) custom-call(s32[1]{0:T(128)S(6)} %copy.14.live_ref, s32[4]{0:T(128)} %count_hbm.1, s32[16]{0:T(128)} %home_hbm.1, s32[16]{0:T(128)} %reach_hbm.1, f32[3,256]{1,0:T(4,128)} %pos_hbm.1, ...), custom_call_target="tpu_custom_call" | custom-call | flops 1000000000 | bytes 3000000 | tf_op jit(solution)/shard_map/prep/pallas_call | solution.py:620
  10.8 0.0 collective-permute-done.refs_1_
  10.8 0.4 %collective-permute-done.1.refs_2_ = bf16[32,256]{1,0:T(8,128)(2,1)S(1)} collective-permute-done((bf16[32,256]{1,0:T(8,128)(2,1)}, bf16[32,256]{1,0:T(8,128)(2,1)S(1)}, u32[]{:S(2)}, u32[]{:S(2)}) %collective-permute-start.1) | collective-permute-done | bytes 16416 | tf_op jit(solution)/shard_map/ppermute | solution.py:571
  11.2 0.9 %collective-permute-done.2.refs_3_ = bf16[32,256]{1,0:T(8,128)(2,1)S(1)} collective-permute-done((bf16[32,256]{1,0:T(8,128)(2,1)}, bf16[32,256]{1,0:T(8,128)(2,1)S(1)}, u32[]{:S(2)}, u32[]{:S(2)}) %collective-permute-start.2) | collective-permute-done | bytes 16416 | tf_op jit(solution)/shard_map/ppermute | solution.py:571
  12.1 0.0 collective-permute-done.3.refs_7_.first_ref
  12.1 0.0 collective-permute-done.4.refs_8_.second_ref
  12.1 0.2 source.1.own_ref
  12.3 0.0 copy-start
  12.3 0.5 %collective-permute-start.5 = (bf16[80,256]{1,0:T(8,128)(2,1)S(1)}, bf16[80,256]{1,0:T(8,128)(2,1)S(1)}, u32[]{:S(2)}, u32[]{:S(2)}) collective-permute-start(bf16[80,256]{1,0:T(8,128)(2,1)S(1)} %source.1.own_ref), channel_id=1, source_target_pairs={{0,4},{4,0},{8,12},{12,8},{16,20},{20,16},{24,28},{28,24},{1,5},{5... | collective-permute-start | bytes 122888 | tf_op jit(solution)/shard_map/ppermute | solution.py:571
  12.9 3.6 %collective-permute-start.8 = (bf16[48,256]{1,0:T(8,128)(2,1)S(1)}, bf16[48,256]{1,0:T(8,128)(2,1)S(1)}, u32[]{:S(2)}, u32[]{:S(2)}) collective-permute-start(bf16[48,256]{1,0:T(8,128)(2,1)S(1)} %slice.4), channel_id=1, source_target_pairs={{0,28},{4,8},{8,4},{12,16},{16,12},{20,24},{24,20},{28,0},{1,29},{... | collective-permute-start | bytes 73736 | tf_op jit(solution)/shard_map/ppermute | solution.py:674
  16.5 0.0 collective-permute-done.5.first_ref
  16.5 1.5 %collective-permute-start.6 = (bf16[1,160,256]{2,1,0:T(8,128)(2,1)S(1)}, bf16[1,160,256]{2,1,0:T(8,128)(2,1)S(1)}, u32[]{:S(2)}, u32[]{:S(2)}) collective-permute-start(bf16[1,160,256]{2,1,0:T(8,128)(2,1)S(1)} %maximum_bitcast_fusion), channel_id=1, source_target_pairs={{0,16},{4,20},{8,24},{12,28},{16,0},{20,4},{24,8},{28,12},{1,17},{... | collective-permute-start | bytes 245768 | tf_op jit(solution)/shard_map/ppermute | solution.py:571
  18.0 1.7 %collective-permute-done.8.second_ref = bf16[48,256]{1,0:T(8,128)(2,1)S(1)} collective-permute-done((bf16[48,256]{1,0:T(8,128)(2,1)S(1)}, bf16[48,256]{1,0:T(8,128)(2,1)S(1)}, u32[]{:S(2)}, u32[]{:S(2)}) %collective-permute-start.8) | collective-permute-done | bytes 24608 | tf_op jit(solution)/shard_map/ppermute | solution.py:674
  19.7 0.0 copy-done.1
  19.7 0.0 copy-done.2
  19.7 2.1 %radial.1 = (bf16[16,768,256]{2,1,0:T(8,128)(2,1)S(1)}, f32[3,8,256]{2,1,0:T(8,128)S(1)}, f32[16,32,256]{2,1,0:T(8,128)S(1)}, f32[16,128]{1,0:T(8,128)S(1)}) custom-call(s32[1]{0:T(128)} %bitcast.4.place_ref, bf16[80,256]{1,0:T(8,128)(2,1)S(1)} %source.1.own_ref, bf16[80,256]{1,0:T(8,128)(2,1)S(1)} %collective-permute-done.5.first_ref, ...), custom_call_target="tpu_custom_call" | custom-call | flops 3000000000 | bytes 9000000 | tf_op jit(solution)/shard_map/radial/pallas_call | solution.py:605
  21.8 0.8 %collective-permute-done.6 = bf16[1,160,256]{2,1,0:T(8,128)(2,1)S(1)} collective-permute-done((bf16[1,160,256]{2,1,0:T(8,128)(2,1)S(1)}, bf16[1,160,256]{2,1,0:T(8,128)(2,1)S(1)}, u32[]{:S(2)}, u32[]{:S(2)}) %collective-permute-start.6) | collective-permute-done | bytes 81952 | tf_op jit(solution)/shard_map/ppermute | solution.py:571
  22.7 0.1 collective-permute-start.7
  22.7 0.0 copy-done
  22.8 2.1 %near_grad.1.near_ref = f32[32,256]{1,0:T(8,128)S(1)} custom-call(bf16[288,256]{1,0:T(8,128)(2,1)S(1)} %bitcast.9, bf16[288,256]{1,0:T(8,128)(2,1)S(1)} %collective-permute-done.3.refs_7_.first_ref, bf16[288,256]{1,0:T(8,128)(2,1)S(1)} %collective-permute-done.4.refs_8_.second_ref, bf16[16,768,256]{2,1,0:T(8,128)(2,1)S(1)} %get-tuple-element.25.radial_ref, ...), custom_call_target="tpu_custom_call" | custom-call | flops 3000000000 | bytes 9000000 | tf_op jit(solution)/shard_map/near_grad/pallas_call | solution.py:605
  24.9 2.1 %near_messages.1 = (f32[32,256]{1,0:T(8,128)S(1)}, bf16[8,32,256]{2,1,0:T(8,128)(2,1)S(1)}) custom-call(bf16[80,256]{1,0:T(8,128)(2,1)S(1)} %source.1.own_ref, bf16[80,256]{1,0:T(8,128)(2,1)S(1)} %collective-permute-done.5.first_ref, bf16[48,256]{1,0:T(8,128)(2,1)S(1)} %collective-permute-done.8.second_ref, ...), custom_call_target="tpu_custom_call" | custom-call | flops 1500000000 | bytes 4500000 | tf_op jit(solution)/shard_map/near_messages/pallas_call | solution.py:605
  27.0 2.2 %half.1 = (f32[544,256]{1,0:T(8,128)S(1)}, f32[544,256]{1,0:T(8,128)S(1)}, bf16[256,256]{1,0:T(8,128)(2,1)S(1)}, f32[16,256]{1,0:T(8,128)S(1)}) custom-call(bf16[2,160,256]{2,1,0:T(8,128)(2,1)S(1)} %pad_maximum_fusion.held_ref), custom_call_target="tpu_custom_call" | custom-call | flops 200000000 | bytes 600000 | tf_op jit(solution)/shard_map/half/pallas_call | solution.py:605
  29.2 0.0 collective-permute-done.7.rest_ref.held_ref
  29.2 1.2 %scaled.1 = (bf16[32,256]{1,0:T(8,128)(2,1)S(1)}, bf16[256,1024]{1,0:T(8,128)(2,1)S(1)}, f32[16,1024]{1,0:T(8,128)S(1)}) custom-call(bf16[2,160,256]{2,1,0:T(8,128)(2,1)S(1)} %collective-permute-done.7.rest_ref.held_ref, f32[32,256]{1,0:T(8,128)S(1)} %near_grad.1.near_ref, f32[16,128]{1,0:T(8,128)S(1)} %get-tuple-element.30.weight_ref, ...), custom_call_target="tpu_custom_call" | custom-call | flops 2000000000 | bytes 6000000 | tf_op jit(solution)/shard_map/scaled/pallas_call | solution.py:605
  30.4 0.1 collective-permute-start.9
  30.5 1.2 %collective-permute-done.9.first_ref = bf16[32,256]{1,0:T(8,128)(2,1)S(1)} collective-permute-done((bf16[32,256]{1,0:T(8,128)(2,1)S(1)}, bf16[32,256]{1,0:T(8,128)(2,1)S(1)}, u32[]{:S(2)}, u32[]{:S(2)}) %collective-permute-start.9) | collective-permute-done | bytes 16416 | tf_op jit(solution)/shard_map/ppermute | solution.py:571
  31.7 1.7 %collective-permute-start.10 = (bf16[64,256]{1,0:T(8,128)(2,1)S(1)}, bf16[64,256]{1,0:T(8,128)(2,1)S(1)}, u32[]{:S(2)}, u32[]{:S(2)}) collective-permute-start(bf16[64,256]{1,0:T(8,128)(2,1)S(1)} %pad_maximum_fusion.1), channel_id=1, source_target_pairs={{0,2},{1,3},{2,0},{3,1},{4,6},{5,7},{6,4},{7,5},{8,10},{9,11},{10,... | collective-permute-start | bytes 98312 | tf_op jit(solution)/shard_map/ppermute | solution.py:571
  33.4 1.6 %messages.1 = (bf16[9,32,256]{2,1,0:T(8,128)(2,1)}, f32[8,128]{1,0:T(8,128)S(1)}) custom-call(bf16[2,160,256]{2,1,0:T(8,128)(2,1)S(1)} %collective-permute-done.7.rest_ref.held_ref, f32[32,256]{1,0:T(8,128)S(1)} %get-tuple-element.28.order_ref.scalar_ref, bf16[8,32,256]{2,1,0:T(8,128)(2,1)S(1)} %get-tuple-element.29.rest_ref, ...), custom_call_target="tpu_custom_call" | custom-call | flops 2000000000 | bytes 6000000 | tf_op jit(solution)/shard_map/messages/pallas_call | solution.py:605
  35.0 0.6 %collective-permute-done.10.other_ref = bf16[64,256]{1,0:T(8,128)(2,1)S(1)} collective-permute-done((bf16[64,256]{1,0:T(8,128)(2,1)S(1)}, bf16[64,256]{1,0:T(8,128)(2,1)S(1)}, u32[]{:S(2)}, u32[]{:S(2)}) %collective-permute-start.10) | collective-permute-done | bytes 32800 | tf_op jit(solution)/shard_map/ppermute | solution.py:571
  35.6 0.8 %final.1 = f32[32,256]{1,0:T(8,128)} custom-call(s32[1]{0:T(128)} %bitcast.lane_ref, bf16[128,128]{1,0:T(8,128)(2,1)S(1)} %get-tuple-element.22.refs_4_.w_ref, bf16[32,256]{1,0:T(8,128)(2,1)S(1)} %get-tuple-element.38.own_ref, bf16[32,256]{1,0:T(8,128)(2,1)S(1)} %collective-permute-done.9.first_ref, bf16[64,256]{1,0:T(8,128)(2,1)S(1)} %collective-permute-done.10.other_ref, ...), custom_call_target="tpu_custom_call" | custom-call | flops 1000000000 | bytes 3000000 | tf_op jit(solution)/shard_map/final/pallas_call | solution.py:605
  (4 shorter events, 0.0 us)
Async XLA Ops:
  0.6 19.1 %copy-start.1 = (s32[3,1024]{1,0:T(4,128)S(1)}, s32[3,1024]{1,0:T(4,128)}, u32[]{:S(2)}) copy-start(s32[3,1024]{1,0:T(4,128)} %wave_ref.1) | copy-start | bytes 36868
  0.6 19.1 %copy-start.2 = (f32[16,32]{1,0:T(8,128)S(1)}, f32[16,32]{1,0:T(8,128)}, u32[]{:S(2)}) copy-start(f32[16,32]{1,0:T(8,128)} %w_rad_ref.1) | copy-start | bytes 6148
  0.7 11.5 %collective-permute-start.3 = (bf16[288,256]{1,0:T(8,128)(2,1)}, bf16[288,256]{1,0:T(8,128)(2,1)S(1)}, u32[]{:S(2)}, u32[]{:S(2)}) collective-permute-start(bf16[288,256]{1,0:T(8,128)(2,1)} %bitcast.6), channel_id=1, source_target_pairs={{0,4},{4,0},{8,12},{12,8},{16,20},{20,16},{24,28},{28,24},{1,5},{5... | collective-permute-start | bytes 442376 | tf_op jit(solution)/shard_map/ppermute | solution.py:571
  3.7 8.5 %collective-permute-start.4 = (bf16[288,256]{1,0:T(8,128)(2,1)}, bf16[288,256]{1,0:T(8,128)(2,1)S(1)}, u32[]{:S(2)}, u32[]{:S(2)}) collective-permute-start(bf16[288,256]{1,0:T(8,128)(2,1)} %bitcast.7), channel_id=1, source_target_pairs={{0,28},{4,8},{8,4},{12,16},{16,12},{20,24},{24,20},{28,0},{1,29},{... | collective-permute-start | bytes 442376 | tf_op jit(solution)/shard_map/ppermute | solution.py:662
  7.2 3.6 %collective-permute-start = (bf16[32,256]{1,0:T(8,128)(2,1)}, bf16[32,256]{1,0:T(8,128)(2,1)S(1)}, u32[]{:S(2)}, u32[]{:S(2)}) collective-permute-start(bf16[32,256]{1,0:T(8,128)(2,1)} %feats_hbm.1), channel_id=1, source_target_pairs={{0,1},{1,0},{2,3},{3,2},{4,5},{5,4},{6,7},{7,6},{8,9},{9,8},{10,11... | collective-permute-start | bytes 49160 | tf_op jit(solution)/shard_map/ppermute | solution.py:571
  7.2 3.9 %collective-permute-start.1 = (bf16[32,256]{1,0:T(8,128)(2,1)}, bf16[32,256]{1,0:T(8,128)(2,1)S(1)}, u32[]{:S(2)}, u32[]{:S(2)}) collective-permute-start(bf16[32,256]{1,0:T(8,128)(2,1)} %feats_hbm.1), channel_id=1, source_target_pairs={{0,2},{1,3},{2,0},{3,1},{4,6},{5,7},{6,4},{7,5},{8,10},{9,11},{10,... | collective-permute-start | bytes 49160 | tf_op jit(solution)/shard_map/ppermute | solution.py:571
  8.8 3.4 %collective-permute-start.2 = (bf16[32,256]{1,0:T(8,128)(2,1)}, bf16[32,256]{1,0:T(8,128)(2,1)S(1)}, u32[]{:S(2)}, u32[]{:S(2)}) collective-permute-start(bf16[32,256]{1,0:T(8,128)(2,1)} %feats_hbm.1), channel_id=1, source_target_pairs={{0,3},{1,2},{2,1},{3,0},{4,7},{5,6},{6,5},{7,4},{8,11},{9,10},{10,... | collective-permute-start | bytes 49160 | tf_op jit(solution)/shard_map/ppermute | solution.py:571
  12.3 10.4 %copy-start = (bf16[9,32,256]{2,1,0:T(8,128)(2,1)S(1)}, bf16[9,32,256]{2,1,0:T(8,128)(2,1)}, u32[]{:S(2)}) copy-start(bf16[9,32,256]{2,1,0:T(8,128)(2,1)} %param.23) | copy-start | bytes 442372
  12.3 4.1 %collective-permute-start.5 = (bf16[80,256]{1,0:T(8,128)(2,1)S(1)}, bf16[80,256]{1,0:T(8,128)(2,1)S(1)}, u32[]{:S(2)}, u32[]{:S(2)}) collective-permute-start(bf16[80,256]{1,0:T(8,128)(2,1)S(1)} %source.1.own_ref), channel_id=1, source_target_pairs={{0,4},{4,0},{8,12},{12,8},{16,20},{20,16},{24,28},{28,24},{1,5},{5... | collective-permute-start | bytes 122888 | tf_op jit(solution)/shard_map/ppermute | solution.py:571
  12.9 6.8 %collective-permute-start.8 = (bf16[48,256]{1,0:T(8,128)(2,1)S(1)}, bf16[48,256]{1,0:T(8,128)(2,1)S(1)}, u32[]{:S(2)}, u32[]{:S(2)}) collective-permute-start(bf16[48,256]{1,0:T(8,128)(2,1)S(1)} %slice.4), channel_id=1, source_target_pairs={{0,28},{4,8},{8,4},{12,16},{16,12},{20,24},{24,20},{28,0},{1,29},{... | collective-permute-start | bytes 73736 | tf_op jit(solution)/shard_map/ppermute | solution.py:674
  16.5 6.2 %collective-permute-start.6 = (bf16[1,160,256]{2,1,0:T(8,128)(2,1)S(1)}, bf16[1,160,256]{2,1,0:T(8,128)(2,1)S(1)}, u32[]{:S(2)}, u32[]{:S(2)}) collective-permute-start(bf16[1,160,256]{2,1,0:T(8,128)(2,1)S(1)} %maximum_bitcast_fusion), channel_id=1, source_target_pairs={{0,16},{4,20},{8,24},{12,28},{16,0},{20,4},{24,8},{28,12},{1,17},{... | collective-permute-start | bytes 245768 | tf_op jit(solution)/shard_map/ppermute | solution.py:571
  22.7 6.5 %collective-permute-start.7 = (bf16[2,160,256]{2,1,0:T(8,128)(2,1)S(1)}, bf16[2,160,256]{2,1,0:T(8,128)(2,1)S(1)}, u32[]{:S(2)}, u32[]{:S(2)}) collective-permute-start(bf16[2,160,256]{2,1,0:T(8,128)(2,1)S(1)} %pad_maximum_fusion.held_ref), channel_id=1, source_target_pairs={{0,8},{4,12},{8,0},{12,4},{16,24},{20,28},{24,16},{28,20},{1,9},{5... | collective-permute-start | bytes 491528 | tf_op jit(solution)/shard_map/ppermute | solution.py:571
  30.4 1.2 %collective-permute-start.9 = (bf16[32,256]{1,0:T(8,128)(2,1)S(1)}, bf16[32,256]{1,0:T(8,128)(2,1)S(1)}, u32[]{:S(2)}, u32[]{:S(2)}) collective-permute-start(bf16[32,256]{1,0:T(8,128)(2,1)S(1)} %get-tuple-element.38.own_ref), channel_id=1, source_target_pairs={{0,1},{1,0},{2,3},{3,2},{4,5},{5,4},{6,7},{7,6},{8,9},{9,8},{10,11... | collective-permute-start | bytes 49160 | tf_op jit(solution)/shard_map/ppermute | solution.py:571
  31.7 3.9 %collective-permute-start.10 = (bf16[64,256]{1,0:T(8,128)(2,1)S(1)}, bf16[64,256]{1,0:T(8,128)(2,1)S(1)}, u32[]{:S(2)}, u32[]{:S(2)}) collective-permute-start(bf16[64,256]{1,0:T(8,128)(2,1)S(1)} %pad_maximum_fusion.1), channel_id=1, source_target_pairs={{0,2},{1,3},{2,0},{3,1},{4,6},{5,7},{6,4},{7,5},{8,10},{9,11},{10,... | collective-permute-start | bytes 98312 | tf_op jit(solution)/shard_map/ppermute | solution.py:571

commit v4 on v3

--- a/solution.py
+++ b/solution.py
@@ -30,7 +30,7 @@
 R5 = math.sqrt(5.0)
 R15 = math.sqrt(15.0)
 
-COST = dict(prep=1, source=1, radial=3, near_grad=3, near_messages=1.5, scaled=2, half=0.2, messages=2, final=1)
+COST = dict(prep=1, source=1, radial=3, near_grad=3, near_messages=4, scaled=2, half=0.2, messages=2, final=1)
 VMEM = pl.BlockSpec(memory_space=pltpu.VMEM)
 SMEM = pl.BlockSpec(memory_space=pltpu.SMEM)
 
@@ -195,7 +195,7 @@
     out_ref[channels + 16 :, :] = (mixed * gain_ref[...]).astype(BF)
 
 
-def geometry(place, spaces, halos, channels, cols_ref, live_ref, coord_ref):
+def geometry(place, spaces, halos, tiles, channels, cols_ref, live_ref, coord_ref):
     atoms = halos[0].shape[1]
     blocks = atoms // BLOCK
     length = SLICE_WIDTH * blocks * spaces
@@ -204,77 +204,56 @@
     centre = (place.astype(F32) + 0.5) * (SLICE_WIDTH * blocks)
     lane = lax.broadcasted_iota(jnp.int32, (1, atoms), 1)
     home = lane // BLOCK
-    tails = []
-    for h in halos:
-        cut = h.shape[0] - channels
-        tails.append(h[cut - 16 : cut, :])
+    none = jnp.zeros((1, atoms), F32)
+
+    def tail_of(halo):
+        cut = halo.shape[0] - channels
+        return halo[cut - 16 : cut, :]
 
     def flag_row(tail, h, r):
         index = h * REACH + r - 1
         return jnp.broadcast_to(tail[9:10, index : index + 1].astype(F32), (1, atoms))
 
-    coords, valids = [], []
-    for t in range(3):
-        x, y, z = unpack_pos(tails[t])
+    def coords_of(t, tail):
+        x, y, z = unpack_pos(tail)
         x = x - (centre - wrap) if t == 2 else x - centre
         x = x * (1.0 / CUTOFF)
         y = (y - SIDE_CENTRE) * (1.0 / CUTOFF)
         z = (z - SIDE_CENTRE) * (1.0 / CUTOFF)
-        coords.append((x, y, z))
-        valids.append(tails[t][10:11].astype(F32))
-        padded = jnp.concatenate([x, y, z, valids[t], jnp.zeros((4, atoms), F32)], 0)
-        coord_ref[t] = padded
-        cols_ref[t * atoms : (t + 1) * atoms, :] = padded.T
-    none = jnp.zeros((1, atoms), F32)
-    for e in range(blocks):
-        row = none
-        for h in range(blocks):
-            d = abs(e - h)
-            value = none + 1.0 if d == 0 else flag_row(tails[0], min(e, h), d)
-            row = jnp.where(home == h, value, row)
-        live_ref[e : e + 1, :] = row
-        ahead = none
-        for h in range(blocks):
-            d = e + blocks - h
-            if d <= REACH:
-                ahead = jnp.where(home == h, flag_row(tails[0], h, d), ahead)
-        for t in (1, 2):
-            behind = none
-            for h in range(blocks):
-                d = h + blocks - e
-                if d <= REACH:
-                    behind = jnp.where(home == h, flag_row(tails[t], e, d), behind)
-            is_ahead = even if t == 1 else jnp.logical_not(even)
-            live_ref[t * blocks + e : t * blocks + e + 1, :] = jnp.where(is_ahead, ahead, behind)
-    return coords[0]
-
-
-def radial_kernel(
-    spaces,
-    place_ref,
-    own_ref,
-    first_ref,
-    second_ref,
-    wave_ref,
-    w_rad_ref,
-    radial_ref,
-    coord_ref,
-    filt_ref,
-    weight_ref,
-    cols_ref,
-    live_ref,
-):
-    atoms = own_ref.shape[1]
-    length = SLICE_WIDTH * (atoms // BLOCK) * spaces
-    halos = (own_ref, first_ref, second_ref)
-    xa, ya, za = geometry(
-        place_ref[0], spaces, halos, w_rad_ref.shape[1], cols_ref, live_ref, coord_ref
-    )
-    w_cols = w_rad_ref[...].T
-    for n in range(NRAD):
-        filt_ref[n] = jnp.broadcast_to(w_cols[:, n : n + 1], filt_ref.shape[1:])
+        return x, y, z
+
+    own_tail = tail_of(halos[0])
+    own = coords_of(0, own_tail)
+    for i, t in enumerate(tiles):
+        tail = tail_of(halos[t])
+        valid = tail[10:11].astype(F32)
+        padded = jnp.concatenate([*coords_of(t, tail), valid, jnp.zeros((4, atoms), F32)], 0)
+        coord_ref[i] = padded
+        cols_ref[i * atoms : (i + 1) * atoms, :] = padded.T
+        for e in range(blocks):
+            row = none
+            if t == 0:
+                for h in range(blocks):
+                    d = abs(e - h)
+                    value = none + 1.0 if d == 0 else flag_row(tail, min(e, h), d)
+                    row = jnp.where(home == h, value, row)
+            else:
+                behind = none
+                for h in range(blocks):
+                    if e + blocks - h <= REACH:
+                        row = jnp.where(home == h, flag_row(own_tail, h, e + blocks - h), row)
+                    if h + blocks - e <= REACH:
+                        behind = jnp.where(home == h, flag_row(tail, e, h + blocks - e), behind)
+                row = jnp.where(even if t == 1 else jnp.logical_not(even), row, behind)
+            live_ref[i * blocks + e : i * blocks + e + 1, :] = row
+    return own
+
+
+def fill_radial(own, tiles, cols_ref, live_ref, radial_ref):
+    xa, ya, za = own
+    atoms = xa.shape[1]
     chunk = BLOCK
-    for index in range(3 * atoms // chunk):
+    for index in range(len(tiles) * atoms // chunk):
         lo = index * chunk
         at = slice(lo, lo + chunk)
         col = cols_ref[at, :]
@@ -284,7 +263,7 @@
         s = jnp.minimum(dx * dx + dy * dy + dz * dz, 1.0)
         gap = 1.0 - s
         envelope = gap * gap * live_ref[index : index + 1, :]
-        if lo < atoms:
+        if tiles[lo // atoms] == 0:
             other = lax.broadcasted_iota(jnp.int32, (chunk, atoms), 0) + lo
             me = lax.broadcasted_iota(jnp.int32, (chunk, atoms), 1)
             envelope = jnp.where(other == me, 0.0, envelope)
@@ -301,12 +280,51 @@
         for n in range(MID, 0, -1):
             value = value * (shrink * math.exp((2 * n - 1) / 2))
             radial_ref[n - 1, at, :] = value.astype(BF)
+
+
+def radial_kernel(
+    spaces,
+    place_ref,
+    own_ref,
+    first_ref,
+    wave_ref,
+    w_rad_ref,
+    radial_ref,
+    coord_ref,
+    filt_ref,
+    weight_ref,
+    cols_ref,
+    live_ref,
+):
+    atoms = own_ref.shape[1]
+    length = SLICE_WIDTH * (atoms // BLOCK) * spaces
+    channels = w_rad_ref.shape[1]
+    halos = (own_ref, first_ref)
+    own = geometry(
+        place_ref[0], spaces, halos, (0, 1), channels, cols_ref, live_ref, coord_ref
+    )
+    w_cols = w_rad_ref[...].T
+    for n in range(NRAD):
+        filt_ref[n] = jnp.broadcast_to(w_cols[:, n : n + 1], filt_ref.shape[1:])
+    fill_radial(own, (0, 1), cols_ref, live_ref, radial_ref)
     weight_ref[...] = mode_weights(wave_ref, length, atoms * spaces)
 
 
-def near_mix(left_ref, radial_ref, filt_ref, total_ref):
+def radial_other_kernel(
+    spaces, place_ref, own_ref, second_ref, filt_ref, radial_ref, coord_ref, cols_ref, live_ref
+):
+    halos = (own_ref, None, second_ref)
+    channels = filt_ref.shape[1]
+    own = geometry(place_ref[0], spaces, halos, (2,), channels, cols_ref, live_ref, coord_ref)
+    fill_radial(own, (2,), cols_ref, live_ref, radial_ref)
+
+
+def near_mix(left_ref, radial_ref, radial_other_ref, filt_ref, total_ref):
+    cut = radial_ref.shape[1]
     for n in range(NRAD):
-        part = dot_nn(left_ref[...], radial_ref[n]).reshape(total_ref.shape) * filt_ref[n][None]
+        part = dot_nn(left_ref[:, 0:cut], radial_ref[n])
+        part = part + dot_nn(left_ref[:, cut:], radial_other_ref[n])
+        part = part.reshape(total_ref.shape) * filt_ref[n][None]
         if n == 0:
             total_ref[...] = part
         else:
@@ -320,28 +338,42 @@
     ]
 
 
-def coord_rows(coord_ref, t):
-    tile = coord_ref[t]
+def coord_tile(coord_ref, coord_other_ref, t):
+    return coord_ref[t] if t < 2 else coord_other_ref[0]
+
+
+def coord_rows(coord_ref, coord_other_ref, t):
+    tile = coord_tile(coord_ref, coord_other_ref, t)
     return (tile[0:1], tile[1:2], tile[2:3])
 
 
 def near_grad_kernel(
-    own_ref, first_ref, second_ref, radial_ref, coord_ref, filt_ref, grad_ref, left_ref, total_ref
+    own_ref,
+    first_ref,
+    second_ref,
+    radial_ref,
+    radial_other_ref,
+    coord_ref,
+    coord_other_ref,
+    filt_ref,
+    grad_ref,
+    left_ref,
+    total_ref,
 ):
     channels, atoms = grad_ref.shape
     for t, halo in enumerate((own_ref, first_ref, second_ref)):
         at = slice(t * atoms, (t + 1) * atoms)
-        valid = coord_ref[t][3:4]
+        valid = coord_tile(coord_ref, coord_other_ref, t)[3:4]
         grads = [
             halo[l * channels : (l + 1) * channels, :].astype(F32) * valid for l in range(NHARM)
         ]
         moved = list(grads)
-        for (l, m), term in shift_terms(*coord_rows(coord_ref, t)).items():
+        for (l, m), term in shift_terms(*coord_rows(coord_ref, coord_other_ref, t)).items():
             moved[m] = moved[m] + grads[l] * term
         for m in range(NHARM):
             left_ref[m * channels : (m + 1) * channels, at] = moved[m].astype(BF)
-    near_mix(left_ref, radial_ref, filt_ref, total_ref)
-    harm = harmonic_rows(*coord_rows(coord_ref, 0))
+    near_mix(left_ref, radial_ref, radial_other_ref, filt_ref, total_ref)
+    harm = harmonic_rows(*coord_rows(coord_ref, coord_other_ref, 0))
     grad = total_ref[0]
     for m in range(1, NHARM):
         grad = grad + total_ref[m] * harm[m]
@@ -487,7 +519,9 @@
     first_ref,
     second_ref,
     radial_ref,
+    radial_other_ref,
     coord_ref,
+    coord_other_ref,
     filt_ref,
     scalar_ref,
     rest_ref,
@@ -500,14 +534,14 @@
         at = slice(t * atoms, (t + 1) * atoms)
         left_ref[0:channels, at] = ref[lo : lo + channels, :]
         source = ref[lo : lo + channels, :].astype(F32)
-        harm = harmonic_rows(*coord_rows(coord_ref, t))
+        harm = harmonic_rows(*coord_rows(coord_ref, coord_other_ref, t))
         for m in range(1, NHARM):
             left_ref[m * channels : (m + 1) * channels, at] = (source * harm[m]).astype(BF)
-    near_mix(left_ref, radial_ref, filt_ref, total_ref)
+    near_mix(left_ref, radial_ref, radial_other_ref, filt_ref, total_ref)
     valid = coord_ref[0][3:4]
     sums = [total_ref[m] for m in range(NHARM)]
     near = list(sums)
-    for (l, m), term in shift_terms(*coord_rows(coord_ref, 0)).items():
+    for (l, m), term in shift_terms(*coord_rows(coord_ref, coord_other_ref, 0)).items():
         near[l] = near[l] + sums[m] * term
     scalar_ref[...] = near[0] * valid
     for l in range(1, NHARM):
@@ -682,22 +716,31 @@
     radial, coord, filt, weight = call(
         functools.partial(radial_kernel, spaces),
         (
-            shape((NRAD, 3 * atoms, atoms), BF),
-            shape((3, 8, atoms), F32),
+            shape((NRAD, 2 * atoms, atoms), BF),
+            shape((2, 8, atoms), F32),
             shape((NRAD, channels, atoms), F32),
             shape((16, KMODE), F32),
         ),
         (place,),
-        (unit, unit_first, unit_second, wave_ints, w_rad),
-        [pltpu.VMEM((3 * atoms, 8), F32), pltpu.VMEM((16, atoms), F32)],
+        (unit, unit_first, wave_ints, w_rad),
+        [pltpu.VMEM((2 * atoms, 8), F32), pltpu.VMEM((16, atoms), F32)],
         "radial",
         COST["radial"],
+    )
+    radial_other, coord_other = call(
+        functools.partial(radial_other_kernel, spaces),
+        (shape((NRAD, atoms, atoms), BF), shape((1, 8, atoms), F32)),
+        (place,),
+        (unit, unit_second, filt),
+        [pltpu.VMEM((atoms, 8), F32), pltpu.VMEM((16, atoms), F32)],
+        "radial_other",
+        1,
     )
     near_grad = call(
         near_grad_kernel,
         shape((channels, atoms), F32),
         (),
-        (cots, first, second, radial, coord, filt),
+        (cots, first, second, radial, radial_other, coord, coord_other, filt),
         near_scratch(channels, atoms),
         "near_grad",
         COST["near_grad"],
@@ -706,7 +749,7 @@
         near_messages_kernel,
         (shape((channels, atoms), F32), shape((NHARM - 1, channels, atoms), BF)),
         (),
-        (unit, unit_first, unit_second, radial, coord, filt),
+        (unit, unit_first, unit_second, radial, radial_other, coord, coord_other, filt),
         near_scratch(channels, atoms),
         "near_messages",
         COST["near_messages"],

time: 36.5 us -> 35.7 us (0.978)
  waiting for transfers between devices: 5.66 us -> 3.61 us
  starting transfers between devices: 15.9 us -> 17 us
    ppermute x1, waiting for transfers between devices: 1.73 us -> 0.3 us  [on_device(): unit_second = lax.ppermute(unit[channels:], 'space', route)]
    ppermute x9, starting transfers between devices: 8.76 us -> 9.86 us  [swapped(): lax.ppermute(block, axis, [(i, i ^ bit) for i in range(lax.axis_size(axis...]
    ppermute x9, waiting for transfers between devices: 3.93 us -> 3.31 us  [swapped(): lax.ppermute(block, axis, [(i, i ^ bit) for i in range(lax.axis_size(axis...]
    pallas_call x8 -> x9, Pallas kernels: 12.3 us -> 12.4 us  [call(): pl.pallas_call(kernel, out_shape=out_shape, in_specs=[SMEM] * len(smem) +...]
  transfers between devices with their start and end apart: 11 -> 11, of which waited for: 6 -> 5; matrix products, arithmetic and copies ran while one was open for 0% -> 0% of each run, Pallas kernels for 31% -> 32%
where the time goes in v4:
time: 35.7 us; the launch traced here: 35.5 us
  starting transfers between devices  17 us (48%)
  Pallas kernels  13.4 us (38%)
  waiting for transfers between devices  3.61 us (10%)
  between operations  1.4 us (4%)
    pallas_call x9, Pallas kernels, call(): pl.pallas_call(kernel, out_shape=out_shape, in_specs=[SMEM] * len(smem) +...  12.4 us
    ppermute x9, starting transfers between devices, swapped(): lax.ppermute(block, axis, [(i, i ^ bit) for i in range(lax.axis_size(axis...  9.86 us
    ppermute x1, starting transfers between devices, on_device(): second = lax.ppermute(cots, 'space', route)  3.57 us
    ppermute x1, starting transfers between devices, on_device(): unit_second = lax.ppermute(unit[channels:], 'space', route)  3.57 us
    ppermute x9, waiting for transfers between devices, swapped(): lax.ppermute(block, axis, [(i, i ^ bit) for i in range(lax.axis_size(axis...  3.31 us
    pallas_call x1, Pallas kernels, on_device(): pl.pallas_call(prep_kernel, out_shape=(shape((channels + 16, atoms), BF),...  1.03 us
  transfers between devices with their start and end apart: 11, of which 5 were waited for; matrix products, arithmetic and copies ran while one was open for 0% of the time, Pallas kernels for 32%

profile of v4, /device:TPU:0, one launch (start us, length us, event | category | flops | bytes accessed | tf_op | source)
XLA Modules:
  0.0 35.5 jit_solution(6185415396699816192)
XLA Ops:
  0.6 0.0 copy-start.1
  0.6 0.0 copy-start.2
  0.7 3.0 %collective-permute-start.3 = (bf16[288,256]{1,0:T(8,128)(2,1)}, bf16[288,256]{1,0:T(8,128)(2,1)S(1)}, u32[]{:S(2)}, u32[]{:S(2)}) collective-permute-start(bf16[288,256]{1,0:T(8,128)(2,1)} %bitcast.6), channel_id=1, source_target_pairs={{0,4},{4,0},{8,12},{12,8},{16,20},{20,16},{24,28},{28,24},{1,5},{5... | collective-permute-start | bytes 442376 | tf_op jit(solution)/shard_map/ppermute | solution.py:605
  3.7 3.6 %collective-permute-start.4 = (bf16[288,256]{1,0:T(8,128)(2,1)}, bf16[288,256]{1,0:T(8,128)(2,1)S(1)}, u32[]{:S(2)}, u32[]{:S(2)}) collective-permute-start(bf16[288,256]{1,0:T(8,128)(2,1)} %bitcast.7), channel_id=1, source_target_pairs={{0,28},{4,8},{8,4},{12,16},{16,12},{20,24},{24,20},{28,0},{1,29},{... | collective-permute-start | bytes 442376 | tf_op jit(solution)/shard_map/ppermute | solution.py:696
  7.2 0.0 collective-permute-start
  7.2 1.5 %collective-permute-start.1 = (bf16[32,256]{1,0:T(8,128)(2,1)}, bf16[32,256]{1,0:T(8,128)(2,1)S(1)}, u32[]{:S(2)}, u32[]{:S(2)}) collective-permute-start(bf16[32,256]{1,0:T(8,128)(2,1)} %feats_hbm.1), channel_id=1, source_target_pairs={{0,2},{1,3},{2,0},{3,1},{4,6},{5,7},{6,4},{7,5},{8,10},{9,11},{10,... | collective-permute-start | bytes 49160 | tf_op jit(solution)/shard_map/ppermute | solution.py:605
  8.8 0.3 collective-permute-start.2
  9.7 1.0 %prep.1 = (bf16[48,256]{1,0:T(8,128)(2,1)S(1)}, f32[32,256]{1,0:T(8,128)S(1)}, bf16[32,256]{1,0:T(8,128)(2,1)S(1)}, bf16[128,128]{1,0:T(8,128)(2,1)S(1)}) custom-call(s32[1]{0:T(128)S(6)} %copy.14.live_ref, s32[4]{0:T(128)} %count_hbm.1, s32[16]{0:T(128)} %home_hbm.1, s32[16]{0:T(128)} %reach_hbm.1, f32[3,256]{1,0:T(4,128)} %pos_hbm.1, ...), custom_call_target="tpu_custom_call" | custom-call | flops 1000000000 | bytes 3000000 | tf_op jit(solution)/shard_map/prep/pallas_call | solution.py:654
  10.8 0.0 collective-permute-done.refs_1_
  10.8 0.4 %collective-permute-done.1.refs_2_ = bf16[32,256]{1,0:T(8,128)(2,1)S(1)} collective-permute-done((bf16[32,256]{1,0:T(8,128)(2,1)}, bf16[32,256]{1,0:T(8,128)(2,1)S(1)}, u32[]{:S(2)}, u32[]{:S(2)}) %collective-permute-start.1) | collective-permute-done | bytes 16416 | tf_op jit(solution)/shard_map/ppermute | solution.py:605
  11.2 0.9 %collective-permute-done.2.refs_3_ = bf16[32,256]{1,0:T(8,128)(2,1)S(1)} collective-permute-done((bf16[32,256]{1,0:T(8,128)(2,1)}, bf16[32,256]{1,0:T(8,128)(2,1)S(1)}, u32[]{:S(2)}, u32[]{:S(2)}) %collective-permute-start.2) | collective-permute-done | bytes 16416 | tf_op jit(solution)/shard_map/ppermute | solution.py:605
  12.1 0.0 collective-permute-done.3.refs_7_.first_ref
  12.1 0.0 collective-permute-done.4.refs_8_.second_ref
  12.1 0.2 source.1.own_ref
  12.3 0.5 %collective-permute-start.5 = (bf16[80,256]{1,0:T(8,128)(2,1)S(1)}, bf16[80,256]{1,0:T(8,128)(2,1)S(1)}, u32[]{:S(2)}, u32[]{:S(2)}) collective-permute-start(bf16[80,256]{1,0:T(8,128)(2,1)S(1)} %source.1.own_ref), channel_id=1, source_target_pairs={{0,4},{4,0},{8,12},{12,8},{16,20},{20,16},{24,28},{28,24},{1,5},{5... | collective-permute-start | bytes 122888 | tf_op jit(solution)/shard_map/ppermute | solution.py:605
  12.9 3.6 %collective-permute-start.8 = (bf16[48,256]{1,0:T(8,128)(2,1)S(1)}, bf16[48,256]{1,0:T(8,128)(2,1)S(1)}, u32[]{:S(2)}, u32[]{:S(2)}) collective-permute-start(bf16[48,256]{1,0:T(8,128)(2,1)S(1)} %slice.4), channel_id=1, source_target_pairs={{0,28},{4,8},{8,4},{12,16},{16,12},{20,24},{24,20},{28,0},{1,29},{... | collective-permute-start | bytes 73736 | tf_op jit(solution)/shard_map/ppermute | solution.py:708
  16.5 0.0 collective-permute-done.5.first_ref
  16.5 1.5 %collective-permute-start.6 = (bf16[1,160,256]{2,1,0:T(8,128)(2,1)S(1)}, bf16[1,160,256]{2,1,0:T(8,128)(2,1)S(1)}, u32[]{:S(2)}, u32[]{:S(2)}) collective-permute-start(bf16[1,160,256]{2,1,0:T(8,128)(2,1)S(1)} %maximum_bitcast_fusion), channel_id=1, source_target_pairs={{0,16},{4,20},{8,24},{12,28},{16,0},{20,4},{24,8},{28,12},{1,17},{... | collective-permute-start | bytes 245768 | tf_op jit(solution)/shard_map/ppermute | solution.py:605
  18.0 0.0 copy-done.1
  18.0 0.0 copy-done.2
  18.0 1.4 %radial.1 = (bf16[16,512,256]{2,1,0:T(8,128)(2,1)S(1)}, f32[2,8,256]{2,1,0:T(8,128)S(1)}, f32[16,32,256]{2,1,0:T(8,128)S(1)}, f32[16,128]{1,0:T(8,128)S(1)}) custom-call(s32[1]{0:T(128)} %bitcast.4.place_ref, bf16[80,256]{1,0:T(8,128)(2,1)S(1)} %source.1.own_ref, bf16[80,256]{1,0:T(8,128)(2,1)S(1)} %collective-permute-done.5.first_ref, ...), custom_call_target="tpu_custom_call" | custom-call | flops 3000000000 | bytes 9000000 | tf_op jit(solution)/shard_map/radial/pallas_call | solution.py:639
  19.4 0.3 collective-permute-done.8.second_ref
  19.7 0.8 %radial_other.1 = (bf16[16,256,256]{2,1,0:T(8,128)(2,1)S(1)}, f32[1,8,256]{2,1,0:T(8,128)S(1)}) custom-call(s32[1]{0:T(128)} %bitcast.4.place_ref, bf16[80,256]{1,0:T(8,128)(2,1)S(1)} %source.1.own_ref, bf16[48,256]{1,0:T(8,128)(2,1)S(1)} %collective-permute-done.8.second_ref, f32[16,32,256]{2,1,0:T(8,128)S(1)} %get-tuple-element.28.filt_ref), custom_call_target="tpu_custom_call" | custom-call | flops 1000000000 | bytes 3000000 | tf_op jit(solution)/shard_map/radial_other/pallas_call | solution.py:639
  20.5 0.0 copy-start
  20.5 2.1 %near_messages.1 = (f32[32,256]{1,0:T(8,128)S(1)}, bf16[8,32,256]{2,1,0:T(8,128)(2,1)S(1)}) custom-call(bf16[80,256]{1,0:T(8,128)(2,1)S(1)} %source.1.own_ref, bf16[80,256]{1,0:T(8,128)(2,1)S(1)} %collective-permute-done.5.first_ref, bf16[48,256]{1,0:T(8,128)(2,1)S(1)} %collective-permute-done.8.second_ref, ...), custom_call_target="tpu_custom_call" | custom-call | flops 4000000000 | bytes 12000000 | tf_op jit(solution)/shard_map/near_messages/pallas_call | solution.py:639
  22.6 0.0 collective-permute-done.6
  22.7 1.3 %collective-permute-start.7 = (bf16[2,160,256]{2,1,0:T(8,128)(2,1)S(1)}, bf16[2,160,256]{2,1,0:T(8,128)(2,1)S(1)}, u32[]{:S(2)}, u32[]{:S(2)}) collective-permute-start(bf16[2,160,256]{2,1,0:T(8,128)(2,1)S(1)} %pad_maximum_fusion.held_ref), channel_id=1, source_target_pairs={{0,8},{4,12},{8,0},{12,4},{16,24},{20,28},{24,16},{28,20},{1,9},{5... | collective-permute-start | bytes 491528 | tf_op jit(solution)/shard_map/ppermute | solution.py:605
  24.0 0.0 copy-done
  24.0 2.1 %near_grad.1.near_ref = f32[32,256]{1,0:T(8,128)S(1)} custom-call(bf16[288,256]{1,0:T(8,128)(2,1)S(1)} %bitcast.9, bf16[288,256]{1,0:T(8,128)(2,1)S(1)} %collective-permute-done.3.refs_7_.first_ref, bf16[288,256]{1,0:T(8,128)(2,1)S(1)} %collective-permute-done.4.refs_8_.second_ref, bf16[16,512,256]{2,1,0:T(8,128)(2,1)S(1)} %get-tuple-element.27.radial_ref, ...), custom_call_target="tpu_custom_call" | custom-call | flops 3000000000 | bytes 9000000 | tf_op jit(solution)/shard_map/near_grad/pallas_call | solution.py:639
  26.1 2.2 %half.1 = (f32[544,256]{1,0:T(8,128)S(1)}, f32[544,256]{1,0:T(8,128)S(1)}, bf16[256,256]{1,0:T(8,128)(2,1)S(1)}, f32[16,256]{1,0:T(8,128)S(1)}) custom-call(bf16[2,160,256]{2,1,0:T(8,128)(2,1)S(1)} %pad_maximum_fusion.held_ref), custom_call_target="tpu_custom_call" | custom-call | flops 200000000 | bytes 600000 | tf_op jit(solution)/shard_map/half/pallas_call | solution.py:639
  28.3 0.0 collective-permute-done.7.rest_ref.held_ref
  28.3 1.2 %scaled.1 = (bf16[32,256]{1,0:T(8,128)(2,1)S(1)}, bf16[256,1024]{1,0:T(8,128)(2,1)S(1)}, f32[16,1024]{1,0:T(8,128)S(1)}) custom-call(bf16[2,160,256]{2,1,0:T(8,128)(2,1)S(1)} %collective-permute-done.7.rest_ref.held_ref, f32[32,256]{1,0:T(8,128)S(1)} %near_grad.1.near_ref, f32[16,128]{1,0:T(8,128)S(1)} %get-tuple-element.34.weight_ref, ...), custom_call_target="tpu_custom_call" | custom-call | flops 2000000000 | bytes 6000000 | tf_op jit(solution)/shard_map/scaled/pallas_call | solution.py:639
  29.5 0.1 collective-permute-start.9
  29.6 1.2 %collective-permute-done.9.first_ref = bf16[32,256]{1,0:T(8,128)(2,1)S(1)} collective-permute-done((bf16[32,256]{1,0:T(8,128)(2,1)S(1)}, bf16[32,256]{1,0:T(8,128)(2,1)S(1)}, u32[]{:S(2)}, u32[]{:S(2)}) %collective-permute-start.9) | collective-permute-done | bytes 16416 | tf_op jit(solution)/shard_map/ppermute | solution.py:605
  30.8 1.5 %collective-permute-start.10 = (bf16[64,256]{1,0:T(8,128)(2,1)S(1)}, bf16[64,256]{1,0:T(8,128)(2,1)S(1)}, u32[]{:S(2)}, u32[]{:S(2)}) collective-permute-start(bf16[64,256]{1,0:T(8,128)(2,1)S(1)} %pad_maximum_fusion.1), channel_id=1, source_target_pairs={{0,2},{1,3},{2,0},{3,1},{4,6},{5,7},{6,4},{7,5},{8,10},{9,11},{10,... | collective-permute-start | bytes 98312 | tf_op jit(solution)/shard_map/ppermute | solution.py:605
  32.3 1.6 %messages.1 = (bf16[9,32,256]{2,1,0:T(8,128)(2,1)}, f32[8,128]{1,0:T(8,128)S(1)}) custom-call(bf16[2,160,256]{2,1,0:T(8,128)(2,1)S(1)} %collective-permute-done.7.rest_ref.held_ref, f32[32,256]{1,0:T(8,128)S(1)} %get-tuple-element.32.order_ref.scalar_ref, bf16[8,32,256]{2,1,0:T(8,128)(2,1)S(1)} %get-tuple-element.33.rest_ref, ...), custom_call_target="tpu_custom_call" | custom-call | flops 2000000000 | bytes 6000000 | tf_op jit(solution)/shard_map/messages/pallas_call | solution.py:639
  33.9 0.8 %collective-permute-done.10.other_ref = bf16[64,256]{1,0:T(8,128)(2,1)S(1)} collective-permute-done((bf16[64,256]{1,0:T(8,128)(2,1)S(1)}, bf16[64,256]{1,0:T(8,128)(2,1)S(1)}, u32[]{:S(2)}, u32[]{:S(2)}) %collective-permute-start.10) | collective-permute-done | bytes 32800 | tf_op jit(solution)/shard_map/ppermute | solution.py:605
  34.7 0.8 %final.1 = f32[32,256]{1,0:T(8,128)} custom-call(s32[1]{0:T(128)} %bitcast.lane_ref, bf16[128,128]{1,0:T(8,128)(2,1)S(1)} %get-tuple-element.24.refs_4_.w_ref, bf16[32,256]{1,0:T(8,128)(2,1)S(1)} %get-tuple-element.42.own_ref, bf16[32,256]{1,0:T(8,128)(2,1)S(1)} %collective-permute-done.9.first_ref, bf16[64,256]{1,0:T(8,128)(2,1)S(1)} %collective-permute-done.10.other_ref, ...), custom_call_target="tpu_custom_call" | custom-call | flops 1000000000 | bytes 3000000 | tf_op jit(solution)/shard_map/final/pallas_call | solution.py:639
  (4 shorter events, 0.0 us)
Async XLA Ops:
  0.6 17.4 %copy-start.1 = (s32[3,1024]{1,0:T(4,128)S(1)}, s32[3,1024]{1,0:T(4,128)}, u32[]{:S(2)}) copy-start(s32[3,1024]{1,0:T(4,128)} %wave_ref.1) | copy-start | bytes 36868
  0.6 17.4 %copy-start.2 = (f32[16,32]{1,0:T(8,128)S(1)}, f32[16,32]{1,0:T(8,128)}, u32[]{:S(2)}) copy-start(f32[16,32]{1,0:T(8,128)} %w_rad_ref.1) | copy-start | bytes 6148
  0.7 11.5 %collective-permute-start.3 = (bf16[288,256]{1,0:T(8,128)(2,1)}, bf16[288,256]{1,0:T(8,128)(2,1)S(1)}, u32[]{:S(2)}, u32[]{:S(2)}) collective-permute-start(bf16[288,256]{1,0:T(8,128)(2,1)} %bitcast.6), channel_id=1, source_target_pairs={{0,4},{4,0},{8,12},{12,8},{16,20},{20,16},{24,28},{28,24},{1,5},{5... | collective-permute-start | bytes 442376 | tf_op jit(solution)/shard_map/ppermute | solution.py:605
  3.7 8.5 %collective-permute-start.4 = (bf16[288,256]{1,0:T(8,128)(2,1)}, bf16[288,256]{1,0:T(8,128)(2,1)S(1)}, u32[]{:S(2)}, u32[]{:S(2)}) collective-permute-start(bf16[288,256]{1,0:T(8,128)(2,1)} %bitcast.7), channel_id=1, source_target_pairs={{0,28},{4,8},{8,4},{12,16},{16,12},{20,24},{24,20},{28,0},{1,29},{... | collective-permute-start | bytes 442376 | tf_op jit(solution)/shard_map/ppermute | solution.py:696
  7.2 3.6 %collective-permute-start = (bf16[32,256]{1,0:T(8,128)(2,1)}, bf16[32,256]{1,0:T(8,128)(2,1)S(1)}, u32[]{:S(2)}, u32[]{:S(2)}) collective-permute-start(bf16[32,256]{1,0:T(8,128)(2,1)} %feats_hbm.1), channel_id=1, source_target_pairs={{0,1},{1,0},{2,3},{3,2},{4,5},{5,4},{6,7},{7,6},{8,9},{9,8},{10,11... | collective-permute-start | bytes 49160 | tf_op jit(solution)/shard_map/ppermute | solution.py:605
  7.2 3.9 %collective-permute-start.1 = (bf16[32,256]{1,0:T(8,128)(2,1)}, bf16[32,256]{1,0:T(8,128)(2,1)S(1)}, u32[]{:S(2)}, u32[]{:S(2)}) collective-permute-start(bf16[32,256]{1,0:T(8,128)(2,1)} %feats_hbm.1), channel_id=1, source_target_pairs={{0,2},{1,3},{2,0},{3,1},{4,6},{5,7},{6,4},{7,5},{8,10},{9,11},{10,... | collective-permute-start | bytes 49160 | tf_op jit(solution)/shard_map/ppermute | solution.py:605
  8.8 3.4 %collective-permute-start.2 = (bf16[32,256]{1,0:T(8,128)(2,1)}, bf16[32,256]{1,0:T(8,128)(2,1)S(1)}, u32[]{:S(2)}, u32[]{:S(2)}) collective-permute-start(bf16[32,256]{1,0:T(8,128)(2,1)} %feats_hbm.1), channel_id=1, source_target_pairs={{0,3},{1,2},{2,1},{3,0},{4,7},{5,6},{6,5},{7,4},{8,11},{9,10},{10,... | collective-permute-start | bytes 49160 | tf_op jit(solution)/shard_map/ppermute | solution.py:605
  12.3 4.1 %collective-permute-start.5 = (bf16[80,256]{1,0:T(8,128)(2,1)S(1)}, bf16[80,256]{1,0:T(8,128)(2,1)S(1)}, u32[]{:S(2)}, u32[]{:S(2)}) collective-permute-start(bf16[80,256]{1,0:T(8,128)(2,1)S(1)} %source.1.own_ref), channel_id=1, source_target_pairs={{0,4},{4,0},{8,12},{12,8},{16,20},{20,16},{24,28},{28,24},{1,5},{5... | collective-permute-start | bytes 122888 | tf_op jit(solution)/shard_map/ppermute | solution.py:605
  12.9 6.8 %collective-permute-start.8 = (bf16[48,256]{1,0:T(8,128)(2,1)S(1)}, bf16[48,256]{1,0:T(8,128)(2,1)S(1)}, u32[]{:S(2)}, u32[]{:S(2)}) collective-permute-start(bf16[48,256]{1,0:T(8,128)(2,1)S(1)} %slice.4), channel_id=1, source_target_pairs={{0,28},{4,8},{8,4},{12,16},{16,12},{20,24},{24,20},{28,0},{1,29},{... | collective-permute-start | bytes 73736 | tf_op jit(solution)/shard_map/ppermute | solution.py:708
  16.5 6.2 %collective-permute-start.6 = (bf16[1,160,256]{2,1,0:T(8,128)(2,1)S(1)}, bf16[1,160,256]{2,1,0:T(8,128)(2,1)S(1)}, u32[]{:S(2)}, u32[]{:S(2)}) collective-permute-start(bf16[1,160,256]{2,1,0:T(8,128)(2,1)S(1)} %maximum_bitcast_fusion), channel_id=1, source_target_pairs={{0,16},{4,20},{8,24},{12,28},{16,0},{20,4},{24,8},{28,12},{1,17},{... | collective-permute-start | bytes 245768 | tf_op jit(solution)/shard_map/ppermute | solution.py:605
  20.5 3.5 %copy-start = (bf16[9,32,256]{2,1,0:T(8,128)(2,1)S(1)}, bf16[9,32,256]{2,1,0:T(8,128)(2,1)}, u32[]{:S(2)}) copy-start(bf16[9,32,256]{2,1,0:T(8,128)(2,1)} %param.23) | copy-start | bytes 442372
  22.7 5.7 %collective-permute-start.7 = (bf16[2,160,256]{2,1,0:T(8,128)(2,1)S(1)}, bf16[2,160,256]{2,1,0:T(8,128)(2,1)S(1)}, u32[]{:S(2)}, u32[]{:S(2)}) collective-permute-start(bf16[2,160,256]{2,1,0:T(8,128)(2,1)S(1)} %pad_maximum_fusion.held_ref), channel_id=1, source_target_pairs={{0,8},{4,12},{8,0},{12,4},{16,24},{20,28},{24,16},{28,20},{1,9},{5... | collective-permute-start | bytes 491528 | tf_op jit(solution)/shard_map/ppermute | solution.py:605
  29.5 1.2 %collective-permute-start.9 = (bf16[32,256]{1,0:T(8,128)(2,1)S(1)}, bf16[32,256]{1,0:T(8,128)(2,1)S(1)}, u32[]{:S(2)}, u32[]{:S(2)}) collective-permute-start(bf16[32,256]{1,0:T(8,128)(2,1)S(1)} %get-tuple-element.42.own_ref), channel_id=1, source_target_pairs={{0,1},{1,0},{2,3},{3,2},{4,5},{5,4},{6,7},{7,6},{8,9},{9,8},{10,11... | collective-permute-start | bytes 49160 | tf_op jit(solution)/shard_map/ppermute | solution.py:605
  30.8 3.9 %collective-permute-start.10 = (bf16[64,256]{1,0:T(8,128)(2,1)S(1)}, bf16[64,256]{1,0:T(8,128)(2,1)S(1)}, u32[]{:S(2)}, u32[]{:S(2)}) collective-permute-start(bf16[64,256]{1,0:T(8,128)(2,1)S(1)} %pad_maximum_fusion.1), channel_id=1, source_target_pairs={{0,2},{1,3},{2,0},{3,1},{4,6},{5,7},{6,4},{7,5},{8,10},{9,11},{10,... | collective-permute-start | bytes 98312 | tf_op jit(solution)/shard_map/ppermute | solution.py:605

commit v5 on v4

--- a/solution.py
+++ b/solution.py
@@ -573,26 +573,15 @@
     token_ref[...] = jnp.zeros_like(token_ref)
 
 
-def final_kernel(
-    lane_ref, w_ref, own_ref, first_ref, other_ref, token_ref, out_ref, all_ref
-):
+def final_kernel(chans, lane_ref, w_ref, *refs):
+    out_ref, all_ref = refs[-2:]
     channels = out_ref.shape[0]
     lane = lane_ref[0]
-    pieces = [own_ref[...], first_ref[...]]
-    if other_ref is not None:
-        pieces += [other_ref[m * channels : (m + 1) * channels, :] for m in range(2)]
-    for m, piece in enumerate(pieces):
+    for m, piece in enumerate(refs[:chans]):
         at = pl.multiple_of((lane ^ m) * channels, channels)
-        all_ref[pl.ds(at, channels), :] = piece
+        all_ref[pl.ds(at, channels), :] = piece[...]
     first = pl.multiple_of(lane * channels, channels)
     out_ref[...] = dot_nn(w_ref[pl.ds(first, channels), :], all_ref[...])
-
-
-def two_chan(kernel, place):
-    def without(*refs):
-        kernel(*refs[:place], None, *refs[place:])
-
-    return without
 
 
 def cost(micros):
@@ -606,10 +595,7 @@
 
 
 def chan_pieces(raw, kept):
-    first = swapped(raw, "chan", 1)
-    if lax.axis_size("chan") == 2:
-        return [kept, first]
-    return [kept, first, swapped(jnp.concatenate([kept, first], 0), "chan", 2)]
+    return [kept] + [swapped(raw, "chan", m) for m in range(1, lax.axis_size("chan"))]
 
 
 def on_device(
@@ -690,7 +676,7 @@
             )
         ]
     )
-    pieces = [feats_copy] + [swapped(features, "chan", m) for m in range(1, chans)]
+    pieces = chan_pieces(features, feats_copy)
     other = [i - 1 if i % 2 == 0 else i + 1 for i in range(spaces)]
     route = [(i, other[i] % spaces) for i in range(spaces)]
     second = lax.ppermute(cots, "space", route)
@@ -806,7 +792,7 @@
         COST["messages"],
     )
     grad_features = call(
-        final_kernel if chans > 2 else two_chan(final_kernel, 4),
+        functools.partial(final_kernel, chans),
         shape((channels, atoms), F32),
         (lane,),
         (w_copy, *scaled_pieces, token),

time: 35.7 us -> 35.2 us (0.986)
  waiting for transfers between devices: 3.61 us -> 2.58 us
  starting transfers between devices: 17 us -> 17.6 us
    ppermute x9 -> x10, waiting for transfers between devices: 3.31 us -> 2.28 us  [swapped(): lax.ppermute(block, axis, [(i, i ^ bit) for i in range(lax.axis_size(axis...]
    ppermute x9 -> x10, starting transfers between devices: 9.86 us -> 10.5 us  [swapped(): lax.ppermute(block, axis, [(i, i ^ bit) for i in range(lax.axis_size(axis...]
  transfers between devices with their start and end apart: 11 -> 12, of which waited for: 5 -> 4; matrix products, arithmetic and copies ran while one was open for 0% -> 0% of each run, Pallas kernels for 32% -> 32%
where the time goes in v5:
time: 35.2 us; the launch traced here: 35.1 us
  starting transfers between devices  17.6 us (50%)
  Pallas kernels  13.4 us (38%)
  waiting for transfers between devices  2.58 us (7%)
  between operations  1.4 us (4%)
    pallas_call x9, Pallas kernels, call(): pl.pallas_call(kernel, out_shape=out_shape, in_specs=[SMEM] * len(smem) +...  12.4 us
    ppermute x10, starting transfers between devices, swapped(): lax.ppermute(block, axis, [(i, i ^ bit) for i in range(lax.axis_size(axis...  10.5 us
    ppermute x1, starting transfers between devices, on_device(): unit_second = lax.ppermute(unit[channels:], 'space', route)  3.57 us
    ppermute x1, starting transfers between devices, on_device(): second = lax.ppermute(cots, 'space', route)  3.57 us
    ppermute x10, waiting for transfers between devices, swapped(): lax.ppermute(block, axis, [(i, i ^ bit) for i in range(lax.axis_size(axis...  2.28 us
    pallas_call x1, Pallas kernels, on_device(): pl.pallas_call(prep_kernel, out_shape=(shape((channels + 16, atoms), BF),...  1.03 us
  transfers between devices with their start and end apart: 12, of which 4 were waited for; matrix products, arithmetic and copies ran while one was open for 0% of the time, Pallas kernels for 32%

profile of v5, /device:TPU:0, one launch (start us, length us, event | category | flops | bytes accessed | tf_op | source)
XLA Modules:
  0.0 35.1 jit_solution(12614246539754514192)
XLA Ops:
  0.6 0.0 copy-start.1
  0.6 0.0 copy-start.2
  0.7 3.0 %collective-permute-start.3 = (bf16[288,256]{1,0:T(8,128)(2,1)}, bf16[288,256]{1,0:T(8,128)(2,1)S(1)}, u32[]{:S(2)}, u32[]{:S(2)}) collective-permute-start(bf16[288,256]{1,0:T(8,128)(2,1)} %bitcast.6), channel_id=1, source_target_pairs={{0,4},{4,0},{8,12},{12,8},{16,20},{20,16},{24,28},{28,24},{1,5},{5... | collective-permute-start | bytes 442376 | tf_op jit(solution)/shard_map/ppermute | solution.py:594
  3.7 3.6 %collective-permute-start.4 = (bf16[288,256]{1,0:T(8,128)(2,1)}, bf16[288,256]{1,0:T(8,128)(2,1)S(1)}, u32[]{:S(2)}, u32[]{:S(2)}) collective-permute-start(bf16[288,256]{1,0:T(8,128)(2,1)} %bitcast.7), channel_id=1, source_target_pairs={{0,28},{4,8},{8,4},{12,16},{16,12},{20,24},{24,20},{28,0},{1,29},{... | collective-permute-start | bytes 442376 | tf_op jit(solution)/shard_map/ppermute | solution.py:682
  7.2 0.0 collective-permute-start
  7.2 1.5 %collective-permute-start.1 = (bf16[32,256]{1,0:T(8,128)(2,1)}, bf16[32,256]{1,0:T(8,128)(2,1)S(1)}, u32[]{:S(2)}, u32[]{:S(2)}) collective-permute-start(bf16[32,256]{1,0:T(8,128)(2,1)} %feats_hbm.1), channel_id=1, source_target_pairs={{0,2},{1,3},{2,0},{3,1},{4,6},{5,7},{6,4},{7,5},{8,10},{9,11},{10,... | collective-permute-start | bytes 49160 | tf_op jit(solution)/shard_map/ppermute | solution.py:594
  8.8 0.3 collective-permute-start.2
  9.7 1.0 %prep.1 = (bf16[48,256]{1,0:T(8,128)(2,1)S(1)}, f32[32,256]{1,0:T(8,128)S(1)}, bf16[32,256]{1,0:T(8,128)(2,1)S(1)}, bf16[128,128]{1,0:T(8,128)(2,1)S(1)}) custom-call(s32[1]{0:T(128)S(6)} %copy.14.live_ref, s32[4]{0:T(128)} %count_hbm.1, s32[16]{0:T(128)} %home_hbm.1, s32[16]{0:T(128)} %reach_hbm.1, f32[3,256]{1,0:T(4,128)} %pos_hbm.1, ...), custom_call_target="tpu_custom_call" | custom-call | flops 1000000000 | bytes 3000000 | tf_op jit(solution)/shard_map/prep/pallas_call | solution.py:640
  10.8 0.0 collective-permute-done.refs_1_
  10.8 0.4 %collective-permute-done.1.refs_2_ = bf16[32,256]{1,0:T(8,128)(2,1)S(1)} collective-permute-done((bf16[32,256]{1,0:T(8,128)(2,1)}, bf16[32,256]{1,0:T(8,128)(2,1)S(1)}, u32[]{:S(2)}, u32[]{:S(2)}) %collective-permute-start.1) | collective-permute-done | bytes 16416 | tf_op jit(solution)/shard_map/ppermute | solution.py:594
  11.2 0.9 %collective-permute-done.2.refs_3_ = bf16[32,256]{1,0:T(8,128)(2,1)S(1)} collective-permute-done((bf16[32,256]{1,0:T(8,128)(2,1)}, bf16[32,256]{1,0:T(8,128)(2,1)S(1)}, u32[]{:S(2)}, u32[]{:S(2)}) %collective-permute-start.2) | collective-permute-done | bytes 16416 | tf_op jit(solution)/shard_map/ppermute | solution.py:594
  12.1 0.0 collective-permute-done.3.refs_7_.first_ref
  12.1 0.0 collective-permute-done.4.refs_8_.second_ref
  12.1 0.2 source.1.own_ref
  12.3 0.5 %collective-permute-start.5 = (bf16[80,256]{1,0:T(8,128)(2,1)S(1)}, bf16[80,256]{1,0:T(8,128)(2,1)S(1)}, u32[]{:S(2)}, u32[]{:S(2)}) collective-permute-start(bf16[80,256]{1,0:T(8,128)(2,1)S(1)} %source.1.own_ref), channel_id=1, source_target_pairs={{0,4},{4,0},{8,12},{12,8},{16,20},{20,16},{24,28},{28,24},{1,5},{5... | collective-permute-start | bytes 122888 | tf_op jit(solution)/shard_map/ppermute | solution.py:594
  12.9 3.6 %collective-permute-start.8 = (bf16[48,256]{1,0:T(8,128)(2,1)S(1)}, bf16[48,256]{1,0:T(8,128)(2,1)S(1)}, u32[]{:S(2)}, u32[]{:S(2)}) collective-permute-start(bf16[48,256]{1,0:T(8,128)(2,1)S(1)} %slice.4), channel_id=1, source_target_pairs={{0,28},{4,8},{8,4},{12,16},{16,12},{20,24},{24,20},{28,0},{1,29},{... | collective-permute-start | bytes 73736 | tf_op jit(solution)/shard_map/ppermute | solution.py:694
  16.5 0.0 collective-permute-done.5.first_ref
  16.5 1.5 %collective-permute-start.6 = (bf16[1,160,256]{2,1,0:T(8,128)(2,1)S(1)}, bf16[1,160,256]{2,1,0:T(8,128)(2,1)S(1)}, u32[]{:S(2)}, u32[]{:S(2)}) collective-permute-start(bf16[1,160,256]{2,1,0:T(8,128)(2,1)S(1)} %maximum_bitcast_fusion), channel_id=1, source_target_pairs={{0,16},{4,20},{8,24},{12,28},{16,0},{20,4},{24,8},{28,12},{1,17},{... | collective-permute-start | bytes 245768 | tf_op jit(solution)/shard_map/ppermute | solution.py:594
  18.0 0.0 copy-done.1
  18.0 0.0 copy-done.2
  18.0 1.4 %radial.1 = (bf16[16,512,256]{2,1,0:T(8,128)(2,1)S(1)}, f32[2,8,256]{2,1,0:T(8,128)S(1)}, f32[16,32,256]{2,1,0:T(8,128)S(1)}, f32[16,128]{1,0:T(8,128)S(1)}) custom-call(s32[1]{0:T(128)} %bitcast.4.place_ref, bf16[80,256]{1,0:T(8,128)(2,1)S(1)} %source.1.own_ref, bf16[80,256]{1,0:T(8,128)(2,1)S(1)} %collective-permute-done.5.first_ref, ...), custom_call_target="tpu_custom_call" | custom-call | flops 3000000000 | bytes 9000000 | tf_op jit(solution)/shard_map/radial/pallas_call | solution.py:625
  19.4 0.3 collective-permute-done.8.second_ref
  19.7 0.8 %radial_other.1 = (bf16[16,256,256]{2,1,0:T(8,128)(2,1)S(1)}, f32[1,8,256]{2,1,0:T(8,128)S(1)}) custom-call(s32[1]{0:T(128)} %bitcast.4.place_ref, bf16[80,256]{1,0:T(8,128)(2,1)S(1)} %source.1.own_ref, bf16[48,256]{1,0:T(8,128)(2,1)S(1)} %collective-permute-done.8.second_ref, f32[16,32,256]{2,1,0:T(8,128)S(1)} %get-tuple-element.28.filt_ref), custom_call_target="tpu_custom_call" | custom-call | flops 1000000000 | bytes 3000000 | tf_op jit(solution)/shard_map/radial_other/pallas_call | solution.py:625
  20.5 0.0 copy-start
  20.5 2.1 %near_messages.1 = (f32[32,256]{1,0:T(8,128)S(1)}, bf16[8,32,256]{2,1,0:T(8,128)(2,1)S(1)}) custom-call(bf16[80,256]{1,0:T(8,128)(2,1)S(1)} %source.1.own_ref, bf16[80,256]{1,0:T(8,128)(2,1)S(1)} %collective-permute-done.5.first_ref, bf16[48,256]{1,0:T(8,128)(2,1)S(1)} %collective-permute-done.8.second_ref, ...), custom_call_target="tpu_custom_call" | custom-call | flops 4000000000 | bytes 12000000 | tf_op jit(solution)/shard_map/near_messages/pallas_call | solution.py:625
  22.6 0.0 collective-permute-done.6
  22.7 1.3 %collective-permute-start.7 = (bf16[2,160,256]{2,1,0:T(8,128)(2,1)S(1)}, bf16[2,160,256]{2,1,0:T(8,128)(2,1)S(1)}, u32[]{:S(2)}, u32[]{:S(2)}) collective-permute-start(bf16[2,160,256]{2,1,0:T(8,128)(2,1)S(1)} %pad_maximum_fusion.held_ref), channel_id=1, source_target_pairs={{0,8},{4,12},{8,0},{12,4},{16,24},{20,28},{24,16},{28,20},{1,9},{5... | collective-permute-start | bytes 491528 | tf_op jit(solution)/shard_map/ppermute | solution.py:594
  24.0 0.0 copy-done
  24.0 2.1 %near_grad.1.near_ref = f32[32,256]{1,0:T(8,128)S(1)} custom-call(bf16[288,256]{1,0:T(8,128)(2,1)S(1)} %bitcast.9, bf16[288,256]{1,0:T(8,128)(2,1)S(1)} %collective-permute-done.3.refs_7_.first_ref, bf16[288,256]{1,0:T(8,128)(2,1)S(1)} %collective-permute-done.4.refs_8_.second_ref, bf16[16,512,256]{2,1,0:T(8,128)(2,1)S(1)} %get-tuple-element.27.radial_ref, ...), custom_call_target="tpu_custom_call" | custom-call | flops 3000000000 | bytes 9000000 | tf_op jit(solution)/shard_map/near_grad/pallas_call | solution.py:625
  26.1 2.2 %half.1 = (f32[544,256]{1,0:T(8,128)S(1)}, f32[544,256]{1,0:T(8,128)S(1)}, bf16[256,256]{1,0:T(8,128)(2,1)S(1)}, f32[16,256]{1,0:T(8,128)S(1)}) custom-call(bf16[2,160,256]{2,1,0:T(8,128)(2,1)S(1)} %pad_maximum_fusion.held_ref), custom_call_target="tpu_custom_call" | custom-call | flops 200000000 | bytes 600000 | tf_op jit(solution)/shard_map/half/pallas_call | solution.py:625
  28.3 0.0 collective-permute-done.7.rest_ref.held_ref
  28.3 1.2 %scaled.1 = (bf16[32,256]{1,0:T(8,128)(2,1)S(1)}, bf16[256,1024]{1,0:T(8,128)(2,1)S(1)}, f32[16,1024]{1,0:T(8,128)S(1)}) custom-call(bf16[2,160,256]{2,1,0:T(8,128)(2,1)S(1)} %collective-permute-done.7.rest_ref.held_ref, f32[32,256]{1,0:T(8,128)S(1)} %near_grad.1.near_ref, f32[16,128]{1,0:T(8,128)S(1)} %get-tuple-element.34.weight_ref, ...), custom_call_target="tpu_custom_call" | custom-call | flops 2000000000 | bytes 6000000 | tf_op jit(solution)/shard_map/scaled/pallas_call | solution.py:625
  29.5 1.6 %collective-permute-start.10 = (bf16[32,256]{1,0:T(8,128)(2,1)S(1)}, bf16[32,256]{1,0:T(8,128)(2,1)S(1)}, u32[]{:S(2)}, u32[]{:S(2)}) collective-permute-start(bf16[32,256]{1,0:T(8,128)(2,1)S(1)} %get-tuple-element.42.refs_0_), channel_id=1, source_target_pairs={{0,2},{1,3},{2,0},{3,1},{4,6},{5,7},{6,4},{7,5},{8,10},{9,11},{10,... | collective-permute-start | bytes 49160 | tf_op jit(solution)/shard_map/ppermute | solution.py:594
  31.1 0.0 collective-permute-start.11
  31.1 0.6 %collective-permute-start.9 = (bf16[32,256]{1,0:T(8,128)(2,1)S(1)}, bf16[32,256]{1,0:T(8,128)(2,1)S(1)}, u32[]{:S(2)}, u32[]{:S(2)}) collective-permute-start(bf16[32,256]{1,0:T(8,128)(2,1)S(1)} %get-tuple-element.42.refs_0_), channel_id=1, source_target_pairs={{0,1},{1,0},{2,3},{3,2},{4,5},{5,4},{6,7},{7,6},{8,9},{9,8},{10,11... | collective-permute-start | bytes 49160 | tf_op jit(solution)/shard_map/ppermute | solution.py:594
  31.7 1.6 %messages.1 = (bf16[9,32,256]{2,1,0:T(8,128)(2,1)}, f32[8,128]{1,0:T(8,128)S(1)}) custom-call(bf16[2,160,256]{2,1,0:T(8,128)(2,1)S(1)} %collective-permute-done.7.rest_ref.held_ref, f32[32,256]{1,0:T(8,128)S(1)} %get-tuple-element.32.order_ref.scalar_ref, bf16[8,32,256]{2,1,0:T(8,128)(2,1)S(1)} %get-tuple-element.33.rest_ref, ...), custom_call_target="tpu_custom_call" | custom-call | flops 2000000000 | bytes 6000000 | tf_op jit(solution)/shard_map/messages/pallas_call | solution.py:625
  33.4 0.0 collective-permute-done.10.refs_2_
  33.4 0.9 %collective-permute-done.11.refs_3_ = bf16[32,256]{1,0:T(8,128)(2,1)S(1)} collective-permute-done((bf16[32,256]{1,0:T(8,128)(2,1)S(1)}, bf16[32,256]{1,0:T(8,128)(2,1)S(1)}, u32[]{:S(2)}, u32[]{:S(2)}) %collective-permute-start.11) | collective-permute-done | bytes 16416 | tf_op jit(solution)/shard_map/ppermute | solution.py:594
  34.3 0.0 collective-permute-done.9.refs_1_
  34.3 0.8 %final.1 = f32[32,256]{1,0:T(8,128)} custom-call(s32[1]{0:T(128)} %bitcast.lane_ref, bf16[128,128]{1,0:T(8,128)(2,1)S(1)} %get-tuple-element.24.refs_4_.w_ref, bf16[32,256]{1,0:T(8,128)(2,1)S(1)} %get-tuple-element.42.refs_0_, bf16[32,256]{1,0:T(8,128)(2,1)S(1)} %collective-permute-done.9.refs_1_, bf16[32,256]{1,0:T(8,128)(2,1)S(1)} %collective-permute-done.10.refs_2_, ...), custom_call_target="tpu_custom_call" | custom-call | flops 1000000000 | bytes 3000000 | tf_op jit(solution)/shard_map/final/pallas_call | solution.py:625
  (3 shorter events, 0.0 us)
Async XLA Ops:
  0.6 17.4 %copy-start.1 = (s32[3,1024]{1,0:T(4,128)S(1)}, s32[3,1024]{1,0:T(4,128)}, u32[]{:S(2)}) copy-start(s32[3,1024]{1,0:T(4,128)} %wave_ref.1) | copy-start | bytes 36868
  0.6 17.4 %copy-start.2 = (f32[16,32]{1,0:T(8,128)S(1)}, f32[16,32]{1,0:T(8,128)}, u32[]{:S(2)}) copy-start(f32[16,32]{1,0:T(8,128)} %w_rad_ref.1) | copy-start | bytes 6148
  0.7 11.5 %collective-permute-start.3 = (bf16[288,256]{1,0:T(8,128)(2,1)}, bf16[288,256]{1,0:T(8,128)(2,1)S(1)}, u32[]{:S(2)}, u32[]{:S(2)}) collective-permute-start(bf16[288,256]{1,0:T(8,128)(2,1)} %bitcast.6), channel_id=1, source_target_pairs={{0,4},{4,0},{8,12},{12,8},{16,20},{20,16},{24,28},{28,24},{1,5},{5... | collective-permute-start | bytes 442376 | tf_op jit(solution)/shard_map/ppermute | solution.py:594
  3.7 8.5 %collective-permute-start.4 = (bf16[288,256]{1,0:T(8,128)(2,1)}, bf16[288,256]{1,0:T(8,128)(2,1)S(1)}, u32[]{:S(2)}, u32[]{:S(2)}) collective-permute-start(bf16[288,256]{1,0:T(8,128)(2,1)} %bitcast.7), channel_id=1, source_target_pairs={{0,28},{4,8},{8,4},{12,16},{16,12},{20,24},{24,20},{28,0},{1,29},{... | collective-permute-start | bytes 442376 | tf_op jit(solution)/shard_map/ppermute | solution.py:682
  7.2 3.6 %collective-permute-start = (bf16[32,256]{1,0:T(8,128)(2,1)}, bf16[32,256]{1,0:T(8,128)(2,1)S(1)}, u32[]{:S(2)}, u32[]{:S(2)}) collective-permute-start(bf16[32,256]{1,0:T(8,128)(2,1)} %feats_hbm.1), channel_id=1, source_target_pairs={{0,1},{1,0},{2,3},{3,2},{4,5},{5,4},{6,7},{7,6},{8,9},{9,8},{10,11... | collective-permute-start | bytes 49160 | tf_op jit(solution)/shard_map/ppermute | solution.py:594
  7.2 3.9 %collective-permute-start.1 = (bf16[32,256]{1,0:T(8,128)(2,1)}, bf16[32,256]{1,0:T(8,128)(2,1)S(1)}, u32[]{:S(2)}, u32[]{:S(2)}) collective-permute-start(bf16[32,256]{1,0:T(8,128)(2,1)} %feats_hbm.1), channel_id=1, source_target_pairs={{0,2},{1,3},{2,0},{3,1},{4,6},{5,7},{6,4},{7,5},{8,10},{9,11},{10,... | collective-permute-start | bytes 49160 | tf_op jit(solution)/shard_map/ppermute | solution.py:594
  8.8 3.4 %collective-permute-start.2 = (bf16[32,256]{1,0:T(8,128)(2,1)}, bf16[32,256]{1,0:T(8,128)(2,1)S(1)}, u32[]{:S(2)}, u32[]{:S(2)}) collective-permute-start(bf16[32,256]{1,0:T(8,128)(2,1)} %feats_hbm.1), channel_id=1, source_target_pairs={{0,3},{1,2},{2,1},{3,0},{4,7},{5,6},{6,5},{7,4},{8,11},{9,10},{10,... | collective-permute-start | bytes 49160 | tf_op jit(solution)/shard_map/ppermute | solution.py:594
  12.3 4.1 %collective-permute-start.5 = (bf16[80,256]{1,0:T(8,128)(2,1)S(1)}, bf16[80,256]{1,0:T(8,128)(2,1)S(1)}, u32[]{:S(2)}, u32[]{:S(2)}) collective-permute-start(bf16[80,256]{1,0:T(8,128)(2,1)S(1)} %source.1.own_ref), channel_id=1, source_target_pairs={{0,4},{4,0},{8,12},{12,8},{16,20},{20,16},{24,28},{28,24},{1,5},{5... | collective-permute-start | bytes 122888 | tf_op jit(solution)/shard_map/ppermute | solution.py:594
  12.9 6.8 %collective-permute-start.8 = (bf16[48,256]{1,0:T(8,128)(2,1)S(1)}, bf16[48,256]{1,0:T(8,128)(2,1)S(1)}, u32[]{:S(2)}, u32[]{:S(2)}) collective-permute-start(bf16[48,256]{1,0:T(8,128)(2,1)S(1)} %slice.4), channel_id=1, source_target_pairs={{0,28},{4,8},{8,4},{12,16},{16,12},{20,24},{24,20},{28,0},{1,29},{... | collective-permute-start | bytes 73736 | tf_op jit(solution)/shard_map/ppermute | solution.py:694
  16.5 6.2 %collective-permute-start.6 = (bf16[1,160,256]{2,1,0:T(8,128)(2,1)S(1)}, bf16[1,160,256]{2,1,0:T(8,128)(2,1)S(1)}, u32[]{:S(2)}, u32[]{:S(2)}) collective-permute-start(bf16[1,160,256]{2,1,0:T(8,128)(2,1)S(1)} %maximum_bitcast_fusion), channel_id=1, source_target_pairs={{0,16},{4,20},{8,24},{12,28},{16,0},{20,4},{24,8},{28,12},{1,17},{... | collective-permute-start | bytes 245768 | tf_op jit(solution)/shard_map/ppermute | solution.py:594
  20.5 3.5 %copy-start = (bf16[9,32,256]{2,1,0:T(8,128)(2,1)S(1)}, bf16[9,32,256]{2,1,0:T(8,128)(2,1)}, u32[]{:S(2)}) copy-start(bf16[9,32,256]{2,1,0:T(8,128)(2,1)} %param.23) | copy-start | bytes 442372
  22.7 5.7 %collective-permute-start.7 = (bf16[2,160,256]{2,1,0:T(8,128)(2,1)S(1)}, bf16[2,160,256]{2,1,0:T(8,128)(2,1)S(1)}, u32[]{:S(2)}, u32[]{:S(2)}) collective-permute-start(bf16[2,160,256]{2,1,0:T(8,128)(2,1)S(1)} %pad_maximum_fusion.held_ref), channel_id=1, source_target_pairs={{0,8},{4,12},{8,0},{12,4},{16,24},{20,28},{24,16},{28,20},{1,9},{5... | collective-permute-start | bytes 491528 | tf_op jit(solution)/shard_map/ppermute | solution.py:594
  29.5 3.8 %collective-permute-start.10 = (bf16[32,256]{1,0:T(8,128)(2,1)S(1)}, bf16[32,256]{1,0:T(8,128)(2,1)S(1)}, u32[]{:S(2)}, u32[]{:S(2)}) collective-permute-start(bf16[32,256]{1,0:T(8,128)(2,1)S(1)} %get-tuple-element.42.refs_0_), channel_id=1, source_target_pairs={{0,2},{1,3},{2,0},{3,1},{4,6},{5,7},{6,4},{7,5},{8,10},{9,11},{10,... | collective-permute-start | bytes 49160 | tf_op jit(solution)/shard_map/ppermute | solution.py:594
  31.1 3.2 %collective-permute-start.11 = (bf16[32,256]{1,0:T(8,128)(2,1)S(1)}, bf16[32,256]{1,0:T(8,128)(2,1)S(1)}, u32[]{:S(2)}, u32[]{:S(2)}) collective-permute-start(bf16[32,256]{1,0:T(8,128)(2,1)S(1)} %get-tuple-element.42.refs_0_), channel_id=1, source_target_pairs={{0,3},{1,2},{2,1},{3,0},{4,7},{5,6},{6,5},{7,4},{8,11},{9,10},{10,... | collective-permute-start | bytes 49160 | tf_op jit(solution)/shard_map/ppermute | solution.py:594
  31.1 3.2 %collective-permute-start.9 = (bf16[32,256]{1,0:T(8,128)(2,1)S(1)}, bf16[32,256]{1,0:T(8,128)(2,1)S(1)}, u32[]{:S(2)}, u32[]{:S(2)}) collective-permute-start(bf16[32,256]{1,0:T(8,128)(2,1)S(1)} %get-tuple-element.42.refs_0_), channel_id=1, source_target_pairs={{0,1},{1,0},{2,3},{3,2},{4,5},{5,4},{6,7},{7,6},{8,9},{9,8},{10,11... | collective-permute-start | bytes 49160 | tf_op jit(solution)/shard_map/ppermute | solution.py:594
